TPU v7x, 32 devices: a whole 2x2x4 slice. The times are simulated.
32 devices in a mesh: clip: 4 (over y, x), row: 8 (over z, core).
Axes of the slice: x: 2, y: 2, z: 4, core: 2. Of those that a mesh axis runs over, the one named last changes fastest.
Arguments:
- frames: bfloat16 [16, 17, 3, 32, 64], P('clip', None, None, 'row'), may hold values from 0 to 1
- valid: int32 [16, 16, 32, 64], P('clip', None, 'row'), may hold values from 0 to 1
- flags: int32 [16, 16, 2], P('clip'), may hold values 0 or 1
- actions: float32 [16, 16, 4], P('clip'), may hold values from -4 to 4
- states: float32 [16, 16, 3], P('clip'), may hold values from -4 to 4
- latent: float32 [16, 8], P('clip'), may hold values from -4 to 4
- w_enc: float32 [75, 32], replicated, may hold values from -0.75 to 0.75
- w_lstm: float32 [1600, 128], replicated, may hold values from -0.15625 to 0.15625
- w_fc: float32 [16, 250, 1024], P('row'), may hold values from -0.1875 to 0.1875
- w_cond: float32 [15, 250], replicated, may hold values from -1.5 to 1.5
- w_deconv: float32 [32, 128], replicated, may hold values from -1 to 1
- w_mask: float32 [32, 11], replicated, may hold values from -2 to 2
- vector: float32 [517], replicated, may hold values from -1 to 2
- m_enc: float32 [75, 32], replicated, may hold values from -2.9802322e-07 to 2.9802322e-07
- m_lstm: float32 [1600, 128], replicated, may hold values from -2.9802322e-07 to 2.9802322e-07
- m_fc: float32 [16, 250, 1024], P('row'), may hold values from -2.9802322e-07 to 2.9802322e-07
- m_cond: float32 [15, 250], replicated, may hold values from -2.9802322e-07 to 2.9802322e-07
- m_deconv: float32 [32, 128], replicated, may hold values from -2.9802322e-07 to 2.9802322e-07
- m_mask: float32 [32, 11], replicated, may hold values from -2.9802322e-07 to 2.9802322e-07
- m_vector: float32 [517], replicated, may hold values from -1.1920929e-06 to 1.1920929e-06
- v_enc: float32 [75, 32], replicated, may hold values from 2.3191553e-16 to 9.276621e-16
- v_lstm: float32 [1600, 128], replicated, may hold values from 2.3191553e-16 to 9.276621e-16
- v_fc: float32 [16, 250, 1024], P('row'), may hold values from 2.3191553e-16 to 9.276621e-16
- v_cond: float32 [15, 250], replicated, may hold values from 2.3191553e-16 to 9.276621e-16
- v_deconv: float32 [32, 128], replicated, may hold values from 2.3191553e-16 to 9.276621e-16
- v_mask: float32 [32, 11], replicated, may hold values from 2.3191553e-16 to 9.276621e-16
- v_vector: float32 [517], replicated, may hold values from 3.7106485e-15 to 1.4842594e-14
Outputs:
- loss_sum: float32 [], replicated
- valid_count: float32 [], replicated
- grad_norm: float32 [], replicated
- new_enc: float32 [75, 32], replicated
- new_lstm: float32 [1600, 128], replicated
- new_fc: float32 [16, 250, 1024], P('row')
- new_cond: float32 [15, 250], replicated
- new_deconv: float32 [32, 128], replicated
- new_mask: float32 [32, 11], replicated
- new_vector: float32 [517], replicated
- first_enc: float32 [75, 32], replicated
- first_lstm: float32 [1600, 128], replicated
- first_fc: float32 [16, 250, 1024], P('row')
- first_cond: float32 [15, 250], replicated
- first_deconv: float32 [32, 128], replicated
- first_mask: float32 [32, 11], replicated
- first_vector: float32 [517], replicated
- second_enc: float32 [75, 32], replicated
- second_lstm: float32 [1600, 128], replicated
- second_fc: float32 [16, 250, 1024], P('row')
- second_cond: float32 [15, 250], replicated
- second_deconv: float32 [32, 128], replicated
- second_mask: float32 [32, 11], replicated
- second_vector: float32 [517], replicated
All inputs are finite; a program needn't handle non-finite values. No bound on the sum of `flags` on one device may be relied on, other than what follows from the above.
Results may differ from a plain program's by a relative error of at most 0.0096.
Values may be sent and summed in bfloat16 or wider, within the bound.
No kernel may reach another device: no remote copies, remote signals or barrier semaphores. Data moves between devices by JAX's collectives and lax.ppermute only.
A program may use at most 128 MiB of HBM per device.

v0:
```python
import jax
import jax.numpy as jnp
from jax import lax
from jax.sharding import PartitionSpec as P

C = 32
KS = 5
NK = 10
STEP_NO = 10
KK = 25
NM = 11
COND = 15
WB = 32


NORM_EPS = 1e-05
CLIP_NORM = 0.001
BETA_ONE = 0.9
BETA_TWO = 0.999
ADAM_EPS = 1e-12
DECAY = 0.01
HIGH = lax.Precision.HIGHEST


def padded_2(cells, sides, width):
    for axis, dim in sides:
        count = lax.axis_size(axis)
        ends = count - 1
        head = lax.slice_in_dim(cells, 0, width, axis=dim)
        tail = lax.slice_in_dim(cells, cells.shape[dim] - width, cells.shape[dim], axis=dim)
        cells = jnp.concatenate(
            [
                lax.ppermute(tail, axis, [(i, (i + 1) % count) for i in range(ends)]),
                cells,
                lax.ppermute(head, axis, [((i + 1) % count, i) for i in range(ends)]),
            ],
            axis=dim,
        )
    return cells


def passed_along(block, axis, distance):
    devices = range(lax.axis_size(axis))
    route = [(i - distance, i) for i in devices if i - distance in devices]
    return lax.ppermute(block, axis, route)


def split_vector(vector):
    counts = [C, C, C, 4 * C, NK * KK, C, NM]
    pieces = []
    start = 0
    for count in counts:
        pieces.append(vector[start : start + count])
        start += count
    return pieces


def norm_act(pre, gain, shift):
    centered = pre - jnp.mean(pre, -1, keepdims=True)
    scale = lax.rsqrt(jnp.mean(centered * centered, -1, keepdims=True) + NORM_EPS)
    return jax.nn.silu(centered * scale * gain + shift)


def cell_step(gates, cell):
    gate_in, gate_keep, gate_out, gate_new = jnp.split(gates, 4, axis=-1)
    new_cell = jax.nn.sigmoid(gate_keep + 1.0) * cell + jax.nn.sigmoid(gate_in) * jnp.tanh(gate_new)
    return (jax.nn.sigmoid(gate_out) * jnp.tanh(new_cell), new_cell)


def upsample(values):
    clips, rows_in, cols_in, depth = values.shape
    grid = values.reshape(clips, rows_in, cols_in, 2, 2, depth // 4)
    return jnp.transpose(grid, (0, 1, 3, 2, 4, 5)).reshape(
        clips, 2 * rows_in, 2 * cols_in, depth // 4
    )


def predict(logits, upper, w_mask, b_mask, prev_pad):
    clips = logits.shape[0]
    kernels = jax.nn.softmax(logits.reshape(clips, NK, KK), axis=-1)
    activated = jax.nn.silu(upper)
    blend = jax.nn.softmax(
        jnp.einsum("byxc,cm->byxm", activated, w_mask, precision=HIGH) + b_mask, axis=-1
    )
    mixing = jnp.einsum("byxk,bko->byxo", blend[..., 1:], kernels, precision=HIGH)
    height = prev_pad.shape[1] - 4
    breadth = prev_pad.shape[2] - 4
    result = blend[..., :1] * prev_pad[:, 2 : 2 + height, 2 : 2 + breadth, :]
    for offset in range(KK):
        top = offset // KS
        left = offset % KS
        result = (
            result
            + mixing[..., offset : offset + 1]
            * prev_pad[:, top : top + height, left : left + breadth, :]
        )
    return result


def patches(padded, stride, out_rows, out_cols):
    pieces = []
    for offset in range(KK):
        top = offset // KS
        left = offset % KS
        pieces.append(
            padded[
                :,
                top : top + stride * (out_rows - 1) + 1 : stride,
                left : left + stride * (out_cols - 1) + 1 : stride,
                :,
            ]
        )
    return jnp.concatenate(pieces, -1)


def unpatch(grads, shape, stride):

    def extract(padded):
        return patches(padded, stride, grads.shape[1], grads.shape[2])

    _, pullback = jax.vjp(extract, jnp.zeros(shape, jnp.float32))
    return pullback(grads)[0]


def product(left, right, form):
    return jnp.einsum(form, left, right, preferred_element_type=jnp.float32)


def learning_rates(rows_total):
    return [
        0.5 * (KK * 3) ** (-0.5),
        0.5 * (KK * 2 * C) ** (-0.5),
        0.5 * (rows_total * WB * C // 16) ** (-0.5),
        0.5 * COND ** (-0.5),
        0.5 * C ** (-0.5),
        0.5 * (C // 4) ** (-0.5),
        0.1,
    ]


def adam(weight, grad, first, second, rate):
    first = BETA_ONE * first + (1.0 - BETA_ONE) * grad
    second = BETA_TWO * second + (1.0 - BETA_TWO) * grad * grad
    update = (
        first
        / (1.0 - BETA_ONE**STEP_NO)
        / (jnp.sqrt(second / (1.0 - BETA_TWO**STEP_NO)) + ADAM_EPS)
    )
    return (weight - rate * (update + DECAY * weight), first, second)


def shards(
    frames,
    valid,
    flags,
    actions,
    states,
    latent,
    w_enc,
    w_lstm,
    w_fc,
    w_cond,
    w_deconv,
    w_mask,
    vector,
    m_enc,
    m_lstm,
    m_fc,
    m_cond,
    m_deconv,
    m_mask,
    m_vector,
    v_enc,
    v_lstm,
    v_fc,
    v_cond,
    v_deconv,
    v_mask,
    v_vector,
):
    clips = frames.shape[0]
    out_rows = frames.shape[3] // 2
    out_cols = frames.shape[4] // 2
    b_enc, g_enc, s_enc, b_lstm, b_fc, b_dec, b_mask = split_vector(vector)
    k_enc = w_enc.astype(jnp.bfloat16)
    k_lstm = w_lstm.astype(jnp.bfloat16)
    k_fc = w_fc.astype(jnp.bfloat16)
    k_dec = w_deconv.astype(jnp.bfloat16)
    images = jnp.transpose(frames, (1, 0, 3, 4, 2))
    padded = padded_2(images, (("row", 2),), 2)
    padded = jnp.pad(padded, ((0, 0), (0, 0), (0, 0), (2, 2), (0, 0)))
    valid_steps = jnp.transpose(valid.astype(jnp.float32), (1, 0, 2, 3))
    presence = flags.astype(jnp.float32)
    conditions = jnp.concatenate(
        [
            actions * presence[..., :1],
            states * presence[..., 1:],
            jnp.broadcast_to(latent[:, None, :], (clips, actions.shape[1], latent.shape[1])),
        ],
        -1,
    )
    conditions = jnp.transpose(conditions, (1, 0, 2))
    valid_count = lax.psum(jnp.sum(valid_steps), ("clip", "row"))
    inv_count = 1.0 / valid_count

    def advance(carry, image_pad):
        hidden, cell = carry
        pre = product(patches(image_pad, 2, out_rows, out_cols), k_enc, "byxk,kc->byxc") + b_enc
        encoded = norm_act(pre, g_enc, s_enc).astype(jnp.bfloat16)
        joined = jnp.concatenate([encoded, hidden], -1)
        joined_pad = padded_2(joined, (("row", 1),), 2)
        joined_pad = jnp.pad(joined_pad, ((0, 0), (0, 0), (2, 2), (0, 0)))
        gates = (
            product(patches(joined_pad, 1, out_rows, out_cols), k_lstm, "byxk,kg->byxg") + b_lstm
        )
        new_hidden, new_cell = cell_step(gates, cell)
        hidden_low = new_hidden.astype(jnp.bfloat16)
        part = product(hidden_low.reshape(clips, out_rows, -1), k_fc, "bjk,jnk->bn")
        part = lax.psum(part, "row")
        upper = product(hidden_low, k_dec, "byxc,cd->byxd")
        return ((hidden_low, new_cell), (pre, joined_pad, gates, cell, hidden_low, part, upper))

    start = (
        jnp.zeros((clips, out_rows, out_cols, C), jnp.bfloat16),
        jnp.zeros((clips, out_rows, out_cols, C), jnp.float32),
    )
    _, saved = lax.scan(advance, start, padded[:-1])
    pre_all, joined_all, gates_all, cells_all, hidden_all, summed_all, uppers = saved
    targets = images[1:].astype(jnp.float32)

    def local_head(item):
        summed_t, upper_t, image_pad, target, mask, cond = item

        def error_of(summed_t, upper_t, w_cond, w_mask, b_fc, b_dec, b_mask):
            logits = summed_t + jnp.dot(cond, w_cond, precision=HIGH) + b_fc
            upper_full = upsample(upper_t) + b_dec
            result = predict(logits, upper_full, w_mask, b_mask, image_pad.astype(jnp.float32))
            return jnp.sum(mask * jnp.sum((result - target) ** 2, -1))

        error, pullback = jax.vjp(error_of, summed_t, upper_t, w_cond, w_mask, b_fc, b_dec, b_mask)
        return (error, pullback(inv_count))

    head_inputs = (summed_all, uppers, padded[:-1], targets, valid_steps, conditions)

    def retreat(carry, item):
        (
            back_hidden,
            back_cell,
            acc_enc,
            acc_lstm,
            acc_dec,
            acc_benc,
            acc_genc,
            acc_senc,
            acc_blstm,
        ) = carry
        saved_t, head_t = item
        pre, joined_pad, gates, cell_prev, hidden_low, image_pad = saved_t
        error, pulled_t = local_head(head_t)
        d_sum = lax.psum(pulled_t[0], "row")
        d_upper = pulled_t[1]
        extra = (error, pulled_t[2:])
        d_sum_low = d_sum.astype(jnp.bfloat16)
        d_upper_low = d_upper.astype(jnp.bfloat16)
        acc_dec = acc_dec + product(hidden_low, d_upper_low, "byxc,byxd->cd")
        back = back_hidden + product(d_upper_low, k_dec, "byxd,cd->byxc")
        back = back + product(d_sum_low, k_fc, "bn,jnk->bjk").reshape(back_hidden.shape)
        _, cell_pull = jax.vjp(cell_step, gates, cell_prev)
        d_gates, back_cell = cell_pull((back, back_cell))
        d_gates_low = d_gates.astype(jnp.bfloat16)
        acc_blstm = acc_blstm + jnp.sum(d_gates, (0, 1, 2))
        acc_lstm = acc_lstm + product(
            patches(joined_pad, 1, out_rows, out_cols), d_gates_low, "byxk,byxg->kg"
        )
        d_pad = unpatch(product(d_gates_low, k_lstm, "byxg,kg->byxk"), joined_pad.shape, 1)[
            :, :, 2:-2, :
        ]
        from_below = passed_along(d_pad[:, :2], "row", -1)
        from_above = passed_along(d_pad[:, -2:], "row", 1)
        d_joined = d_pad[:, 2:-2].at[:, -2:].add(from_below).at[:, :2].add(from_above)
        _, norm_pull = jax.vjp(norm_act, pre, g_enc, s_enc)
        d_pre, d_gain, d_shift = norm_pull(d_joined[..., :C])
        acc_benc = acc_benc + jnp.sum(d_pre, (0, 1, 2))
        acc_genc = acc_genc + d_gain
        acc_senc = acc_senc + d_shift
        acc_enc = acc_enc + product(
            patches(image_pad, 2, out_rows, out_cols), d_pre.astype(jnp.bfloat16), "byxk,byxc->kc"
        )
        new_carry = (
            d_joined[..., C:],
            back_cell,
            acc_enc,
            acc_lstm,
            acc_dec,
            acc_benc,
            acc_genc,
            acc_senc,
            acc_blstm,
        )
        return (new_carry, (d_sum_low, extra))

    zeros_state = jnp.zeros((clips, out_rows, out_cols, C), jnp.float32)
    zeros_small = jnp.zeros((C,), jnp.float32)
    init = (
        zeros_state,
        zeros_state,
        jnp.zeros(w_enc.shape, jnp.float32),
        jnp.zeros(w_lstm.shape, jnp.float32),
        jnp.zeros(w_deconv.shape, jnp.float32),
        zeros_small,
        zeros_small,
        zeros_small,
        jnp.zeros((4 * C,), jnp.float32),
    )
    final, (d_sums_low, extra) = lax.scan(
        retreat,
        init,
        ((pre_all, joined_all, gates_all, cells_all, hidden_all, padded[:-1]), head_inputs),
        reverse=True,
    )
    error_sum = jnp.sum(extra[0])
    head_sums = [jnp.sum(grad, 0) for grad in extra[1]]
    acc_enc, acc_lstm, acc_dec, acc_benc, acc_genc, acc_senc, acc_blstm = final[2:]
    flat_hidden = hidden_all.reshape(hidden_all.shape[0], clips, out_rows, -1)
    d_fc = lax.psum(
        product(flat_hidden, d_sums_low, "tbjk,tbn->jnk").astype(jnp.bfloat16), "clip"
    ).astype(jnp.float32)
    fc_squares = jnp.sum(d_fc * d_fc) / lax.axis_size("clip")
    d_vector = jnp.concatenate(
        [acc_benc, acc_genc, acc_senc, acc_blstm, head_sums[2], head_sums[3], head_sums[4]]
    )
    d_enc, d_lstm, d_cond, d_dec, d_mask, d_vector, loss_sum, squares = lax.psum(
        (acc_enc, acc_lstm, head_sums[0], acc_dec, head_sums[1], d_vector, error_sum, fc_squares),
        ("clip", "row"),
    )
    grads = (d_enc, d_lstm, d_fc, d_cond, d_dec, d_mask, d_vector)
    for index in (0, 1, 3, 4, 5, 6):
        squares = squares + jnp.sum(grads[index] * grads[index])
    grad_norm = jnp.sqrt(squares)
    factor = CLIP_NORM / jnp.maximum(grad_norm, CLIP_NORM)
    rates = learning_rates(w_fc.shape[0] * lax.axis_size("row"))
    weights = (w_enc, w_lstm, w_fc, w_cond, w_deconv, w_mask, vector)
    firsts = (m_enc, m_lstm, m_fc, m_cond, m_deconv, m_mask, m_vector)
    seconds = (v_enc, v_lstm, v_fc, v_cond, v_deconv, v_mask, v_vector)
    new = [
        adam(weights[index], grads[index] * factor, firsts[index], seconds[index], rates[index])
        for index in range(7)
    ]
    return (
        loss_sum,
        valid_count,
        grad_norm,
        new[0][0],
        new[1][0],
        new[2][0],
        new[3][0],
        new[4][0],
        new[5][0],
        new[6][0],
        new[0][1],
        new[1][1],
        new[2][1],
        new[3][1],
        new[4][1],
        new[5][1],
        new[6][1],
        new[0][2],
        new[1][2],
        new[2][2],
        new[3][2],
        new[4][2],
        new[5][2],
        new[6][2],
    )


def solution(mesh):
    placed = (
        P("clip", None, None, "row", None),
        P("clip", None, "row", None),
        P("clip", None, None),
        P("clip", None, None),
        P("clip", None, None),
        P("clip", None),
        P(),
        P(),
        P("row", None, None),
        P(),
        P(),
        P(),
        P(),
        P(),
        P(),
        P("row", None, None),
        P(),
        P(),
        P(),
        P(),
        P(),
        P(),
        P("row", None, None),
        P(),
        P(),
        P(),
        P(),
    )
    return jax.shard_map(
        shards,
        mesh=mesh,
        in_specs=placed,
        out_specs=(
            P(),
            P(),
            P(),
            P(),
            P(),
            P("row", None, None),
            P(),
            P(),
            P(),
            P(),
            P(),
            P(),
            P("row", None, None),
            P(),
            P(),
            P(),
            P(),
            P(),
            P(),
            P("row", None, None),
            P(),
            P(),
            P(),
            P(),
        ),
        check_vma=False,
    )
```

profile of v0, /device:TPU:0, one launch (start us, length us, event | category | flops | bytes accessed | tf_op | source)
XLA Modules:
  0.0 3529.7 jit_solution(4021180090912550064)
XLA Ops:
  21.3 44.1 %psum.95 = f32[]{:T(128)} all-reduce(f32[]{:T(128)} %fusion.103), channel_id=1, replica_groups=mesh['clip'=4,'row'=8] {'clip','row'}, use_global_device_ids=true, to_apply=%region_6.7 | all-reduce | flops 1 | bytes 8 | tf_op jit(solution)/shard_map/psum | solution.py:203
  72.4 7.1 copy.137
  79.5 887.7 %while.82 = (s32[]{:T(128)}, bf16[4,2,32,32]{3,2,1,0:T(8,128)(2,1)S(1)}, f32[4,2,32,32]{3,2,1,0:T(8,128)S(1)}, f32[16,4,2,32,32]{4,3,2,1,0:T(8,128)}, bf16[16,4,...) while((s32[]{:T(128)}, ...), condition=%wide.region_4.5_spmd.clone, body=%wide.region_0.4_spmd.clone.sunk | while | flops 113667304 | bytes 7654937 | solution.py:227
  106.0 3.0 collective-permute-start.1
  119.1 15.7 psum.109
  162.8 3.0 collective-permute-start.1
  175.9 14.4 psum.109
  218.2 3.0 collective-permute-start.1
  231.4 14.3 psum.109
  273.5 3.0 collective-permute-start.1
  286.7 14.4 psum.109
  329.0 3.0 collective-permute-start.1
  342.2 14.3 psum.109
  384.4 3.0 collective-permute-start.1
  397.5 14.4 psum.109
  452.9 14.3 psum.109
  508.2 14.4 psum.109
  550.6 3.0 collective-permute-start.1
  563.7 14.3 psum.109
  619.0 14.4 psum.109
  674.4 14.3 psum.109
  729.7 14.4 psum.109
  785.2 14.3 psum.109
  840.5 14.4 psum.109
  882.9 3.0 collective-permute-start.1
  896.0 14.3 psum.109
  951.3 14.4 psum.109
  972.1 2295.5 %while.83 = (s32[]{:T(128)}, f32[4,2,32,32]{3,2,1,0:T(8,128)}, f32[4,2,32,32]{3,2,1,0:T(8,128)}, f32[75,32]{0,1:T(8,128)}, f32[1600,128]{1,0:T(8,128)}, /*index=...) while((s32[]{:T(128)}, f32[4,2,32,32]{3,2,1,0:T(8,128)}, ...), condition=%wide.region_53.54_spmd.clone, body=%wide.region_7.53_spmd.clone.sunk | while | flops 246273104 | bytes 28242368 | solution.py:315
  982.6 10.7 multiply_reduce_fusion.47
  998.5 13.6 psum.110
  1125.1 10.7 multiply_reduce_fusion.47
  1141.0 14.7 psum.110
  1268.5 10.7 multiply_reduce_fusion.47
  1284.5 14.8 psum.110
  1412.1 10.7 multiply_reduce_fusion.47
  1428.0 14.8 psum.110
  1555.6 10.7 multiply_reduce_fusion.47
  1571.6 14.8 psum.110
  1699.1 10.7 multiply_reduce_fusion.47
  1715.1 14.8 psum.110
  1842.7 10.7 multiply_reduce_fusion.47
  1858.6 14.8 psum.110
  1986.2 10.7 multiply_reduce_fusion.47
  2002.1 14.8 psum.110
  2129.7 10.7 multiply_reduce_fusion.47
  2145.7 14.8 psum.110
  2273.3 10.7 multiply_reduce_fusion.47
  2289.2 14.8 psum.110
  2416.8 10.7 multiply_reduce_fusion.47
  2432.7 14.8 psum.110
  2560.4 10.7 multiply_reduce_fusion.47
  2576.3 14.8 psum.110
  2703.9 10.7 multiply_reduce_fusion.47
  2719.9 14.8 psum.110
  2847.4 10.7 multiply_reduce_fusion.47
  2863.4 14.8 psum.110
  2990.9 10.7 multiply_reduce_fusion.47
  3006.9 14.8 psum.110
  3134.5 10.7 multiply_reduce_fusion.47
  3150.4 14.8 psum.110
  3272.7 122.1 %all-reduce.60.cloned.1.call-done = f32[1600,128]{1,0:T(8,128)} async-done(((f32[1600,128]{1,0:T(8,128)}), f32[1600,128]{1,0:T(8,128)}) %all-reduce.60.cloned.1.call-update) | async-done | bytes 819216 | tf_op jit(solution)/shard_map/psum | solution.py:332
  3396.8 54.6 %all-reduce.58.cloned.1.call-done = bf16[2,250,1024]{2,1,0:T(8,128)(2,1)} async-done(((bf16[2,250,1024]{2,1,0:T(8,128)(2,1)}), bf16[2,250,1024]{2,1,0:T(8,128)(2,1)}) %all-reduce.58.cloned.1.call-update) | async-done | bytes 1024016 | tf_op jit(solution)/shard_map/psum | solution.py:325
  3454.4 40.4 %all-reduce.54 = (f32[]{:T(128)}, f32[]{:T(128)}, f32[75,32]{0,1:T(8,128)S(1)}, f32[15,250]{1,0:T(8,128)S(1)}, f32[32,128]{1,0:T(8,128)S(1)}, /*index=5*/f32[32,11]{0,1:T(8,128)S(1)}, f32[517]{0:T(1024)S(1)}) all-reduce(f32[]{:T(128)} %reduce_sum.907, f32[]{:T(128)S(6)} %div.345, ...), channel_id=1, replica_groups=mesh['clip'=4,'row'=8] {'clip','row'}, use_global_device_ids=true, to_apply=%region_55.56 | all-reduce | flops 11117 | bytes 88936 | tf_op jit(solution)/shard_map/psum | solution.py:332
  3502.5 5.4 multiply_subtract_fusion
  (4230 shorter events, 2554.3 us)
Async XLA Ops:
  7.2 3387.6 %all-reduce.60.cloned.1.call-start = ((), (), s32[]{:S(2)}) async-start(), calls=%async_computation.1 | async-start | bytes 1638400 | tf_op jit(solution)/shard_map/psum | solution.py:332
  8.3 63.1 %collective-permute-start.4 = (bf16[17,4,2,64,3]{3,1,4,2,0:T(4,128)(2,1)S(1)}, bf16[17,4,2,64,3]{3,1,4,2,0:T(4,128)(2,1)S(1)}, u32[]{:S(2)}, u32[]{:S(2)}) collective-permute-start(bf16[17,4,2,64,3]{3,1,4,2,0:T(4,128)(2,1)S(1)} %get-tuple-element.2044), channel_id=1, source_target_pairs={{0,1},{1,2},{2,3},{3,4},{4,5},{5,6},{6,7},{8,9},{9,10},{10,11},{11... | collective-permute-start | bytes 156680 | tf_op jit(solution)/shard_map/ppermute | solution.py:33
  10.7 60.8 %collective-permute-start.5 = (bf16[17,4,2,64,3]{3,1,4,2,0:T(4,128)(2,1)S(1)}, bf16[17,4,2,64,3]{3,1,4,2,0:T(4,128)(2,1)S(1)}, u32[]{:S(2)}, u32[]{:S(2)}) collective-permute-start(bf16[17,4,2,64,3]{3,1,4,2,0:T(4,128)(2,1)S(1)} %get-tuple-element.2045), channel_id=1, source_target_pairs={{1,0},{2,1},{3,2},{4,3},{5,4},{6,5},{7,6},{9,8},{10,9},{11,10},{12... | collective-permute-start | bytes 156680 | tf_op jit(solution)/shard_map/ppermute | solution.py:35
  104.7 5.1 collective-permute-start
  106.0 3.9 collective-permute-start.1
  161.5 5.1 collective-permute-start
  162.8 3.9 collective-permute-start.1
  216.9 5.1 collective-permute-start
  218.2 3.9 collective-permute-start.1
  272.2 5.1 collective-permute-start
  273.5 3.9 collective-permute-start.1
  327.7 5.1 collective-permute-start
  329.0 3.9 collective-permute-start.1
  383.1 5.1 collective-permute-start
  384.4 3.9 collective-permute-start.1
  438.5 5.1 collective-permute-start
  493.8 5.1 collective-permute-start
  549.3 5.1 collective-permute-start
  550.6 3.9 collective-permute-start.1
  604.5 5.1 collective-permute-start
  605.8 3.9 collective-permute-start.1
  660.0 5.1 collective-permute-start
  715.3 5.1 collective-permute-start
  716.6 3.9 collective-permute-start.1
  770.8 5.1 collective-permute-start
  826.1 5.1 collective-permute-start
  827.4 3.9 collective-permute-start.1
  881.6 5.1 collective-permute-start
  882.9 3.9 collective-permute-start.1
  936.9 5.1 collective-permute-start
  938.2 3.9 collective-permute-start.1
  1020.1 89.5 %collective-permute-start.2 = (f32[4,2,32,64]{3,2,1,0:T(8,128)}, f32[4,2,32,64]{3,2,1,0:T(8,128)}, u32[]{:S(2)}, u32[]{:S(2)}) collective-permute-start(f32[4,2,32,64]{3,2,1,0:T(8,128)} %get-tuple-element.2699), channel_id=1, source_target_pairs={{0,1},{1,2},{2,3},{3,4},{4,5},{5,6},{6,7},{8,9},{9,10},{10,11},{11... | collective-permute-start | bytes 196616 | tf_op jit(solution)/shard_map/while/body/eval_jaxpr/ppermute | solution.py:45
  1022.5 87.1 %collective-permute-start.3 = (f32[4,2,32,64]{3,2,1,0:T(8,128)}, f32[4,2,32,64]{3,2,1,0:T(8,128)}, u32[]{:S(2)}, u32[]{:S(2)}) collective-permute-start(f32[4,2,32,64]{3,2,1,0:T(8,128)} %get-tuple-element.2700), channel_id=1, source_target_pairs={{1,0},{2,1},{3,2},{4,3},{5,4},{6,5},{7,6},{9,8},{10,9},{11,10},{12... | collective-permute-start | bytes 196616 | tf_op jit(solution)/shard_map/while/body/eval_jaxpr/ppermute | solution.py:45
  1163.7 89.4 %collective-permute-start.2 = (f32[4,2,32,64]{3,2,1,0:T(8,128)}, f32[4,2,32,64]{3,2,1,0:T(8,128)}, u32[]{:S(2)}, u32[]{:S(2)}) collective-permute-start(f32[4,2,32,64]{3,2,1,0:T(8,128)} %get-tuple-element.2699), channel_id=1, source_target_pairs={{0,1},{1,2},{2,3},{3,4},{4,5},{5,6},{6,7},{8,9},{9,10},{10,11},{11... | collective-permute-start | bytes 196616 | tf_op jit(solution)/shard_map/while/body/eval_jaxpr/ppermute | solution.py:45
  1165.7 87.4 %collective-permute-start.3 = (f32[4,2,32,64]{3,2,1,0:T(8,128)}, f32[4,2,32,64]{3,2,1,0:T(8,128)}, u32[]{:S(2)}, u32[]{:S(2)}) collective-permute-start(f32[4,2,32,64]{3,2,1,0:T(8,128)} %get-tuple-element.2700), channel_id=1, source_target_pairs={{1,0},{2,1},{3,2},{4,3},{5,4},{6,5},{7,6},{9,8},{10,9},{11,10},{12... | collective-permute-start | bytes 196616 | tf_op jit(solution)/shard_map/while/body/eval_jaxpr/ppermute | solution.py:45
  1307.3 89.4 %collective-permute-start.2 = (f32[4,2,32,64]{3,2,1,0:T(8,128)}, f32[4,2,32,64]{3,2,1,0:T(8,128)}, u32[]{:S(2)}, u32[]{:S(2)}) collective-permute-start(f32[4,2,32,64]{3,2,1,0:T(8,128)} %get-tuple-element.2699), channel_id=1, source_target_pairs={{0,1},{1,2},{2,3},{3,4},{4,5},{5,6},{6,7},{8,9},{9,10},{10,11},{11... | collective-permute-start | bytes 196616 | tf_op jit(solution)/shard_map/while/body/eval_jaxpr/ppermute | solution.py:45
  1309.2 87.4 %collective-permute-start.3 = (f32[4,2,32,64]{3,2,1,0:T(8,128)}, f32[4,2,32,64]{3,2,1,0:T(8,128)}, u32[]{:S(2)}, u32[]{:S(2)}) collective-permute-start(f32[4,2,32,64]{3,2,1,0:T(8,128)} %get-tuple-element.2700), channel_id=1, source_target_pairs={{1,0},{2,1},{3,2},{4,3},{5,4},{6,5},{7,6},{9,8},{10,9},{11,10},{12... | collective-permute-start | bytes 196616 | tf_op jit(solution)/shard_map/while/body/eval_jaxpr/ppermute | solution.py:45
  1450.8 89.4 %collective-permute-start.2 = (f32[4,2,32,64]{3,2,1,0:T(8,128)}, f32[4,2,32,64]{3,2,1,0:T(8,128)}, u32[]{:S(2)}, u32[]{:S(2)}) collective-permute-start(f32[4,2,32,64]{3,2,1,0:T(8,128)} %get-tuple-element.2699), channel_id=1, source_target_pairs={{0,1},{1,2},{2,3},{3,4},{4,5},{5,6},{6,7},{8,9},{9,10},{10,11},{11... | collective-permute-start | bytes 196616 | tf_op jit(solution)/shard_map/while/body/eval_jaxpr/ppermute | solution.py:45
  1452.8 87.4 %collective-permute-start.3 = (f32[4,2,32,64]{3,2,1,0:T(8,128)}, f32[4,2,32,64]{3,2,1,0:T(8,128)}, u32[]{:S(2)}, u32[]{:S(2)}) collective-permute-start(f32[4,2,32,64]{3,2,1,0:T(8,128)} %get-tuple-element.2700), channel_id=1, source_target_pairs={{1,0},{2,1},{3,2},{4,3},{5,4},{6,5},{7,6},{9,8},{10,9},{11,10},{12... | collective-permute-start | bytes 196616 | tf_op jit(solution)/shard_map/while/body/eval_jaxpr/ppermute | solution.py:45
  1594.4 89.3 %collective-permute-start.2 = (f32[4,2,32,64]{3,2,1,0:T(8,128)}, f32[4,2,32,64]{3,2,1,0:T(8,128)}, u32[]{:S(2)}, u32[]{:S(2)}) collective-permute-start(f32[4,2,32,64]{3,2,1,0:T(8,128)} %get-tuple-element.2699), channel_id=1, source_target_pairs={{0,1},{1,2},{2,3},{3,4},{4,5},{5,6},{6,7},{8,9},{9,10},{10,11},{11... | collective-permute-start | bytes 196616 | tf_op jit(solution)/shard_map/while/body/eval_jaxpr/ppermute | solution.py:45
  1596.3 87.4 %collective-permute-start.3 = (f32[4,2,32,64]{3,2,1,0:T(8,128)}, f32[4,2,32,64]{3,2,1,0:T(8,128)}, u32[]{:S(2)}, u32[]{:S(2)}) collective-permute-start(f32[4,2,32,64]{3,2,1,0:T(8,128)} %get-tuple-element.2700), channel_id=1, source_target_pairs={{1,0},{2,1},{3,2},{4,3},{5,4},{6,5},{7,6},{9,8},{10,9},{11,10},{12... | collective-permute-start | bytes 196616 | tf_op jit(solution)/shard_map/while/body/eval_jaxpr/ppermute | solution.py:45
  1737.8 89.4 %collective-permute-start.2 = (f32[4,2,32,64]{3,2,1,0:T(8,128)}, f32[4,2,32,64]{3,2,1,0:T(8,128)}, u32[]{:S(2)}, u32[]{:S(2)}) collective-permute-start(f32[4,2,32,64]{3,2,1,0:T(8,128)} %get-tuple-element.2699), channel_id=1, source_target_pairs={{0,1},{1,2},{2,3},{3,4},{4,5},{5,6},{6,7},{8,9},{9,10},{10,11},{11... | collective-permute-start | bytes 196616 | tf_op jit(solution)/shard_map/while/body/eval_jaxpr/ppermute | solution.py:45
  1739.8 87.4 %collective-permute-start.3 = (f32[4,2,32,64]{3,2,1,0:T(8,128)}, f32[4,2,32,64]{3,2,1,0:T(8,128)}, u32[]{:S(2)}, u32[]{:S(2)}) collective-permute-start(f32[4,2,32,64]{3,2,1,0:T(8,128)} %get-tuple-element.2700), channel_id=1, source_target_pairs={{1,0},{2,1},{3,2},{4,3},{5,4},{6,5},{7,6},{9,8},{10,9},{11,10},{12... | collective-permute-start | bytes 196616 | tf_op jit(solution)/shard_map/while/body/eval_jaxpr/ppermute | solution.py:45
  1881.4 89.3 %collective-permute-start.2 = (f32[4,2,32,64]{3,2,1,0:T(8,128)}, f32[4,2,32,64]{3,2,1,0:T(8,128)}, u32[]{:S(2)}, u32[]{:S(2)}) collective-permute-start(f32[4,2,32,64]{3,2,1,0:T(8,128)} %get-tuple-element.2699), channel_id=1, source_target_pairs={{0,1},{1,2},{2,3},{3,4},{4,5},{5,6},{6,7},{8,9},{9,10},{10,11},{11... | collective-permute-start | bytes 196616 | tf_op jit(solution)/shard_map/while/body/eval_jaxpr/ppermute | solution.py:45
  1883.3 87.4 %collective-permute-start.3 = (f32[4,2,32,64]{3,2,1,0:T(8,128)}, f32[4,2,32,64]{3,2,1,0:T(8,128)}, u32[]{:S(2)}, u32[]{:S(2)}) collective-permute-start(f32[4,2,32,64]{3,2,1,0:T(8,128)} %get-tuple-element.2700), channel_id=1, source_target_pairs={{1,0},{2,1},{3,2},{4,3},{5,4},{6,5},{7,6},{9,8},{10,9},{11,10},{12... | collective-permute-start | bytes 196616 | tf_op jit(solution)/shard_map/while/body/eval_jaxpr/ppermute | solution.py:45
  2024.9 89.4 %collective-permute-start.2 = (f32[4,2,32,64]{3,2,1,0:T(8,128)}, f32[4,2,32,64]{3,2,1,0:T(8,128)}, u32[]{:S(2)}, u32[]{:S(2)}) collective-permute-start(f32[4,2,32,64]{3,2,1,0:T(8,128)} %get-tuple-element.2699), channel_id=1, source_target_pairs={{0,1},{1,2},{2,3},{3,4},{4,5},{5,6},{6,7},{8,9},{9,10},{10,11},{11... | collective-permute-start | bytes 196616 | tf_op jit(solution)/shard_map/while/body/eval_jaxpr/ppermute | solution.py:45
  2026.9 87.4 %collective-permute-start.3 = (f32[4,2,32,64]{3,2,1,0:T(8,128)}, f32[4,2,32,64]{3,2,1,0:T(8,128)}, u32[]{:S(2)}, u32[]{:S(2)}) collective-permute-start(f32[4,2,32,64]{3,2,1,0:T(8,128)} %get-tuple-element.2700), channel_id=1, source_target_pairs={{1,0},{2,1},{3,2},{4,3},{5,4},{6,5},{7,6},{9,8},{10,9},{11,10},{12... | collective-permute-start | bytes 196616 | tf_op jit(solution)/shard_map/while/body/eval_jaxpr/ppermute | solution.py:45
  2168.5 89.4 %collective-permute-start.2 = (f32[4,2,32,64]{3,2,1,0:T(8,128)}, f32[4,2,32,64]{3,2,1,0:T(8,128)}, u32[]{:S(2)}, u32[]{:S(2)}) collective-permute-start(f32[4,2,32,64]{3,2,1,0:T(8,128)} %get-tuple-element.2699), channel_id=1, source_target_pairs={{0,1},{1,2},{2,3},{3,4},{4,5},{5,6},{6,7},{8,9},{9,10},{10,11},{11... | collective-permute-start | bytes 196616 | tf_op jit(solution)/shard_map/while/body/eval_jaxpr/ppermute | solution.py:45
  2170.4 87.4 %collective-permute-start.3 = (f32[4,2,32,64]{3,2,1,0:T(8,128)}, f32[4,2,32,64]{3,2,1,0:T(8,128)}, u32[]{:S(2)}, u32[]{:S(2)}) collective-permute-start(f32[4,2,32,64]{3,2,1,0:T(8,128)} %get-tuple-element.2700), channel_id=1, source_target_pairs={{1,0},{2,1},{3,2},{4,3},{5,4},{6,5},{7,6},{9,8},{10,9},{11,10},{12... | collective-permute-start | bytes 196616 | tf_op jit(solution)/shard_map/while/body/eval_jaxpr/ppermute | solution.py:45
  2312.0 89.3 %collective-permute-start.2 = (f32[4,2,32,64]{3,2,1,0:T(8,128)}, f32[4,2,32,64]{3,2,1,0:T(8,128)}, u32[]{:S(2)}, u32[]{:S(2)}) collective-permute-start(f32[4,2,32,64]{3,2,1,0:T(8,128)} %get-tuple-element.2699), channel_id=1, source_target_pairs={{0,1},{1,2},{2,3},{3,4},{4,5},{5,6},{6,7},{8,9},{9,10},{10,11},{11... | collective-permute-start | bytes 196616 | tf_op jit(solution)/shard_map/while/body/eval_jaxpr/ppermute | solution.py:45
  2313.9 87.4 %collective-permute-start.3 = (f32[4,2,32,64]{3,2,1,0:T(8,128)}, f32[4,2,32,64]{3,2,1,0:T(8,128)}, u32[]{:S(2)}, u32[]{:S(2)}) collective-permute-start(f32[4,2,32,64]{3,2,1,0:T(8,128)} %get-tuple-element.2700), channel_id=1, source_target_pairs={{1,0},{2,1},{3,2},{4,3},{5,4},{6,5},{7,6},{9,8},{10,9},{11,10},{12... | collective-permute-start | bytes 196616 | tf_op jit(solution)/shard_map/while/body/eval_jaxpr/ppermute | solution.py:45
  2455.5 89.4 %collective-permute-start.2 = (f32[4,2,32,64]{3,2,1,0:T(8,128)}, f32[4,2,32,64]{3,2,1,0:T(8,128)}, u32[]{:S(2)}, u32[]{:S(2)}) collective-permute-start(f32[4,2,32,64]{3,2,1,0:T(8,128)} %get-tuple-element.2699), channel_id=1, source_target_pairs={{0,1},{1,2},{2,3},{3,4},{4,5},{5,6},{6,7},{8,9},{9,10},{10,11},{11... | collective-permute-start | bytes 196616 | tf_op jit(solution)/shard_map/while/body/eval_jaxpr/ppermute | solution.py:45
  2457.5 87.4 %collective-permute-start.3 = (f32[4,2,32,64]{3,2,1,0:T(8,128)}, f32[4,2,32,64]{3,2,1,0:T(8,128)}, u32[]{:S(2)}, u32[]{:S(2)}) collective-permute-start(f32[4,2,32,64]{3,2,1,0:T(8,128)} %get-tuple-element.2700), channel_id=1, source_target_pairs={{1,0},{2,1},{3,2},{4,3},{5,4},{6,5},{7,6},{9,8},{10,9},{11,10},{12... | collective-permute-start | bytes 196616 | tf_op jit(solution)/shard_map/while/body/eval_jaxpr/ppermute | solution.py:45
  2599.1 89.3 %collective-permute-start.2 = (f32[4,2,32,64]{3,2,1,0:T(8,128)}, f32[4,2,32,64]{3,2,1,0:T(8,128)}, u32[]{:S(2)}, u32[]{:S(2)}) collective-permute-start(f32[4,2,32,64]{3,2,1,0:T(8,128)} %get-tuple-element.2699), channel_id=1, source_target_pairs={{0,1},{1,2},{2,3},{3,4},{4,5},{5,6},{6,7},{8,9},{9,10},{10,11},{11... | collective-permute-start | bytes 196616 | tf_op jit(solution)/shard_map/while/body/eval_jaxpr/ppermute | solution.py:45
  2601.0 87.4 %collective-permute-start.3 = (f32[4,2,32,64]{3,2,1,0:T(8,128)}, f32[4,2,32,64]{3,2,1,0:T(8,128)}, u32[]{:S(2)}, u32[]{:S(2)}) collective-permute-start(f32[4,2,32,64]{3,2,1,0:T(8,128)} %get-tuple-element.2700), channel_id=1, source_target_pairs={{1,0},{2,1},{3,2},{4,3},{5,4},{6,5},{7,6},{9,8},{10,9},{11,10},{12... | collective-permute-start | bytes 196616 | tf_op jit(solution)/shard_map/while/body/eval_jaxpr/ppermute | solution.py:45
  2742.6 89.4 %collective-permute-start.2 = (f32[4,2,32,64]{3,2,1,0:T(8,128)}, f32[4,2,32,64]{3,2,1,0:T(8,128)}, u32[]{:S(2)}, u32[]{:S(2)}) collective-permute-start(f32[4,2,32,64]{3,2,1,0:T(8,128)} %get-tuple-element.2699), channel_id=1, source_target_pairs={{0,1},{1,2},{2,3},{3,4},{4,5},{5,6},{6,7},{8,9},{9,10},{10,11},{11... | collective-permute-start | bytes 196616 | tf_op jit(solution)/shard_map/while/body/eval_jaxpr/ppermute | solution.py:45
  2744.6 87.4 %collective-permute-start.3 = (f32[4,2,32,64]{3,2,1,0:T(8,128)}, f32[4,2,32,64]{3,2,1,0:T(8,128)}, u32[]{:S(2)}, u32[]{:S(2)}) collective-permute-start(f32[4,2,32,64]{3,2,1,0:T(8,128)} %get-tuple-element.2700), channel_id=1, source_target_pairs={{1,0},{2,1},{3,2},{4,3},{5,4},{6,5},{7,6},{9,8},{10,9},{11,10},{12... | collective-permute-start | bytes 196616 | tf_op jit(solution)/shard_map/while/body/eval_jaxpr/ppermute | solution.py:45
  2886.2 89.3 %collective-permute-start.2 = (f32[4,2,32,64]{3,2,1,0:T(8,128)}, f32[4,2,32,64]{3,2,1,0:T(8,128)}, u32[]{:S(2)}, u32[]{:S(2)}) collective-permute-start(f32[4,2,32,64]{3,2,1,0:T(8,128)} %get-tuple-element.2699), channel_id=1, source_target_pairs={{0,1},{1,2},{2,3},{3,4},{4,5},{5,6},{6,7},{8,9},{9,10},{10,11},{11... | collective-permute-start | bytes 196616 | tf_op jit(solution)/shard_map/while/body/eval_jaxpr/ppermute | solution.py:45
  2888.1 87.4 %collective-permute-start.3 = (f32[4,2,32,64]{3,2,1,0:T(8,128)}, f32[4,2,32,64]{3,2,1,0:T(8,128)}, u32[]{:S(2)}, u32[]{:S(2)}) collective-permute-start(f32[4,2,32,64]{3,2,1,0:T(8,128)} %get-tuple-element.2700), channel_id=1, source_target_pairs={{1,0},{2,1},{3,2},{4,3},{5,4},{6,5},{7,6},{9,8},{10,9},{11,10},{12... | collective-permute-start | bytes 196616 | tf_op jit(solution)/shard_map/while/body/eval_jaxpr/ppermute | solution.py:45
  3029.7 89.4 %collective-permute-start.2 = (f32[4,2,32,64]{3,2,1,0:T(8,128)}, f32[4,2,32,64]{3,2,1,0:T(8,128)}, u32[]{:S(2)}, u32[]{:S(2)}) collective-permute-start(f32[4,2,32,64]{3,2,1,0:T(8,128)} %get-tuple-element.2699), channel_id=1, source_target_pairs={{0,1},{1,2},{2,3},{3,4},{4,5},{5,6},{6,7},{8,9},{9,10},{10,11},{11... | collective-permute-start | bytes 196616 | tf_op jit(solution)/shard_map/while/body/eval_jaxpr/ppermute | solution.py:45
  3031.6 87.4 %collective-permute-start.3 = (f32[4,2,32,64]{3,2,1,0:T(8,128)}, f32[4,2,32,64]{3,2,1,0:T(8,128)}, u32[]{:S(2)}, u32[]{:S(2)}) collective-permute-start(f32[4,2,32,64]{3,2,1,0:T(8,128)} %get-tuple-element.2700), channel_id=1, source_target_pairs={{1,0},{2,1},{3,2},{4,3},{5,4},{6,5},{7,6},{9,8},{10,9},{11,10},{12... | collective-permute-start | bytes 196616 | tf_op jit(solution)/shard_map/while/body/eval_jaxpr/ppermute | solution.py:45
  3173.2 89.4 %collective-permute-start.2 = (f32[4,2,32,64]{3,2,1,0:T(8,128)}, f32[4,2,32,64]{3,2,1,0:T(8,128)}, u32[]{:S(2)}, u32[]{:S(2)}) collective-permute-start(f32[4,2,32,64]{3,2,1,0:T(8,128)} %get-tuple-element.2699), channel_id=1, source_target_pairs={{0,1},{1,2},{2,3},{3,4},{4,5},{5,6},{6,7},{8,9},{9,10},{10,11},{11... | collective-permute-start | bytes 196616 | tf_op jit(solution)/shard_map/while/body/eval_jaxpr/ppermute | solution.py:45
  3175.2 87.4 %collective-permute-start.3 = (f32[4,2,32,64]{3,2,1,0:T(8,128)}, f32[4,2,32,64]{3,2,1,0:T(8,128)}, u32[]{:S(2)}, u32[]{:S(2)}) collective-permute-start(f32[4,2,32,64]{3,2,1,0:T(8,128)} %get-tuple-element.2700), channel_id=1, source_target_pairs={{1,0},{2,1},{3,2},{4,3},{5,4},{6,5},{7,6},{9,8},{10,9},{11,10},{12... | collective-permute-start | bytes 196616 | tf_op jit(solution)/shard_map/while/body/eval_jaxpr/ppermute | solution.py:45
  3267.7 183.6 %all-reduce.58.cloned.1.call-start = ((), (), s32[]{:S(2)}) async-start(), calls=%async_computation | async-start | bytes 2097152 | tf_op jit(solution)/shard_map/psum | solution.py:325
  (842 other events, 8475.7 us)
Sparse Core Ops, SparseCore 0:
  3267.8 126.9 all-reduce.59
  3398.4 52.8 all-reduce.57
where the time goes:
time: 3550 us; the launch traced here: 3530 us
  local copies, waits for them, and re-layouts  1850 us (52%)
  blocking collectives  551 us (16%)
  other arithmetic  521 us (15%)
  matrix products  264 us (7%)
  waiting for transfers between devices  179 us (5%)
  starting transfers between devices  125 us (4%)
    slice x864, local copies, waits for them, and re-layouts, patches(): padded[:, top:top + stride * (out_rows - 1) + 1:stride, left:left + strid...  1370 us
    psum x16, blocking collectives, retreat(): d_sum = lax.psum(pulled_t[0], 'row')  236 us
    psum x16, blocking collectives, advance(): part = lax.psum(part, 'row')  231 us
    reduce_sum x16, other arithmetic, predict(): mixing[..., offset:offset + 1]  172 us
    dot_general x161, matrix products, product(): return jnp.einsum(form, left, right, preferred_element_type=jnp.float32)  165 us
    concatenate x64, local copies, waits for them, and re-layouts, patches(): return jnp.concatenate(pieces, -1)  138 us
    psum x1, waiting for transfers between devices, shards(): lax.psum((acc_enc, acc_lstm, head_sums[0], acc_dec, head_sums[1], d_vecto...  122 us
    dynamic_update_slice x80, local copies, waits for them, and re-layouts, shards(): lax.scan(retreat, init, ((pre_all, joined_all, gates_all, cells_all, hidd...  101 us

commit v1 on v0

--- a/solution.py
+++ b/solution.py
@@ -1,6 +1,11 @@
+import functools
+
 import jax
 import jax.numpy as jnp
+import numpy as np
 from jax import lax
+from jax.experimental import pallas as pl
+from jax.experimental.pallas import tpu as pltpu
 from jax.sharding import PartitionSpec as P
 
 C = 32
@@ -149,7 +154,7 @@
     return (weight - rate * (update + DECAY * weight), first, second)
 
 
-def shards(
+def strips(
     frames,
     valid,
     flags,
@@ -374,6 +379,544 @@
     )
 
 
+LANES = 128
+TILES = 4
+BANDS = 4
+HALVES = 2
+FAR = 1
+WIN = 9 * 16
+BF = jnp.bfloat16
+F32 = jnp.float32
+VMEM_BYTES = 56 * 1024 * 1024
+
+
+def window_places():
+    places = np.zeros((4, WIN, 32), np.float32)
+    encoder = np.zeros((WIN, KK * 3), np.float32)
+    for sub in range(4):
+        for tap in range(KK):
+            off_y = tap // KS - 2 + sub // 2
+            off_x = tap % KS - 2 + sub % 2
+            block = (off_y // 2 + 1) * 3 + off_x // 2 + 1
+            base = block * 16 + (off_y % 2) * 8 + (off_x % 2) * 4
+            for channel in range(3):
+                places[sub, base + channel, tap] = 1.0
+                if sub == 0:
+                    encoder[base + channel, tap * 3 + channel] = 1.0
+    return places, encoder
+
+
+def lane_places():
+    lane = lax.broadcasted_iota(jnp.int32, (8, LANES), 1)
+    return lane % WB, lane // WB
+
+
+def moved(tile, lanes, d_col, d_band):
+    if d_col == 0 and d_band == 0:
+        return tile
+    col, band = lanes
+    rows = tile.shape[0]
+    shift = (-(WB * d_band + d_col)) % LANES
+    rolled = pltpu.roll(tile.reshape(rows // 8, 8, LANES), shift, 2)
+    keep = None
+    for place, delta, count in ((col, d_col, WB), (band, d_band, BANDS)):
+        if delta > 0:
+            inside = place < count - delta
+        elif delta < 0:
+            inside = place >= -delta
+        else:
+            continue
+        keep = inside if keep is None else keep & inside
+    return jnp.where(keep[None], rolled, 0.0).reshape(rows, LANES)
+
+
+def spread(tiles, lanes, reach, target, width, start):
+    rows = tiles[0].shape[0]
+    for index in range(TILES + 2 * reach):
+        tile = index - reach
+        for shift in range(2 * reach + 1):
+            place = shift * width + start
+            target[index, place : place + rows, :] = moved(
+                tiles[tile % TILES], lanes, shift - reach, tile // TILES
+            ).astype(target.dtype)
+
+
+def stacked(ref, tile, count):
+    rows = count * ref.shape[1]
+    return jnp.concatenate(
+        [ref[tile : tile + count].reshape(rows, LANES), ref[tile + 1 : tile + 1 + count].reshape(rows, LANES)],
+        axis=1,
+    )
+
+
+def nn(left, right):
+    return lax.dot_general(left, right, (((1,), (0,)), ((), ())), preferred_element_type=F32)
+
+
+def nt(left, right):
+    return lax.dot_general(left, right, (((1,), (1,)), ((), ())), preferred_element_type=F32)
+
+
+def logistic(v):
+    return 0.5 * jnp.tanh(0.5 * v) + 0.5
+
+
+def image_tiles(x_ref, t):
+    return [x_ref[t, tile].astype(F32) for tile in range(TILES)]
+
+
+def block_swap(parts, band):
+    swapped = []
+    for out in range(BANDS):
+        total = None
+        for part in range(BANDS):
+            shift = (WB * (part - out)) % LANES
+            value = parts[part] if shift == 0 else pltpu.roll(parts[part], shift, 1)
+            total = value if total is None else jnp.where(band == part, value, total)
+        swapped.append(total)
+    return swapped
+
+
+def twice(tile):
+    return jnp.concatenate([tile, tile], axis=1)
+
+
+def forward_kernel(
+    half_ref, x_ref, we_ref, wx_ref, wh_ref, bias_ref,
+    enc_ref, hid_ref, act_ref, cell_ref, strip_ref,
+    win_s, enc_s, hid_s, state_s,
+):
+    steps = enc_ref.shape[0]
+    lanes = lane_places()
+
+    def encode(t, _):
+        spread(image_tiles(x_ref, t), lanes, 1, win_s, 16, 0)
+        tiles = []
+        for two in range(0, TILES, 2):
+            pre = nn(we_ref[...], stacked(win_s, two, 3)) + twice(bias_ref[0:C])
+            centered = pre - jnp.mean(pre, 0, keepdims=True)
+            scale = lax.rsqrt(jnp.mean(centered * centered, 0, keepdims=True) + NORM_EPS)
+            value = centered * scale * twice(bias_ref[C : 2 * C]) + twice(bias_ref[2 * C : 3 * C])
+            value = (value * logistic(value)).astype(BF)
+            for one in range(2):
+                part = value[:, one * LANES : (one + 1) * LANES]
+                enc_ref[t, two + one] = part
+                tiles.append(part.astype(F32))
+        spread(tiles, lanes, 2, enc_s, C, 0)
+        for two in range(0, TILES, 2):
+            gates = nn(wx_ref[...], stacked(enc_s, two, KS)) + twice(bias_ref[3 * C : 7 * C])
+            for one in range(2):
+                act_ref[t, two + one] = gates[:, one * LANES : (one + 1) * LANES]
+        return 0
+
+    lax.fori_loop(0, steps, encode, 0)
+    hid_s[...] = jnp.zeros_like(hid_s)
+    state_s[...] = jnp.zeros_like(state_s)
+
+    def advance(t, _):
+        hidden = []
+        for two in range(0, TILES, 2):
+            sums = nn(wh_ref[...], stacked(hid_s, two, KS))
+            for one in range(2):
+                tile = two + one
+                gates = act_ref[t, tile] + sums[:, one * LANES : (one + 1) * LANES]
+                gate_in = logistic(gates[0:C])
+                gate_keep = logistic(gates[C : 2 * C] + 1.0)
+                gate_out = logistic(gates[2 * C : 3 * C])
+                gate_new = jnp.tanh(gates[3 * C : 4 * C])
+                cell = gate_keep * state_s[tile] + gate_in * gate_new
+                act_ref[t, tile, 0:C] = gate_in
+                act_ref[t, tile, C : 2 * C] = gate_keep
+                act_ref[t, tile, 2 * C : 3 * C] = gate_out
+                act_ref[t, tile, 3 * C : 4 * C] = gate_new
+                state_s[tile] = cell
+                cell_ref[t, tile] = cell
+                low = (gate_out * jnp.tanh(cell)).astype(BF)
+                hid_ref[t, tile] = low
+                hidden.append(low.astype(F32))
+        spread(hidden, lanes, 2, hid_s, C, 0)
+        return 0
+
+    lax.fori_loop(0, steps, advance, 0)
+    own = steps // HALVES
+    base = half_ref[0] * own
+
+    def to_strips(i, _):
+        for pair in range(2):
+            rows = []
+            for low_row in range(2):
+                tile = hid_ref[base + i, 2 * pair + low_row].astype(F32)
+                rows.append(block_swap([tile[8 * q : 8 * q + 8] for q in range(4)], lanes[1]))
+            for band in range(BANDS):
+                strip_ref[2 * band + pair, i] = jnp.concatenate(
+                    [rows[0][band], rows[1][band]], axis=0
+                ).astype(BF)
+        return 0
+
+    lax.fori_loop(0, own, to_strips, 0)
+
+
+def head_kernel(
+    half_ref, x_ref, hid_ref, logit_ref, wd_ref, wdt_ref, wm_ref, wmt_ref, bias_ref, place_ref, placet_ref,
+    back_ref, dlog_ref, dwd_ref, dwm_ref, sums_ref,
+    win_s, dk_s,
+):
+    own = logit_ref.shape[0]
+    base = half_ref[0] * own
+    lanes = lane_places()
+    dwd_ref[...] = jnp.zeros_like(dwd_ref)
+    dwm_ref[...] = jnp.zeros_like(dwm_ref)
+    sums_ref[...] = jnp.zeros_like(sums_ref)
+    row8 = lax.broadcasted_iota(jnp.int32, (8, 2 * LANES), 0)
+    color = (row8 % 4) != 3
+    row16 = lax.broadcasted_iota(jnp.int32, (16, 32), 0)
+    lane16 = lax.broadcasted_iota(jnp.int32, (16, 32), 1)
+
+    def frame(i, _):
+        t = base + i
+        spread(image_tiles(x_ref, t), lanes, 1, win_s, 16, 0)
+        logits = logit_ref[i]
+        powers = jnp.exp(logits - jnp.max(logits, -1, keepdims=True))
+        kernels = powers / jnp.sum(powers, -1, keepdims=True)
+        kernels = jnp.where(row16 == 0, (lane16 == KK // 2).astype(F32), jnp.where(row16 <= NK, kernels, 0.0))
+        kernels_low = kernels.astype(BF)
+        dk_s[...] = jnp.zeros_like(dk_s)
+        for two in range(0, TILES, 2):
+            hidden = jnp.concatenate([hid_ref[t, two], hid_ref[t, two + 1]], axis=1)
+            window = stacked(win_s, two, 3)
+            upper = nn(wdt_ref[...], hidden) + twice(bias_ref[0 : 4 * C])
+            gate = logistic(upper)
+            active = (upper * gate).astype(BF)
+            scores = nn(wm_ref[...], active) + twice(bias_ref[4 * C : 4 * C + 64])
+            scores = scores.reshape(4, 16, 2 * LANES)
+            powers = jnp.exp(scores - jnp.max(scores, 1, keepdims=True))
+            masks = powers / jnp.sum(powers, 1, keepdims=True)
+            after = jnp.concatenate([x_ref[t + 1, two], x_ref[t + 1, two + 1]], axis=1).astype(F32)
+            d_scores = []
+            for sub in range(4):
+                mask_low = masks[sub].astype(BF)
+                spots = nt(place_ref[sub], kernels_low).astype(BF)
+                mixing = nn(spots, mask_low)
+                both = jnp.sum((mixing * window).reshape(18, 8, 2 * LANES), 0)
+                result = both + pltpu.roll(both, 4, 0)
+                goal = after[(sub // 2) * 8 : (sub // 2) * 8 + 8]
+                turned = pltpu.roll(goal, 4, 0)
+                goal = jnp.where((row8 < 4) == (sub % 2 == 0), goal, turned)
+                counted = goal[3:4]
+                diff = jnp.where(color, result - goal, 0.0)
+                weighted = diff * counted
+                lost = weighted * diff
+                sums_ref[192:200] += lost[:, :LANES] + lost[:, LANES:]
+                d_result = 2.0 * weighted
+                d_mix = (window.reshape(18, 8, 2 * LANES) * d_result[None]).reshape(WIN, 2 * LANES).astype(BF)
+                spots_t = nn(kernels_low, placet_ref[sub]).astype(BF)
+                d_mask = nn(spots_t, d_mix)
+                d_spots = nt(mask_low, d_mix)
+                dk_s[...] += lax.dot_general(
+                    d_spots, place_ref[sub].astype(F32), (((1,), (0,)), ((), ())),
+                    preferred_element_type=F32, precision=HIGH,
+                )
+                inner = jnp.sum(masks[sub] * d_mask, 0, keepdims=True)
+                d_scores.append(masks[sub] * (d_mask - inner))
+            d_score = jnp.concatenate(d_scores, axis=0)
+            sums_ref[128:192] += d_score[:, :LANES] + d_score[:, LANES:]
+            d_score_low = d_score.astype(BF)
+            d_active = nn(wmt_ref[...], d_score_low)
+            dwm_ref[...] += nt(active, d_score_low)
+            d_upper = d_active * (gate * (1.0 + upper * (1.0 - gate)))
+            sums_ref[0:128] += d_upper[:, :LANES] + d_upper[:, LANES:]
+            d_upper_low = d_upper.astype(BF)
+            dwd_ref[...] += nt(hidden, d_upper_low)
+            back = nn(wd_ref[...], d_upper_low).astype(BF)
+            for one in range(2):
+                back_ref[i, two + one] = back[:, one * LANES : (one + 1) * LANES]
+        d_kernels = dk_s[...]
+        inner = jnp.sum(d_kernels * kernels, -1, keepdims=True)
+        dlog_ref[i] = kernels * (d_kernels - inner)
+        return 0
+
+    lax.fori_loop(0, own, frame, 0)
+
+
+def backward_kernel(
+    half_ref, x_ref, enc_ref, hid_ref, act_ref, cell_ref, dec_ref, fc_ref, wb_ref, we_ref, bias_ref,
+    dw_ref, dwe_ref, sums_ref,
+    gate_s, keep_s, denc_s, back_s, state_s, win_s, join_s,
+):
+    steps = enc_ref.shape[0]
+    own = steps // HALVES
+    base = half_ref[0] * own
+    lanes = lane_places()
+    back_s[...] = jnp.zeros_like(back_s)
+    state_s[...] = jnp.zeros_like(state_s)
+    dw_ref[...] = jnp.zeros_like(dw_ref)
+    dwe_ref[...] = jnp.zeros_like(dwe_ref)
+    sums_ref[...] = jnp.zeros_like(sums_ref)
+
+    def retreat(step, _):
+        t = steps - 1 - step
+        half = t // own
+        inside = t % own
+        mine = jnp.where(half == half_ref[0], 1.0, 0.0)
+        earlier = jnp.maximum(t - 1, 0)
+        started = jnp.where(t > 0, 1.0, 0.0)
+        tiles = []
+        for tile in range(TILES):
+            pair = tile // 2
+            low_row = tile % 2
+            parts = [
+                fc_ref[half, 2 * band + pair, inside].astype(F32)[8 * low_row : 8 * low_row + 8]
+                for band in range(BANDS)
+            ]
+            from_fc = jnp.concatenate(block_swap(parts, lanes[1]), axis=0)
+            back = back_s[tile] + from_fc + dec_ref[half, inside, tile].astype(F32)
+            gate_in = act_ref[t, tile, 0:C]
+            gate_keep = act_ref[t, tile, C : 2 * C]
+            gate_out = act_ref[t, tile, 2 * C : 3 * C]
+            gate_new = act_ref[t, tile, 3 * C : 4 * C]
+            bent = jnp.tanh(cell_ref[t, tile])
+            d_cell = state_s[tile] + back * gate_out * (1.0 - bent * bent)
+            state_s[tile] = d_cell * gate_keep
+            d_gates = jnp.concatenate(
+                [
+                    d_cell * gate_new * gate_in * (1.0 - gate_in),
+                    d_cell * (cell_ref[earlier, tile] * started) * gate_keep * (1.0 - gate_keep),
+                    back * bent * gate_out * (1.0 - gate_out),
+                    d_cell * gate_in * (1.0 - gate_new * gate_new),
+                ],
+                axis=0,
+            )
+            sums_ref[3 * C : 7 * C] += d_gates * mine
+            low = d_gates.astype(BF)
+            keep_s[t, tile] = low
+            tiles.append(low.astype(F32))
+        for index in range(TILES + 4):
+            tile = index - 2
+            gate_s[index] = moved(tiles[tile % TILES], lanes, 0, tile // TILES).astype(BF)
+        for two in range(0, TILES, 2):
+            sums = nn(wb_ref[...], stacked(gate_s, two, KS))
+            for one in range(2):
+                part = sums[:, one * LANES : (one + 1) * LANES]
+                total = None
+                for shift in range(KS):
+                    value = moved(part[shift * 2 * C : (shift + 1) * 2 * C], lanes, 2 - shift, 0)
+                    total = value if total is None else total + value
+                denc_s[t, two + one] = total[:C]
+                back_s[two + one] = total[C:]
+        return 0
+
+    lax.fori_loop(0, steps, retreat, 0)
+
+    def gather(i, _):
+        t = base + i
+        earlier = jnp.maximum(t - 1, 0)
+        started = jnp.where(t > 0, 1.0, 0.0)
+        spread([enc_ref[t, tile].astype(F32) for tile in range(TILES)], lanes, 2, join_s, 2 * C, 0)
+        spread(
+            [hid_ref[earlier, tile].astype(F32) * started for tile in range(TILES)], lanes, 2, join_s, 2 * C, C
+        )
+        spread(image_tiles(x_ref, t), lanes, 1, win_s, 16, 0)
+        for two in range(0, TILES, 2):
+            d_gates = jnp.concatenate([keep_s[t, two], keep_s[t, two + 1]], axis=1)
+            dw_ref[...] += nt(stacked(join_s, two, KS), d_gates)
+            window = stacked(win_s, two, 3)
+            pre = nn(we_ref[...], window) + twice(bias_ref[0:C])
+            centered = pre - jnp.mean(pre, 0, keepdims=True)
+            scale = lax.rsqrt(jnp.mean(centered * centered, 0, keepdims=True) + NORM_EPS)
+            normal = centered * scale
+            gain = twice(bias_ref[C : 2 * C])
+            value = normal * gain + twice(bias_ref[2 * C : 3 * C])
+            gate = logistic(value)
+            d_out = jnp.concatenate([denc_s[t, two], denc_s[t, two + 1]], axis=1)
+            d_value = d_out * (gate * (1.0 + value * (1.0 - gate)))
+            d_gain = d_value * normal
+            d_normal = d_value * gain
+            d_pre = scale * (
+                d_normal
+                - jnp.mean(d_normal, 0, keepdims=True)
+                - normal * jnp.mean(d_normal * normal, 0, keepdims=True)
+            )
+            sums_ref[0:C] += d_pre[:, :LANES] + d_pre[:, LANES:]
+            sums_ref[C : 2 * C] += d_gain[:, :LANES] + d_gain[:, LANES:]
+            sums_ref[2 * C : 3 * C] += d_value[:, :LANES] + d_value[:, LANES:]
+            dwe_ref[...] += nt(d_pre.astype(BF), window)
+        return 0
+
+    lax.fori_loop(0, own, gather, 0)
+
+
+SMEM_SPEC = pl.BlockSpec(memory_space=pltpu.SMEM)
+VMEM_SPEC = pl.BlockSpec(memory_space=pltpu.VMEM)
+
+
+def call(kernel, outs, scratch, half, *operands):
+    return pl.pallas_call(
+        kernel,
+        out_shape=[jax.ShapeDtypeStruct(shape, kind) for shape, kind in outs],
+        in_specs=[SMEM_SPEC] + [VMEM_SPEC] * len(operands),
+        out_specs=[VMEM_SPEC] * len(outs),
+        scratch_shapes=[pltpu.VMEM(shape, kind) for shape, kind in scratch],
+        compiler_params=pltpu.CompilerParams(vmem_limit_bytes=VMEM_BYTES),
+    )(half, *operands)
+
+
+def columns(values):
+    return jnp.broadcast_to(values[:, None], (values.shape[0], LANES))
+
+
+def pieces_to_clips(block):
+    return lax.all_to_all(block, "row", 0, 0, tiled=True)
+
+
+def whole_clips(
+    frames, valid, flags, actions, states, latent,
+    w_enc, w_lstm, w_fc, w_cond, w_deconv, w_mask, vector,
+    m_enc, m_lstm, m_fc, m_cond, m_deconv, m_mask, m_vector,
+    v_enc, v_lstm, v_fc, v_cond, v_deconv, v_mask, v_vector,
+):
+    clips, shots, _, strip_rows, width = frames.shape
+    steps = shots - 1
+    own = steps // HALVES
+    count = lax.axis_size("row")
+    place = lax.axis_index("row")
+    clip = place // HALVES
+    half = place % HALVES
+    half_1 = half.reshape(1).astype(jnp.int32)
+    b_enc, g_enc, s_enc, b_lstm, b_fc, b_dec, b_mask = split_vector(vector)
+    k_enc = w_enc.astype(BF)
+    k_lstm = w_lstm.astype(BF)
+    k_dec = w_deconv.astype(BF)
+    k_mask = w_mask.astype(BF)
+    places, encoder = window_places()
+    flagged = jnp.pad(valid.astype(BF), ((0, 0), (1, 0), (0, 0), (0, 0)))
+    pieces = jnp.concatenate([frames, flagged[:, :, None]], axis=2)
+    pieces = jnp.repeat(pieces, HALVES, axis=0)
+    pieces = pieces_to_clips(pieces)
+    grid = pieces.reshape(BANDS, 2, shots, 4, 2, 2, width // 2, 2)
+    grid = jnp.transpose(grid, (2, 1, 4, 5, 7, 3, 0, 6))
+    x = grid.reshape(shots, TILES, 16, LANES)
+
+    wide_enc = jnp.einsum("rk,ko->or", jnp.asarray(encoder, BF), k_enc, preferred_element_type=F32).astype(BF)
+    taps = k_lstm.reshape(KS, KS, 2, C, 4 * C)
+    wx = taps[:, :, 0].reshape(KK * C, 4 * C).T
+    wh = taps[:, :, 1].reshape(KK * C, 4 * C).T
+    bias = columns(jnp.concatenate([b_enc, g_enc, s_enc, b_lstm]))
+    cells = (steps, TILES, C, LANES)
+    enc, hid, act, cell, strips_out = call(
+        forward_kernel,
+        [(cells, BF), (cells, BF), ((steps, TILES, 4 * C, LANES), F32), (cells, F32), ((count, own, 16, LANES), BF)],
+        [((6, 48, LANES), BF), ((8, KS * C, LANES), BF), ((8, KS * C, LANES), BF), ((TILES, C, LANES), F32)],
+        half_1, x, wide_enc, wx, wh, bias,
+    )
+    items = clips * steps
+    strip_hid = pieces_to_clips(strips_out).reshape(items, 2, WB * C)
+    k_fc = w_fc.astype(BF).reshape(2, NK * KK, WB, 4, 8)
+    k_fc = jnp.transpose(k_fc, (0, 1, 4, 3, 2)).reshape(2, NK * KK, WB * C)
+    parts = jnp.einsum("mjk,jnk->mn", strip_hid, k_fc, preferred_element_type=F32)
+    summed = jnp.sum(pieces_to_clips(parts.reshape(count, own, NK * KK)), 0)
+    presence = flags.astype(F32)
+    conditions = jnp.concatenate(
+        [
+            actions * presence[..., :1],
+            states * presence[..., 1:],
+            jnp.broadcast_to(latent[:, None, :], (clips, steps, latent.shape[1])),
+        ],
+        -1,
+    )
+    cond = lax.dynamic_slice(conditions, (clip, half * own, 0), (1, own, COND))[0]
+    logits = summed + (jnp.dot(cond, w_cond, precision=HIGH) + b_fc)
+    logits = jnp.pad(
+        logits.reshape(own, NK, KK), ((0, 0), (1, 5), (0, 32 - KK)), constant_values=-1e30
+    )
+    wdt = k_dec.T
+    eye = jnp.eye(4, dtype=BF)
+    pad_mask = jnp.pad(k_mask, ((0, 0), (0, 16 - NM)))
+    wmt = jnp.einsum("ab,cm->acbm", eye, pad_mask).reshape(4 * C, 64)
+    head_bias = columns(
+        jnp.concatenate([jnp.tile(b_dec, 4), jnp.tile(jnp.pad(b_mask, (0, 16 - NM), constant_values=-1e30), 4)])
+    )
+    dec, d_logit, d_dec, d_mask_wide, head_sums = call(
+        head_kernel,
+        [
+            ((own, TILES, C, LANES), BF), ((own, 16, 32), F32), ((C, 4 * C), F32), ((4 * C, 64), F32),
+            ((200, LANES), F32),
+        ],
+        [((6, 48, LANES), F32), ((16, 32), F32)],
+        half_1, x, hid, logits, k_dec, wdt, wmt.T, wmt, head_bias,
+        jnp.asarray(places, BF), jnp.asarray(places.transpose(0, 2, 1), BF),
+    )
+    d_logit = d_logit[:, 1 : NK + 1, :KK].reshape(own, NK * KK)
+    d_sum = lax.all_gather(d_logit.astype(BF), "row").reshape(items, NK * KK)
+    back_fc = jnp.einsum("mn,jnk->mjk", d_sum, k_fc, preferred_element_type=F32).astype(BF)
+    back_fc = pieces_to_clips(back_fc.reshape(count, own, 16, LANES))
+    swap = [(index, index ^ 1) for index in range(count)]
+
+    def in_order(block):
+        other = lax.ppermute(block, "row", swap)
+        return jnp.stack([jnp.where(half == 0, block, other), jnp.where(half == 0, other, block)])
+
+    wb = jnp.transpose(k_lstm.reshape(KS, KS, 2 * C, 4 * C)[::-1], (1, 2, 0, 3)).reshape(KS * 2 * C, KS * 4 * C)
+    d_lstm, d_enc_wide, sums = call(
+        backward_kernel,
+        [((KK * 2 * C, 4 * C), F32), ((C, WIN), F32), ((7 * C, LANES), F32)],
+        [
+            ((8, 4 * C, LANES), BF), ((steps, TILES, 4 * C, LANES), BF), (cells, F32), ((TILES, C, LANES), F32),
+            ((TILES, C, LANES), F32), ((6, 48, LANES), BF), ((8, KS * 2 * C, LANES), BF),
+        ],
+        half_1, x, enc, hid, act, cell, in_order(dec), in_order(back_fc), wb, wide_enc, bias,
+    )
+    d_fc = jnp.einsum("mjk,mn->jnk", strip_hid, d_sum, preferred_element_type=F32).astype(BF)
+    d_fc = jnp.transpose(d_fc.reshape(2, NK * KK, 8, 4, WB), (0, 1, 4, 3, 2)).reshape(2, NK * KK, WB * C)
+    d_fc = lax.psum(d_fc, "clip").astype(F32)
+    fc_squares = jnp.sum(d_fc * d_fc) / lax.axis_size("clip")
+
+    d_enc = jnp.einsum("rk,or->ko", jnp.asarray(encoder, F32), d_enc_wide, precision=HIGH)
+    d_cond = jnp.dot(cond.T, d_logit, precision=HIGH)
+    d_mask = jnp.sum(jnp.stack([d_mask_wide[s * C : (s + 1) * C, s * 16 : s * 16 + NM] for s in range(4)]), 0)
+    line_sums = jnp.sum(sums, 1)
+    head_lines = jnp.sum(head_sums, 1)
+    d_vector = jnp.concatenate(
+        [
+            line_sums,
+            jnp.sum(d_logit, 0),
+            jnp.sum(head_lines[:128].reshape(4, C), 0),
+            jnp.sum(head_lines[128:192].reshape(4, 16), 0)[:NM],
+        ]
+    )
+    loss_part = jnp.sum(head_lines[192:196])
+    count_part = jnp.sum(valid.astype(F32))
+    d_enc, d_lstm, d_cond, d_dec, d_mask, d_vector, loss_sum, squares, valid_count = lax.psum(
+        (d_enc, d_lstm, d_cond, d_dec, d_mask, d_vector, loss_part, fc_squares, count_part), ("clip", "row")
+    )
+    inv_count = 1.0 / valid_count
+    grads = (d_enc, d_lstm, d_fc, d_cond, d_dec, d_mask, d_vector)
+    for index in (0, 1, 3, 4, 5, 6):
+        squares = squares + jnp.sum(grads[index] * grads[index])
+    grad_norm = jnp.sqrt(squares) * inv_count
+    factor = inv_count * (CLIP_NORM / jnp.maximum(grad_norm, CLIP_NORM))
+    rates = learning_rates(w_fc.shape[0] * count)
+    weights = (w_enc, w_lstm, w_fc, w_cond, w_deconv, w_mask, vector)
+    firsts = (m_enc, m_lstm, m_fc, m_cond, m_deconv, m_mask, m_vector)
+    seconds = (v_enc, v_lstm, v_fc, v_cond, v_deconv, v_mask, v_vector)
+    new = [
+        adam(weights[index], grads[index] * factor, firsts[index], seconds[index], rates[index])
+        for index in range(7)
+    ]
+    outs = [loss_sum, valid_count, grad_norm]
+    for kind in range(3):
+        outs.extend(new[index][kind] for index in range(7))
+    return tuple(outs)
+
+
+def shards(frames, *rest):
+    clips, _, _, strip_rows, width = frames.shape
+    count = lax.axis_size("row")
+    one_clip = strip_rows * count // 2 == TILES * BANDS and width // 2 == WB
+    if one_clip and clips * HALVES == count:
+        return whole_clips(frames, *rest)
+    return strips(frames, *rest)
+
+
 def solution(mesh):
     placed = (
         P("clip", None, None, "row", None),

time: 3550 us -> 408 us (0.11)
  local copies, waits for them, and re-layouts: 1850 us -> 67.9 us
  blocking collectives: 551 us -> 54.8 us
  other arithmetic: 521 us -> 32.9 us
  matrix products: 264 us -> 5.62 us
  starting transfers between devices: 125 us -> 19.4 us
  Pallas kernels: 0 us -> 85.4 us
  waiting for transfers between devices: 179 us -> 119 us
    slice x930 -> x6, local copies, waits for them, and re-layouts: 1420 us -> 1.54 us  [the longest x1 0.85 us: whole_clips(): d_logit = d_logit[:, 1:NK + 1, :KK].reshape(own, NK * KK)]
    psum x34 -> x1, blocking collectives: 551 us -> 40.8 us  [whole_clips(): lax.psum((d_enc, d_lstm, d_cond, d_dec, d_mask, d_vector, loss_part, fc_s...]
    reduce_sum x238 -> x16, other arithmetic: 336 us -> 13.6 us  [the longest x6 4.97 us: whole_clips(): squares = squares + jnp.sum(grads[index] * grads[index])]
    dot_general x289 -> x7, matrix products: 264 us -> 5.62 us  [the longest x1 1.4 us: whole_clips(): jnp.einsum('mjk,mn->jnk', strip_hid, d_sum, preferred_element_type=F32)]
    concatenate x65 -> x0, local copies, waits for them, and re-layouts: 138 us -> none  [the longest x64 138 us: patches(): return jnp.concatenate(pieces, -1)]
    ppermute x66 -> x2, starting transfers between devices: 125 us -> 0.32 us  [in_order(): other = lax.ppermute(block, 'row', swap)]
    dynamic_update_slice x96 -> x0, local copies, waits for them, and re-layouts: 111 us -> none  [the longest x80 101 us: shards(): lax.scan(retreat, init, ((pre_all, joined_all, gates_all, cells_all, hidd...]
    pallas_call x0 -> x3, Pallas kernels: none -> 85.4 us  [call(): pl.pallas_call(kernel, out_shape=[jax.ShapeDtypeStruct(shape, kind) for s...]
where the time goes in v1:
time: 408 us; the launch traced here: 406 us
  waiting for transfers between devices  119 us (29%)
  Pallas kernels  85.4 us (21%)
  local copies, waits for them, and re-layouts  67.9 us (17%)
  blocking collectives  54.8 us (13%)
  other arithmetic  32.9 us (8%)
  between operations  21.8 us (5%)
  starting transfers between devices  19.4 us (5%)
  matrix products  5.62 us (1%)
    pallas_call x3, Pallas kernels, call(): pl.pallas_call(kernel, out_shape=[jax.ShapeDtypeStruct(shape, kind) for s...  85.4 us
    psum x1, waiting for transfers between devices, whole_clips(): lax.psum((d_enc, d_lstm, d_cond, d_dec, d_mask, d_vector, loss_part, fc_s...  85.1 us
    psum x1, blocking collectives, whole_clips(): lax.psum((d_enc, d_lstm, d_cond, d_dec, d_mask, d_vector, loss_part, fc_s...  40.8 us
    unnamed x103, local copies, waits for them, and re-layouts  31.6 us
    psum x1, waiting for transfers between devices, whole_clips(): d_fc = lax.psum(d_fc, 'clip').astype(F32)  22.9 us
    all_to_all x4, starting transfers between devices, pieces_to_clips(): return lax.all_to_all(block, 'row', 0, 0, tiled=True)  18.8 us
    all_gather x1, blocking collectives, whole_clips(): d_sum = lax.all_gather(d_logit.astype(BF), 'row').reshape(items, NK * KK)  14 us
    sub x7, other arithmetic, adam(): return (weight - rate * (update + DECAY * weight), first, second)  12 us
  transfers between devices with their start and end apart: 8, of which 5 were waited for; matrix products, arithmetic and copies ran while one was open for 15% of the time, Pallas kernels for 6%

profile of v1, /device:TPU:0, one launch (start us, length us, event | category | flops | bytes accessed | tf_op | source)
XLA Modules:
  0.0 406.5 jit_solution(15127587543301827520)
XLA Ops:
  7.2 1.0 convert_element_type.57
  8.3 1.2 pad_maximum_fusion.2
  9.6 1.1 reshape.152
  10.7 6.3 %all-to-all-start = ((bf16[8,2,8704]{2,1,0:T(2,128)(2,1)}), bf16[8,2,8704]{2,1,0:T(2,128)(2,1)S(1)}, u32[]{:S(2)}, u32[]{:S(2)}) async-start(bf16[8,2,8704]{2,1,0:T(2,128)(2,1)} %reshape.152), calls=%async_computation | async-start | bytes 557056 | tf_op jit(solution)/shard_map/all_to_all | solution.py:768
  17.8 0.8 copy.183
  18.7 0.8 copy.182
  19.5 0.8 fusion.5.we_ref
  20.3 0.7 multiply_bitcast_fusion
  21.0 6.1 %all-to-all-done = bf16[8,2,8704]{2,1,0:T(2,128)(2,1)S(1)} async-done(((bf16[8,2,8704]{2,1,0:T(2,128)(2,1)}), bf16[8,2,8704]{2,1,0:T(2,128)(2,1)S(1)}, u32[]{:S(2)}, u32[]{:S(2)}) %all-to-all-start) | async-done | bytes 278560 | tf_op jit(solution)/shard_map/all_to_all | solution.py:768
  27.5 2.1 copy.180
  29.6 2.8 copy.181
  32.5 1.3 reshape.133.x_ref
  33.7 0.7 broadcast_in_dim.12.bias_ref
  34.5 23.3 %shard_map.478 = (bf16[16,4,32,128]{3,2,1,0:T(8,128)(2,1)}, bf16[16,4,32,128]{3,2,1,0:T(8,128)(2,1)}, f32[16,4,128,128]{3,2,1,0:T(8,128)}, f32[16,4,32,128]{3,2,1,0:T(8,128)}, bf16[8,8,16,128]{3,2,1,0:T(8,128)(2,1)}) custom-call(s32[1]{0:T(128)} %bitcast.half_ref, bf16[17,4,16,128]{3,2,1,0:T(8,128)(2,1)} %reshape.133.x_ref, bf16[32,144]{1,0:T(8,128)(2,1)} %fusion.5.we_ref, ...), custom_call_target="tpu_custom_call" | custom-call | tf_op jit(solution)/shard_map/pallas_call | solution.py:753
  57.8 4.0 all-to-all-start.1
  65.0 2.8 copy.184
  68.5 1.4 copy.189
  69.8 1.4 copy.188
  71.2 1.6 reshape.138
  72.8 1.4 copy.191.wmt_ref
  74.2 1.3 convert_element_type.63.wd_ref
  75.5 1.4 copy.190
  78.2 1.3 tile.21
  79.5 1.2 tile.8
  80.7 1.3 tile.9
  82.0 1.1 copy.197
  83.1 3.0 rev.3
  86.1 1.9 copy.223
  88.2 0.7 copy.204
  88.9 4.1 %copy.198 = f32[2,250,1024]{1,2,0:T(8,128)} copy(f32[2,250,1024]{2,0,1:T(2,128)} %param.46) | data formatting | bytes 4096000 | tf_op args[15]
  93.0 4.2 %copy.199 = f32[2,250,1024]{1,2,0:T(8,128)} copy(f32[2,250,1024]{2,0,1:T(2,128)} %param.53) | data formatting | bytes 4096000 | tf_op args[22]
  97.4 1.0 dot_general.33
  98.4 0.9 convolution_bitcast_fusion
  99.3 5.0 %all-to-all-start.2 = ((f32[8,8,250]{2,1,0:T(8,128)}), f32[8,8,250]{2,1,0:T(8,128)S(1)}, u32[]{:S(2)}, u32[]{:S(2)}) async-start(f32[8,8,250]{2,1,0:T(8,128)} %convolution_bitcast_fusion), calls=%async_computation.2 | async-start | bytes 131072 | tf_op jit(solution)/shard_map/all_to_all | solution.py:768
  104.3 1.7 reshape.140
  106.1 4.2 %all-to-all-done.2 = f32[8,8,250]{2,1,0:T(8,128)S(1)} async-done(((f32[8,8,250]{2,1,0:T(8,128)}), f32[8,8,250]{2,1,0:T(8,128)S(1)}, u32[]{:S(2)}, u32[]{:S(2)}) %all-to-all-start.2) | async-done | bytes 64032 | tf_op jit(solution)/shard_map/all_to_all | solution.py:768
  110.3 0.9 fusion.6
  111.9 0.7 broadcast_in_dim.14.bias_ref
  112.6 38.0 %shard_map.479 = (bf16[8,4,32,128]{3,2,1,0:T(8,128)(2,1)}, f32[8,16,32]{2,1,0:T(8,128)}, f32[32,128]{1,0:T(8,128)}, f32[128,64]{1,0:T(8,128)}, f32[200,128]{1,0:T(8,128)}) custom-call(s32[1]{0:T(128)} %bitcast.half_ref, bf16[17,4,16,128]{3,2,1,0:T(8,128)(2,1)} %reshape.133.x_ref, bf16[16,4,32,128]{3,2,1,0:T(8,128)(2,1)} %get-tuple-element.37.hid_ref, ...), custom_call_target="tpu_custom_call" | custom-call | tf_op jit(solution)/shard_map/pallas_call | solution.py:753
  150.6 0.8 slice.83
  151.4 2.1 slice_reduce_fusion.1
  153.6 14.0 %all_gather.4 = bf16[8,8,250]{2,1,0:T(8,128)(2,1)S(1)} all-gather(bf16[1,8,250]{2,1,0:T(8,128)(2,1)S(1)} %convert_element_type.67), channel_id=1, replica_groups=mesh['clip'=4,'row'=8] {'row'}, dimensions={0}, use_global_device_ids=true | all-gather | bytes 36000 | tf_op jit(solution)/shard_map/all_gather | solution.py:849
  168.3 0.9 reshape.143
  169.2 3.4 all-to-all-start.3
  173.1 1.6 reduce_sum.151
  174.7 1.4 fusion.4
  176.1 1.3 copy.193
  177.5 2.9 copy.194
  182.3 1.0 select_bitcast_fusion.3
  183.3 0.8 pad_maximum_fusion.dec_ref
  184.2 0.8 pad_maximum_fusion.1.fc_ref
  185.0 24.1 %shard_map.480 = (f32[1600,128]{1,0:T(8,128)}, f32[32,144]{1,0:T(8,128)}, f32[224,128]{1,0:T(8,128)}) custom-call(s32[1]{0:T(128)} %bitcast.half_ref, bf16[17,4,16,128]{3,2,1,0:T(8,128)(2,1)} %reshape.133.x_ref, bf16[16,4,32,128]{3,2,1,0:T(8,128)(2,1)} %get-tuple-element.41.enc_ref, bf16[16,4,32,128]{3,2,1,0:T(8,128)(2,1)} %get-tuple-element.37.hid_ref, ...), custom_call_target="tpu_custom_call" | custom-call | tf_op jit(solution)/shard_map/pallas_call | solution.py:753
  209.2 1.0 reduce_sum.163
  210.2 0.9 fusion.35
  211.3 22.9 %all-reduce.8.cloned.1.call-done = bf16[2,250,1024]{1,2,0:T(8,128)(2,1)} async-done(((bf16[2,250,1024]{1,2,0:T(8,128)(2,1)}), bf16[2,250,1024]{1,2,0:T(8,128)(2,1)}) %all-reduce.8.cloned.1.call-update) | async-done | bytes 1024016 | tf_op jit(solution)/shard_map/psum | solution.py:870
  234.2 2.5 fusion.2
  237.3 40.8 %all-reduce.4 = (f32[]{:T(128)}, f32[]{:T(128)}, f32[]{:T(128)}, f32[75,32]{0,1:T(8,128)S(1)}, f32[15,250]{1,0:T(8,128)S(1)}, /*index=5*/f32[32,128]{1,0:T(8,128)S(1)}, f32[32,11]{1,0:T(8,128)S(1)}, f32[517]{0:T(1024)S(1)}) all-reduce(f32[]{:T(128)} %slice_reduce_fusion, ...), channel_id=1, replica_groups=mesh['clip'=4,'row'=8] {'clip','row'}, use_global_device_ids=true, to_apply=%region_3.4 | all-reduce | flops 11118 | bytes 88944 | tf_op jit(solution)/shard_map/psum | solution.py:888
  283.1 85.1 %all-reduce.10.cloned.1.call-done = f32[1600,128]{1,0:T(8,128)} async-done(((f32[1600,128]{1,0:T(8,128)}), f32[1600,128]{1,0:T(8,128)}) %all-reduce.10.cloned.1.call-update) | async-done | bytes 819216 | tf_op jit(solution)/shard_map/psum | solution.py:888
  368.2 2.0 multiply_reduce_fusion
  375.6 6.0 %multiply_subtract_fusion = (f32[2,250,1024]{1,2,0:T(8,128)}, f32[2,250,1024]{1,2,0:T(8,128)}, f32[2,250,1024]{1,2,0:T(8,128)}) fusion(f32[2,250,1024]{1,2,0:T(8,128)S(1)} %copy.184, f32[]{:T(128)S(6)} %mul.376, bf16[2,250,1024]{1,2,0:T(8,128)(2,1)S(1)} %copy-done.1, f32[2,250,1024]{1,2,0:T(8,128)} %copy.198, f32[2,250,1024]{1,2,0:T(8,128)} %copy.199), kind=kLoop, calls=%fused_computation.7 | loop fusion | flops 8704000 | bytes 13312004 | tf_op jit(solution)/shard_map/sub | solution.py:154
  381.6 4.1 %copy.207 = f32[2,250,1024]{2,0,1:T(2,128)} copy(f32[2,250,1024]{1,2,0:T(8,128)} %get-tuple-element.190) | data formatting | bytes 4096000
  385.7 4.3 %copy.209 = f32[2,250,1024]{2,0,1:T(2,128)} copy(f32[2,250,1024]{1,2,0:T(8,128)} %get-tuple-element.191) | data formatting | bytes 4096000
  390.1 2.3 copy.211
  395.0 3.5 multiply_subtract_fusion.1
  (155 shorter events, 18.5 us)
Async XLA Ops:
  7.2 9.8 %copy-start.4 = (f32[1600,128]{1,0:T(8,128)S(1)}, f32[1600,128]{1,0:T(8,128)}, u32[]{:S(2)}) copy-start(f32[1600,128]{1,0:T(8,128)} %param.38) | copy-start | bytes 2457604
  9.4 7.7 %copy-start.38 = (s32[4,16,2]{1,2,0:T(2,128)S(1)}, s32[4,16,2]{1,2,0:T(2,128)}, u32[]{:S(2)}) copy-start(s32[4,16,2]{1,2,0:T(2,128)} %param.33) | copy-start | bytes 1540
  9.6 9.9 %copy-start.21 = (f32[32,11]{0,1:T(8,128)S(1)}, f32[32,11]{0,1:T(8,128)}, u32[]{:S(2)}) copy-start(f32[32,11]{0,1:T(8,128)} %param.42) | copy-start | bytes 4228
  9.6 9.9 %copy-start.12 = (f32[75,32]{0,1:T(8,128)S(1)}, f32[75,32]{0,1:T(8,128)}, u32[]{:S(2)}) copy-start(f32[75,32]{0,1:T(8,128)} %param.37) | copy-start | bytes 28804
  9.6 9.9 %copy-start.20 = (bf16[144,75]{1,0:T(8,128)(2,1)S(1)}, bf16[144,75]{1,0:T(8,128)(2,1)}, u32[]{:S(2)}) copy-start(bf16[144,75]{1,0:T(8,128)(2,1)} %constant.63.clone) | copy-start | bytes 64804
  10.7 16.4 %all-to-all-start = ((bf16[8,2,8704]{2,1,0:T(2,128)(2,1)}), bf16[8,2,8704]{2,1,0:T(2,128)(2,1)S(1)}, u32[]{:S(2)}, u32[]{:S(2)}) async-start(bf16[8,2,8704]{2,1,0:T(2,128)(2,1)} %reshape.152), calls=%async_computation | async-start | bytes 557056 | tf_op jit(solution)/shard_map/all_to_all | solution.py:768
  17.1 10.0 %copy-start.2 = (bf16[1600,128]{1,0:T(8,128)(2,1)}, bf16[1600,128]{1,0:T(8,128)(2,1)S(1)}, u32[]{:S(2)}) copy-start(bf16[1600,128]{1,0:T(8,128)(2,1)S(1)} %convert_element_type.60) | copy-start | bytes 1228804
  29.6 4.2 %slice-start = ((f32[517]{0:T(1024)}), f32[224]{0:T(256)S(1)}, s32[]{:S(2)}) async-start(f32[517]{0:T(1024)} %param.43), calls=%async_computation.6 | async-start | bytes 2048 | tf_op jit(solution)/shard_map/slice | solution.py:58
  32.4 29.4 %copy-start.6 = (s32[4,16,4,64]{3,2,1,0:T(4,128)S(1)}, s32[4,16,4,64]{3,2,1,0:T(4,128)}, u32[]{:S(2)}) copy-start(s32[4,16,4,64]{3,2,1,0:T(4,128)} %param.32) | copy-start | bytes 196612
  32.5 30.0 %copy-start.30 = (f32[517]{0:T(1024)S(1)}, f32[517]{0:T(1024)}, u32[]{:S(2)}) copy-start(f32[517]{0:T(1024)} %param.43) | copy-start | bytes 6208
  57.8 39.6 %all-to-all-start.1 = ((bf16[8,8,16,128]{3,2,1,0:T(8,128)(2,1)}), bf16[8,8,16,128]{3,2,1,0:T(8,128)(2,1)}, u32[]{:S(2)}, u32[]{:S(2)}) async-start(bf16[8,8,16,128]{3,2,1,0:T(8,128)(2,1)} %get-tuple-element.38), calls=%async_computation.1 | async-start | bytes 524288 | tf_op jit(solution)/shard_map/all_to_all | solution.py:768
  67.7 14.2 %copy-start.3 = (bf16[1600,128]{1,0:T(8,128)(2,1)S(1)}, bf16[1600,128]{1,0:T(8,128)(2,1)}, u32[]{:S(2)}) copy-start(bf16[1600,128]{1,0:T(8,128)(2,1)} %copy-done.2) | copy-start | bytes 1228804
  83.1 5.0 %copy-start.32 = (f32[32,11]{0,1:T(8,128)S(1)}, f32[32,11]{0,1:T(8,128)}, u32[]{:S(2)}) copy-start(f32[32,11]{0,1:T(8,128)} %param.49) | copy-start | bytes 4228
  83.1 5.1 %copy-start.33 = (f32[32,11]{0,1:T(8,128)S(1)}, f32[32,11]{0,1:T(8,128)}, u32[]{:S(2)}) copy-start(f32[32,11]{0,1:T(8,128)} %param.56) | copy-start | bytes 4228
  93.0 4.2 %copy-start.10 = (f32[4,16,3]{2,1,0:T(8,128)S(1)}, f32[4,16,3]{2,1,0:T(8,128)}, u32[]{:S(2)}) copy-start(f32[4,16,3]{2,1,0:T(8,128)} %copy.189) | copy-start | bytes 2308
  93.0 4.2 %copy-start.35 = (f32[4,16,1]{1,2,0:T(1,128)S(1)}, f32[4,16,1]{1,2,0:T(1,128)}, u32[]{:S(2)}) copy-start(f32[4,16,1]{1,2,0:T(1,128)} %get-tuple-element.207) | copy-start | bytes 772
  93.0 4.3 %copy-start.9 = (f32[4,16,4]{2,1,0:T(8,128)S(1)}, f32[4,16,4]{2,1,0:T(8,128)}, u32[]{:S(2)}) copy-start(f32[4,16,4]{2,1,0:T(8,128)} %copy.188) | copy-start | bytes 3076
  93.0 4.3 %copy-start.34 = (f32[4,16,1]{1,2,0:T(1,128)S(1)}, f32[4,16,1]{1,2,0:T(1,128)}, u32[]{:S(2)}) copy-start(f32[4,16,1]{1,2,0:T(1,128)} %get-tuple-element.208) | copy-start | bytes 772
  97.2 7.1 %copy-start.40 = (f32[64]{0:T(128)S(1)}, f32[64]{0:T(128)}, u32[]{:S(2)}) copy-start(f32[64]{0:T(128)} %tile.21) | copy-start | bytes 772
  97.2 7.1 %copy-start.41 = (f32[128]{0:T(128)S(1)}, f32[128]{0:T(128)}, u32[]{:S(2)}) copy-start(f32[128]{0:T(128)} %tile.9) | copy-start | bytes 1540
  97.2 13.1 %copy-start.39 = (f32[4,8]{1,0:T(4,128)S(1)}, f32[4,8]{1,0:T(4,128)}, u32[]{:S(2)}) copy-start(f32[4,8]{1,0:T(4,128)} %param.36) | copy-start | bytes 388
  97.2 13.1 %copy-start.18 = (f32[15,250]{1,0:T(8,128)S(1)}, f32[15,250]{1,0:T(8,128)}, u32[]{:S(2)}) copy-start(f32[15,250]{1,0:T(8,128)} %param.40) | copy-start | bytes 45004
  99.3 10.9 %all-to-all-start.2 = ((f32[8,8,250]{2,1,0:T(8,128)}), f32[8,8,250]{2,1,0:T(8,128)S(1)}, u32[]{:S(2)}, u32[]{:S(2)}) async-start(f32[8,8,250]{2,1,0:T(8,128)} %convolution_bitcast_fusion), calls=%async_computation.2 | async-start | bytes 131072 | tf_op jit(solution)/shard_map/all_to_all | solution.py:768
  169.2 13.1 %all-to-all-start.3 = ((bf16[8,8,16,128]{3,2,1,0:T(8,128)(2,1)}), bf16[8,8,16,128]{3,2,1,0:T(8,128)(2,1)S(1)}, u32[]{:S(2)}, u32[]{:S(2)}) async-start(bf16[8,8,16,128]{3,2,1,0:T(8,128)(2,1)} %reshape.143), calls=%async_computation.3 | async-start | bytes 524288 | tf_op jit(solution)/shard_map/all_to_all | solution.py:768
  172.6 61.6 %all-reduce.8.cloned.1.call-start = ((), (), s32[]{:S(2)}) async-start(), calls=%async_computation.4 | async-start | bytes 2097152 | tf_op jit(solution)/shard_map/psum | solution.py:870
  172.8 9.4 %collective-permute-start = (bf16[8,4,32,128]{3,2,1,0:T(8,128)(2,1)}, bf16[8,4,32,128]{3,2,1,0:T(8,128)(2,1)}, u32[]{:S(2)}, u32[]{:S(2)}) collective-permute-start(bf16[8,4,32,128]{3,2,1,0:T(8,128)(2,1)} %get-tuple-element.44), channel_id=1, source_target_pairs={{0,1},{1,0},{2,3},{3,2},{4,5},{5,4},{6,7},{7,6},{8,9},{9,8},{10,11... | collective-permute-start | bytes 786440 | tf_op jit(solution)/shard_map/ppermute | solution.py:855
  177.4 3.0 copy-start.7
  177.4 3.1 copy-start.14
  177.4 3.4 copy-start.42
  177.4 4.1 %copy-start.22 = (f32[10,25]{1,0:T(8,128)S(1)}, f32[10,25]{1,0:T(8,128)}, u32[]{:S(2)}) copy-start(f32[10,25]{1,0:T(8,128)} %get-tuple-element.205) | copy-start | bytes 3004
  177.4 4.3 %slice-start.1 = ((f32[200]{0:T(256)}), f32[128]{0:T(128)S(1)}, s32[]{:S(2)}) async-start(f32[200]{0:T(256)} %reduce_sum.151), calls=%async_computation.7 | async-start | bytes 1024 | tf_op jit(solution)/shard_map/slice | solution.py:882
  177.5 4.8 %copy-start.8 = (bf16[8,4,32,128]{3,2,1,0:T(8,128)(2,1)S(1)}, bf16[8,4,32,128]{3,2,1,0:T(8,128)(2,1)}, u32[]{:S(2)}) copy-start(bf16[8,4,32,128]{3,2,1,0:T(8,128)(2,1)} %get-tuple-element.44) | copy-start | bytes 786436
  180.4 187.9 %all-reduce.10.cloned.1.call-start = ((), (), s32[]{:S(2)}) async-start(), calls=%async_computation.5 | async-start | bytes 1638400 | tf_op jit(solution)/shard_map/psum | solution.py:888
  182.3 1.9 collective-permute-start.1
  185.0 25.2 %copy-start.11 = (f32[144,75]{1,0:T(8,128)S(1)}, f32[144,75]{1,0:T(8,128)}, u32[]{:S(2)}) copy-start(f32[144,75]{1,0:T(8,128)} %constant.66.clone) | copy-start | bytes 129604
  209.1 28.2 %copy-start.29 = (f32[32,128]{1,0:T(8,128)S(1)}, f32[32,128]{1,0:T(8,128)}, u32[]{:S(2)}) copy-start(f32[32,128]{1,0:T(8,128)} %get-tuple-element.47) | copy-start | bytes 49156
  209.1 164.4 %copy-start.16 = (f32[32,11]{1,0:T(8,128)S(1)}, f32[32,11]{1,0:T(8,128)}, u32[]{:S(2)}) copy-start(f32[32,11]{1,0:T(8,128)} %copy.206) | copy-start | bytes 4228
  209.1 164.4 %copy-start.17 = (f32[32,11]{1,0:T(8,128)S(1)}, f32[32,11]{1,0:T(8,128)}, u32[]{:S(2)}) copy-start(f32[32,11]{1,0:T(8,128)} %copy.204) | copy-start | bytes 4228
  234.2 141.4 %copy-start.1 = (bf16[2,250,1024]{1,2,0:T(8,128)(2,1)S(1)}, bf16[2,250,1024]{1,2,0:T(8,128)(2,1)}, u32[]{:S(2)}) copy-start(bf16[2,250,1024]{1,2,0:T(8,128)(2,1)} %all-reduce.8.cloned.1.call-done) | copy-start | bytes 3072004
  385.7 4.3 %copy-start = (f32[2,250,1024]{1,2,0:T(8,128)S(1)}, f32[2,250,1024]{1,2,0:T(8,128)}, u32[]{:S(2)}) copy-start(f32[2,250,1024]{1,2,0:T(8,128)} %get-tuple-element.192) | copy-start | bytes 6144004
  390.0 2.5 copy-start.31
  390.0 2.5 copy-start.36
  390.0 2.5 copy-start.37
  390.0 3.1 copy-start.15
  390.0 3.1 copy-start.23
  390.0 3.1 copy-start.24
  390.0 3.7 copy-start.19
  390.0 3.7 copy-start.25
  390.0 3.7 copy-start.26
  390.1 4.3 %copy-start.13 = (f32[75,32]{0,1:T(8,128)S(1)}, f32[75,32]{0,1:T(8,128)}, u32[]{:S(2)}) copy-start(f32[75,32]{0,1:T(8,128)} %param.37) | copy-start | bytes 28804
  390.1 4.3 %copy-start.27 = (f32[75,32]{0,1:T(8,128)S(1)}, f32[75,32]{0,1:T(8,128)}, u32[]{:S(2)}) copy-start(f32[75,32]{0,1:T(8,128)} %param.44) | copy-start | bytes 28804
  390.1 4.3 %copy-start.28 = (f32[75,32]{0,1:T(8,128)S(1)}, f32[75,32]{0,1:T(8,128)}, u32[]{:S(2)}) copy-start(f32[75,32]{0,1:T(8,128)} %param.51) | copy-start | bytes 28804
  390.1 4.9 %copy-start.5 = (f32[1600,128]{1,0:T(8,128)S(1)}, f32[1600,128]{1,0:T(8,128)}, u32[]{:S(2)}) copy-start(f32[1600,128]{1,0:T(8,128)} %param.38) | copy-start | bytes 2457604
Sparse Core Ops, SparseCore 0:
  180.5 53.6 all-reduce.7
  240.0 128.1 all-reduce.9

commit v2 on v1

--- a/solution.py
+++ b/solution.py
@@ -398,7 +398,7 @@
             off_y = tap // KS - 2 + sub // 2
             off_x = tap % KS - 2 + sub % 2
             block = (off_y // 2 + 1) * 3 + off_x // 2 + 1
-            base = block * 16 + (off_y % 2) * 8 + (off_x % 2) * 4
+            base = block * 16 + (off_x % 2) * 8 + (off_y % 2) * 4
             for channel in range(3):
                 places[sub, base + channel, tap] = 1.0
                 if sub == 0:
@@ -461,6 +461,34 @@
     return 0.5 * jnp.tanh(0.5 * v) + 0.5
 
 
+def one_hot_eye(size):
+    row = lax.broadcasted_iota(jnp.int32, (size, size), 0)
+    return (row == lax.broadcasted_iota(jnp.int32, (size, size), 1)).astype(BF)
+
+
+def one_hot_mod(shape, period, axis):
+    folded = lax.broadcasted_iota(jnp.int32, shape, axis) % period
+    return (folded == lax.broadcasted_iota(jnp.int32, shape, 1 - axis)).astype(BF)
+
+
+def unpack_images(raw_ref, x_ref):
+    source = lax.broadcasted_iota(jnp.int32, (LANES, 4 * LANES), 0)
+    goal = lax.broadcasted_iota(jnp.int32, (LANES, 4 * LANES), 1)
+    same = (source // 64 == goal // 256) & (source % 2 == goal // LANES % 2) & (source // 2 % WB == goal % WB)
+    picks = [(same & (goal // WB % BANDS == band)).astype(BF) for band in range(BANDS)]
+    for pair in range(2):
+        total = nn(raw_ref[pair], picks[0])
+        for band in range(1, BANDS):
+            total = total + nn(raw_ref[2 * band + pair], picks[band])
+        for t in range(x_ref.shape[0]):
+            rows = total[8 * t : 8 * t + 8]
+            for low_row in range(2):
+                start = 2 * LANES * low_row
+                x_ref[t, 2 * pair + low_row] = jnp.concatenate(
+                    [rows[:, start : start + LANES], rows[:, start + LANES : start + 2 * LANES]], axis=0
+                ).astype(BF)
+
+
 def image_tiles(x_ref, t):
     return [x_ref[t, tile].astype(F32) for tile in range(TILES)]
 
@@ -482,12 +510,18 @@
 
 
 def forward_kernel(
-    half_ref, x_ref, we_ref, wx_ref, wh_ref, bias_ref,
-    enc_ref, hid_ref, act_ref, cell_ref, strip_ref,
-    win_s, enc_s, hid_s, state_s,
+    half_ref, raw_ref, we_ref, w_ref, bias_ref,
+    x_ref, enc_ref, hid_ref, act_ref, cell_ref, strip_ref,
+    win_s, enc_s, hid_s, state_s, rows_s, wx_s, wh_s,
 ):
     steps = enc_ref.shape[0]
     lanes = lane_places()
+    for kind, target in ((0, wx_s), (1, wh_s)):
+        for tap in range(KK):
+            start = tap * 2 * C + kind * C
+            rows_s[tap * C : (tap + 1) * C, :] = w_ref[start : start + C, :].astype(BF)
+        target[...] = nt(one_hot_eye(4 * C), rows_s[...]).astype(BF)
+    unpack_images(raw_ref, x_ref)
 
     def encode(t, _):
         spread(image_tiles(x_ref, t), lanes, 1, win_s, 16, 0)
@@ -504,7 +538,7 @@
                 tiles.append(part.astype(F32))
         spread(tiles, lanes, 2, enc_s, C, 0)
         for two in range(0, TILES, 2):
-            gates = nn(wx_ref[...], stacked(enc_s, two, KS)) + twice(bias_ref[3 * C : 7 * C])
+            gates = nn(wx_s[...], stacked(enc_s, two, KS)) + twice(bias_ref[3 * C : 7 * C])
             for one in range(2):
                 act_ref[t, two + one] = gates[:, one * LANES : (one + 1) * LANES]
         return 0
@@ -516,7 +550,7 @@
     def advance(t, _):
         hidden = []
         for two in range(0, TILES, 2):
-            sums = nn(wh_ref[...], stacked(hid_s, two, KS))
+            sums = nn(wh_s[...], stacked(hid_s, two, KS))
             for one in range(2):
                 tile = two + one
                 gates = act_ref[t, tile] + sums[:, one * LANES : (one + 1) * LANES]
@@ -557,10 +591,27 @@
 
 
 def head_kernel(
-    half_ref, x_ref, hid_ref, logit_ref, wd_ref, wdt_ref, wm_ref, wmt_ref, bias_ref, place_ref, placet_ref,
+    half_ref, x_ref, hid_ref, logit_ref, w_ref, mask_ref, bias_ref, place_ref, placet_ref,
     back_ref, dlog_ref, dwd_ref, dwm_ref, sums_ref,
-    win_s, dk_s,
+    win_s, dk_s, wd_ref, wdt_ref, wm_ref, wmt_ref, over_ref,
 ):
+    wd_ref[...] = w_ref[...].astype(BF)
+    wdt_ref[...] = nt(one_hot_eye(4 * C), wd_ref[...]).astype(BF)
+    copies = one_hot_mod((4 * C, C), C, 0)
+    fourfold = nn(copies, mask_ref[...].astype(BF)).astype(BF)
+    row = lax.broadcasted_iota(jnp.int32, (4 * C, 64), 0)
+    wmt_ref[...] = jnp.where(
+        row // C == lax.broadcasted_iota(jnp.int32, (4 * C, 64), 1) // 16,
+        nn(fourfold, one_hot_mod((NM, 64), 16, 1)), 0.0,
+    ).astype(BF)
+    row = lax.broadcasted_iota(jnp.int32, (64, 4 * C), 0)
+    wm_ref[...] = jnp.where(
+        row // 16 == lax.broadcasted_iota(jnp.int32, (64, 4 * C), 1) // C,
+        nt(one_hot_mod((64, NM), 16, 0), fourfold), 0.0,
+    ).astype(BF)
+    for sub in range(4):
+        over_ref[sub * C : (sub + 1) * C, :] = bias_ref[7 * C : 8 * C]
+        over_ref[4 * C + sub * 16 : 4 * C + (sub + 1) * 16, :] = bias_ref[8 * C : 8 * C + 16]
     own = logit_ref.shape[0]
     base = half_ref[0] * own
     lanes = lane_places()
@@ -584,10 +635,10 @@
         for two in range(0, TILES, 2):
             hidden = jnp.concatenate([hid_ref[t, two], hid_ref[t, two + 1]], axis=1)
             window = stacked(win_s, two, 3)
-            upper = nn(wdt_ref[...], hidden) + twice(bias_ref[0 : 4 * C])
+            upper = nn(wdt_ref[...], hidden) + twice(over_ref[0 : 4 * C])
             gate = logistic(upper)
             active = (upper * gate).astype(BF)
-            scores = nn(wm_ref[...], active) + twice(bias_ref[4 * C : 4 * C + 64])
+            scores = nn(wm_ref[...], active) + twice(over_ref[4 * C : 4 * C + 64])
             scores = scores.reshape(4, 16, 2 * LANES)
             powers = jnp.exp(scores - jnp.max(scores, 1, keepdims=True))
             masks = powers / jnp.sum(powers, 1, keepdims=True)
@@ -599,9 +650,9 @@
                 mixing = nn(spots, mask_low)
                 both = jnp.sum((mixing * window).reshape(18, 8, 2 * LANES), 0)
                 result = both + pltpu.roll(both, 4, 0)
-                goal = after[(sub // 2) * 8 : (sub // 2) * 8 + 8]
+                goal = after[(sub % 2) * 8 : (sub % 2) * 8 + 8]
                 turned = pltpu.roll(goal, 4, 0)
-                goal = jnp.where((row8 < 4) == (sub % 2 == 0), goal, turned)
+                goal = jnp.where((row8 < 4) == (sub // 2 == 0), goal, turned)
                 counted = goal[3:4]
                 diff = jnp.where(color, result - goal, 0.0)
                 weighted = diff * counted
@@ -639,10 +690,14 @@
 
 
 def backward_kernel(
-    half_ref, x_ref, enc_ref, hid_ref, act_ref, cell_ref, dec_ref, fc_ref, wb_ref, we_ref, bias_ref,
+    half_ref, x_ref, enc_ref, hid_ref, act_ref, cell_ref, dec_ref, fc_ref, w_ref, we_ref, bias_ref,
     dw_ref, dwe_ref, sums_ref,
-    gate_s, keep_s, denc_s, back_s, state_s, win_s, join_s,
+    gate_s, keep_s, denc_s, back_s, state_s, win_s, join_s, wb_ref,
 ):
+    for tap in range(KK):
+        place = tap % KS * 2 * C
+        turn = (KS - 1 - tap // KS) * 4 * C
+        wb_ref[place : place + 2 * C, turn : turn + 4 * C] = w_ref[tap * 2 * C : (tap + 1) * 2 * C, :].astype(BF)
     steps = enc_ref.shape[0]
     own = steps // HALVES
     base = half_ref[0] * own
@@ -764,8 +819,36 @@
     return jnp.broadcast_to(values[:, None], (values.shape[0], LANES))
 
 
-def pieces_to_clips(block):
-    return lax.all_to_all(block, "row", 0, 0, tiled=True)
+def exchange(block, axes):
+    return lax.all_to_all(block, axes, 0, 0, tiled=True)
+
+
+def to_all(block, axes):
+    count = lax.axis_size(axes)
+    return exchange(jnp.broadcast_to(block[None], (count,) + block.shape), axes)
+
+
+def strip_order():
+    sent = np.arange(WB * C)
+    natural = sent % WB * C + sent // WB % 4 * 8 + sent // LANES
+    order = np.zeros((WB * C, WB * C), np.float32)
+    order[sent, natural] = 1.0
+    return order
+
+
+def in_three(values):
+    terms = []
+    for _ in range(3):
+        low = lax.optimization_barrier(values.astype(BF))
+        terms.append(low)
+        values = values - low.astype(F32)
+    return jnp.concatenate(terms)
+
+
+def in_rows(values):
+    flat = values.reshape(-1)
+    rows = -(-flat.shape[0] // LANES)
+    return jnp.pad(flat, (0, rows * LANES - flat.shape[0])).reshape(rows, LANES)
 
 
 def whole_clips(
@@ -783,37 +866,39 @@
     half = place % HALVES
     half_1 = half.reshape(1).astype(jnp.int32)
     b_enc, g_enc, s_enc, b_lstm, b_fc, b_dec, b_mask = split_vector(vector)
-    k_enc = w_enc.astype(BF)
-    k_lstm = w_lstm.astype(BF)
-    k_dec = w_deconv.astype(BF)
-    k_mask = w_mask.astype(BF)
     places, encoder = window_places()
     flagged = jnp.pad(valid.astype(BF), ((0, 0), (1, 0), (0, 0), (0, 0)))
-    pieces = jnp.concatenate([frames, flagged[:, :, None]], axis=2)
-    pieces = jnp.repeat(pieces, HALVES, axis=0)
-    pieces = pieces_to_clips(pieces)
-    grid = pieces.reshape(BANDS, 2, shots, 4, 2, 2, width // 2, 2)
-    grid = jnp.transpose(grid, (2, 1, 4, 5, 7, 3, 0, 6))
-    x = grid.reshape(shots, TILES, 16, LANES)
-
-    wide_enc = jnp.einsum("rk,ko->or", jnp.asarray(encoder, BF), k_enc, preferred_element_type=F32).astype(BF)
-    taps = k_lstm.reshape(KS, KS, 2, C, 4 * C)
-    wx = taps[:, :, 0].reshape(KK * C, 4 * C).T
-    wh = taps[:, :, 1].reshape(KK * C, 4 * C).T
-    bias = columns(jnp.concatenate([b_enc, g_enc, s_enc, b_lstm]))
+    pieces = jnp.concatenate([frames, flagged[:, :, None]], axis=2).reshape(clips, shots, 4, 2, 2, width)
+    pieces = jnp.transpose(pieces, (0, 1, 4, 2, 3, 5)).reshape(clips, shots * 8, LANES)
+    pieces = jnp.pad(pieces, ((0, 0), (0, 8), (0, 0)))
+    raw = exchange(jnp.repeat(pieces, HALVES, axis=0), "row")
+
+    wide_enc = jnp.einsum(
+        "rk,ko->or", jnp.asarray(encoder, BF), w_enc.astype(BF), preferred_element_type=F32
+    ).astype(BF)
+    bias = columns(
+        jnp.concatenate([vector[: 7 * C], b_dec, jnp.pad(b_mask, (0, 16 - NM), constant_values=-1e30)])
+    )
     cells = (steps, TILES, C, LANES)
-    enc, hid, act, cell, strips_out = call(
+    x, enc, hid, act, cell, strips_out = call(
         forward_kernel,
-        [(cells, BF), (cells, BF), ((steps, TILES, 4 * C, LANES), F32), (cells, F32), ((count, own, 16, LANES), BF)],
-        [((6, 48, LANES), BF), ((8, KS * C, LANES), BF), ((8, KS * C, LANES), BF), ((TILES, C, LANES), F32)],
-        half_1, x, wide_enc, wx, wh, bias,
+        [
+            ((shots, TILES, 16, LANES), BF), (cells, BF), (cells, BF), ((steps, TILES, 4 * C, LANES), F32),
+            (cells, F32), ((count, own, 16, LANES), BF),
+        ],
+        [
+            ((6, 48, LANES), BF), ((8, KS * C, LANES), BF), ((8, KS * C, LANES), BF), ((TILES, C, LANES), F32),
+            ((KK * C, LANES), BF), ((4 * C, KK * C), BF), ((4 * C, KK * C), BF),
+        ],
+        half_1, raw, wide_enc, w_lstm, bias,
     )
     items = clips * steps
-    strip_hid = pieces_to_clips(strips_out).reshape(items, 2, WB * C)
-    k_fc = w_fc.astype(BF).reshape(2, NK * KK, WB, 4, 8)
-    k_fc = jnp.transpose(k_fc, (0, 1, 4, 3, 2)).reshape(2, NK * KK, WB * C)
+    order = jnp.asarray(strip_order(), BF)
+    k_fc = w_fc.astype(BF)
+    strip_hid = exchange(strips_out, "row").reshape(items * 2, WB * C)
+    strip_hid = jnp.dot(strip_hid, order, preferred_element_type=F32).astype(BF).reshape(items, 2, WB * C)
     parts = jnp.einsum("mjk,jnk->mn", strip_hid, k_fc, preferred_element_type=F32)
-    summed = jnp.sum(pieces_to_clips(parts.reshape(count, own, NK * KK)), 0)
+    summed = jnp.sum(exchange(parts.reshape(count, own, NK * KK), "row"), 0)
     presence = flags.astype(F32)
     conditions = jnp.concatenate(
         [
@@ -828,70 +913,86 @@
     logits = jnp.pad(
         logits.reshape(own, NK, KK), ((0, 0), (1, 5), (0, 32 - KK)), constant_values=-1e30
     )
-    wdt = k_dec.T
-    eye = jnp.eye(4, dtype=BF)
-    pad_mask = jnp.pad(k_mask, ((0, 0), (0, 16 - NM)))
-    wmt = jnp.einsum("ab,cm->acbm", eye, pad_mask).reshape(4 * C, 64)
-    head_bias = columns(
-        jnp.concatenate([jnp.tile(b_dec, 4), jnp.tile(jnp.pad(b_mask, (0, 16 - NM), constant_values=-1e30), 4)])
-    )
     dec, d_logit, d_dec, d_mask_wide, head_sums = call(
         head_kernel,
         [
             ((own, TILES, C, LANES), BF), ((own, 16, 32), F32), ((C, 4 * C), F32), ((4 * C, 64), F32),
             ((200, LANES), F32),
         ],
-        [((6, 48, LANES), F32), ((16, 32), F32)],
-        half_1, x, hid, logits, k_dec, wdt, wmt.T, wmt, head_bias,
+        [
+            ((6, 48, LANES), F32), ((16, 32), F32), ((C, 4 * C), BF), ((4 * C, C), BF), ((64, 4 * C), BF),
+            ((4 * C, 64), BF), ((4 * C + 64, LANES), F32),
+        ],
+        half_1, x, hid, logits, w_deconv, w_mask, bias,
         jnp.asarray(places, BF), jnp.asarray(places.transpose(0, 2, 1), BF),
     )
     d_logit = d_logit[:, 1 : NK + 1, :KK].reshape(own, NK * KK)
-    d_sum = lax.all_gather(d_logit.astype(BF), "row").reshape(items, NK * KK)
+    d_sum = to_all(d_logit.astype(BF), "row").reshape(items, NK * KK)
     back_fc = jnp.einsum("mn,jnk->mjk", d_sum, k_fc, preferred_element_type=F32).astype(BF)
-    back_fc = pieces_to_clips(back_fc.reshape(count, own, 16, LANES))
+    back_fc = lax.dot_general(
+        back_fc.reshape(items * 2, WB * C), order, (((1,), (1,)), ((), ())), preferred_element_type=F32
+    ).astype(BF)
+    back_fc = exchange(back_fc.reshape(count, own, 16, LANES), "row")
     swap = [(index, index ^ 1) for index in range(count)]
 
     def in_order(block):
         other = lax.ppermute(block, "row", swap)
         return jnp.stack([jnp.where(half == 0, block, other), jnp.where(half == 0, other, block)])
 
-    wb = jnp.transpose(k_lstm.reshape(KS, KS, 2 * C, 4 * C)[::-1], (1, 2, 0, 3)).reshape(KS * 2 * C, KS * 4 * C)
     d_lstm, d_enc_wide, sums = call(
         backward_kernel,
         [((KK * 2 * C, 4 * C), F32), ((C, WIN), F32), ((7 * C, LANES), F32)],
         [
             ((8, 4 * C, LANES), BF), ((steps, TILES, 4 * C, LANES), BF), (cells, F32), ((TILES, C, LANES), F32),
             ((TILES, C, LANES), F32), ((6, 48, LANES), BF), ((8, KS * 2 * C, LANES), BF),
+            ((KS * 2 * C, KS * 4 * C), BF),
         ],
-        half_1, x, enc, hid, act, cell, in_order(dec), in_order(back_fc), wb, wide_enc, bias,
-    )
-    d_fc = jnp.einsum("mjk,mn->jnk", strip_hid, d_sum, preferred_element_type=F32).astype(BF)
-    d_fc = jnp.transpose(d_fc.reshape(2, NK * KK, 8, 4, WB), (0, 1, 4, 3, 2)).reshape(2, NK * KK, WB * C)
-    d_fc = lax.psum(d_fc, "clip").astype(F32)
-    fc_squares = jnp.sum(d_fc * d_fc) / lax.axis_size("clip")
+        half_1, x, enc, hid, act, cell, in_order(dec), in_order(back_fc), w_lstm, wide_enc, bias,
+    )
+    groups = lax.axis_size("clip")
+    part = WB * C // groups
+    d_fc = jnp.einsum(
+        "mjqk,mn->qjnk", strip_hid.reshape(items, 2, groups, part), d_sum, preferred_element_type=F32
+    ).astype(BF)
+    d_fc = jnp.sum(exchange(d_fc, "clip").astype(F32), 0)
+    fc_squares = jnp.sum(d_fc * d_fc)
+    d_fc = jnp.transpose(to_all(d_fc.astype(BF), "clip"), (1, 2, 0, 3)).reshape(w_fc.shape).astype(F32)
 
     d_enc = jnp.einsum("rk,or->ko", jnp.asarray(encoder, F32), d_enc_wide, precision=HIGH)
     d_cond = jnp.dot(cond.T, d_logit, precision=HIGH)
-    d_mask = jnp.sum(jnp.stack([d_mask_wide[s * C : (s + 1) * C, s * 16 : s * 16 + NM] for s in range(4)]), 0)
-    line_sums = jnp.sum(sums, 1)
+    d_mask = sum(d_mask_wide[sub * C : (sub + 1) * C, sub * 16 : sub * 16 + NM] for sub in range(4))
     head_lines = jnp.sum(head_sums, 1)
     d_vector = jnp.concatenate(
         [
-            line_sums,
+            jnp.sum(sums, 1),
             jnp.sum(d_logit, 0),
             jnp.sum(head_lines[:128].reshape(4, C), 0),
             jnp.sum(head_lines[128:192].reshape(4, 16), 0)[:NM],
         ]
     )
-    loss_part = jnp.sum(head_lines[192:196])
-    count_part = jnp.sum(valid.astype(F32))
-    d_enc, d_lstm, d_cond, d_dec, d_mask, d_vector, loss_sum, squares, valid_count = lax.psum(
-        (d_enc, d_lstm, d_cond, d_dec, d_mask, d_vector, loss_part, fc_squares, count_part), ("clip", "row")
-    )
+    scalars = jnp.stack([jnp.sum(head_lines[192:196]), jnp.sum(valid.astype(F32)), fc_squares])
+    both = ("clip", "row")
+    devices = lax.axis_size(both)
+    small = [d_enc, d_cond, d_dec, d_mask, d_vector]
+    block = jnp.concatenate([in_rows(value.astype(BF)) for value in [d_lstm] + small])
+    each = -(-block.shape[0] // devices)
+    block = jnp.pad(block, ((0, devices * each - block.shape[0]), (0, 0))).reshape(devices, each, LANES)
+    extra = jnp.pad(in_three(scalars), (0, LANES - 9))
+    extra = jnp.broadcast_to(extra, (devices, 1, LANES))
+    fill = jnp.zeros((devices, -(each + 1) % 16, LANES), BF)
+    got = jnp.sum(exchange(jnp.concatenate([block, extra, fill], axis=1), both).astype(F32), 0)
+    loss_sum, valid_count, squares = got[each, 0:3] + got[each, 3:6] + got[each, 6:9]
+    got = to_all(got.astype(BF), both)[:, :each].reshape(devices * each, LANES).astype(F32)
+    summed = []
+    start = 0
+    for value in [d_lstm] + small:
+        rows = -(-value.size // LANES)
+        summed.append(got[start : start + rows].reshape(-1)[: value.size].reshape(value.shape))
+        start += rows
+    d_lstm, d_enc, d_cond, d_dec, d_mask, d_vector = summed
     inv_count = 1.0 / valid_count
     grads = (d_enc, d_lstm, d_fc, d_cond, d_dec, d_mask, d_vector)
-    for index in (0, 1, 3, 4, 5, 6):
-        squares = squares + jnp.sum(grads[index] * grads[index])
+    squares = squares + jnp.sum(got * got)
     grad_norm = jnp.sqrt(squares) * inv_count
     factor = inv_count * (CLIP_NORM / jnp.maximum(grad_norm, CLIP_NORM))
     rates = learning_rates(w_fc.shape[0] * count)

time: 408 us -> 281 us (0.69)
  waiting for transfers between devices: 119 us -> 59.3 us
  blocking collectives: 54.8 us -> 0 us
  local copies, waits for them, and re-layouts: 67.9 us -> 48.4 us
  between operations: 21.8 us -> 4.56 us
  starting transfers between devices: 19.4 us -> 35.5 us
    psum x2 -> x0, waiting for transfers between devices: 108 us -> none  [the longest x1 85.1 us: whole_clips(): lax.psum((d_enc, d_lstm, d_cond, d_dec, d_mask, d_vector, loss_part, fc_s...]
    all_to_all x4 -> x9, waiting for transfers between devices: 10.7 us -> 58.7 us  [exchange(): return lax.all_to_all(block, axes, 0, 0, tiled=True)]
    psum x1 -> x0, blocking collectives: 40.8 us -> none  [whole_clips(): lax.psum((d_enc, d_lstm, d_cond, d_dec, d_mask, d_vector, loss_part, fc_s...]
    all_to_all x4 -> x9, starting transfers between devices: 18.8 us -> 35.1 us  [exchange(): return lax.all_to_all(block, axes, 0, 0, tiled=True)]
    all_gather x1 -> x0, blocking collectives: 14 us -> none  [whole_clips(): d_sum = lax.all_gather(d_logit.astype(BF), 'row').reshape(items, NK * KK)]
    unnamed x103 -> x80, local copies, waits for them, and re-layouts: 31.6 us -> 24.4 us
    convert_element_type x4 -> x10, other arithmetic: 1.47 us -> 8.36 us  [the longest x1 2.28 us: whole_clips(): k_fc = w_fc.astype(BF)]
    transpose x3 -> x0, local copies, waits for them, and re-layouts: 6.3 us -> none  [the longest x1 2.87 us: whole_clips(): jnp.transpose(d_fc.reshape(2, NK * KK, 8, 4, WB), (0, 1, 4, 3, 2))]
  transfers between devices with their start and end apart: 8 -> 11, of which waited for: 5 -> 9; matrix products, arithmetic and copies ran while one was open for 15% -> 13% of each run, Pallas kernels for 6% -> 9%
where the time goes in v2:
time: 281 us; the launch traced here: 279 us
  Pallas kernels  86.2 us (31%)
  waiting for transfers between devices  59.3 us (21%)
  local copies, waits for them, and re-layouts  48.4 us (17%)
  other arithmetic  36.3 us (13%)
  starting transfers between devices  35.5 us (13%)
  matrix products  8.08 us (3%)
  between operations  4.56 us (2%)
    pallas_call x3, Pallas kernels, call(): pl.pallas_call(kernel, out_shape=[jax.ShapeDtypeStruct(shape, kind) for s...  86.2 us
    all_to_all x9, waiting for transfers between devices, exchange(): return lax.all_to_all(block, axes, 0, 0, tiled=True)  58.7 us
    all_to_all x9, starting transfers between devices, exchange(): return lax.all_to_all(block, axes, 0, 0, tiled=True)  35.1 us
    unnamed x80, local copies, waits for them, and re-layouts  24.4 us
    sub x7, other arithmetic, adam(): return (weight - rate * (update + DECAY * weight), first, second)  12.8 us
  transfers between devices with their start and end apart: 11, of which 9 were waited for; matrix products, arithmetic and copies ran while one was open for 13% of the time, Pallas kernels for 9%

profile of v2, /device:TPU:0, one launch (start us, length us, event | category | flops | bytes accessed | tf_op | source)
XLA Modules:
  0.0 278.5 jit_solution(7562395371919283728)
XLA Ops:
  0.7 1.1 copy.154
  1.8 0.9 convert_element_type.124
  3.5 0.8 broadcast_in_dim.16
  4.2 6.3 %all-to-all-start = ((bf16[8,144,128]{2,1,0:T(8,128)(2,1)}), bf16[8,144,128]{2,1,0:T(8,128)(2,1)S(1)}, u32[]{:S(2)}, u32[]{:S(2)}) async-start(bf16[8,144,128]{2,1,0:T(8,128)(2,1)} %bitcast.4), calls=%async_computation | async-start | bytes 589824 | tf_op jit(solution)/shard_map/all_to_all | solution.py:823
  10.8 0.8 fusion.3.we_ref
  11.6 9.4 %all-to-all-done.raw_ref = bf16[8,144,128]{2,1,0:T(8,128)(2,1)S(1)} async-done(((bf16[8,144,128]{2,1,0:T(8,128)(2,1)}), bf16[8,144,128]{2,1,0:T(8,128)(2,1)S(1)}, u32[]{:S(2)}, u32[]{:S(2)}) %all-to-all-start) | async-done | bytes 294944 | tf_op jit(solution)/shard_map/all_to_all | solution.py:823
  21.0 0.8 broadcast_in_dim.17.bias_ref
  21.8 24.0 %shard_map.487 = (bf16[17,4,16,128]{3,2,1,0:T(8,128)(2,1)}, bf16[16,4,32,128]{3,2,1,0:T(8,128)(2,1)}, bf16[16,4,32,128]{3,2,1,0:T(8,128)(2,1)}, f32[16,4,128,128...) custom-call(s32[1]{0:T(128)} %bitcast.half_ref, bf16[8,144,128]{2,1,0:T(8,128)(2,1)} %copy-done.5, ...), custom_call_target="tpu_custom_call" | custom-call | tf_op jit(solution)/shard_map/pallas_call | solution.py:808
  45.8 3.6 %all-to-all-start.1 = ((bf16[8,8,16,128]{3,2,1,0:T(8,128)(2,1)}), bf16[8,8,16,128]{3,2,1,0:T(8,128)(2,1)S(1)}, u32[]{:S(2)}, u32[]{:S(2)}) async-start(bf16[8,8,16,128]{3,2,1,0:T(8,128)(2,1)} %get-tuple-element.43), calls=%async_computation.1 | async-start | bytes 524288 | tf_op jit(solution)/shard_map/all_to_all | solution.py:823
  50.0 2.3 convert_element_type.128
  54.6 4.5 %all-to-all-done.1 = bf16[8,8,16,128]{3,2,1,0:T(8,128)(2,1)S(1)} async-done(((bf16[8,8,16,128]{3,2,1,0:T(8,128)(2,1)}), bf16[8,8,16,128]{3,2,1,0:T(8,128)(2,1)S(1)}, u32[]{:S(2)}, u32[]{:S(2)}) %all-to-all-start.1) | async-done | bytes 262176 | tf_op jit(solution)/shard_map/all_to_all | solution.py:823
  59.1 0.8 reshape.170
  59.9 1.4 convolution_convert_fusion.2
  61.3 0.8 dot_general.31
  62.1 2.0 convolution_bitcast_fusion
  64.1 4.0 %all-to-all-start.2 = ((f32[8,8,250]{2,1,0:T(8,128)}), f32[8,8,250]{2,1,0:T(8,128)}, u32[]{:S(2)}, u32[]{:S(2)}) async-start(f32[8,8,250]{2,1,0:T(8,128)} %convolution_bitcast_fusion), calls=%async_computation.2 | async-start | bytes 131072 | tf_op jit(solution)/shard_map/all_to_all | solution.py:823
  68.8 0.9 reshape_reshape.3
  69.7 4.4 %all-to-all-done.2 = f32[8,8,250]{2,1,0:T(8,128)} async-done(((f32[8,8,250]{2,1,0:T(8,128)}), f32[8,8,250]{2,1,0:T(8,128)}, u32[]{:S(2)}, u32[]{:S(2)}) %all-to-all-start.2) | async-done | bytes 64032 | tf_op jit(solution)/shard_map/all_to_all | solution.py:823
  74.1 0.9 reduce_sum.110
  75.6 0.9 fusion.5
  77.2 38.2 %shard_map.488 = (bf16[8,4,32,128]{3,2,1,0:T(8,128)(2,1)}, f32[8,16,32]{2,1,0:T(8,128)}, f32[32,128]{1,0:T(8,128)}, f32[128,64]{1,0:T(8,128)}, f32[200,128]{1,0:T(8,128)}) custom-call(s32[1]{0:T(128)} %bitcast.half_ref, bf16[17,4,16,128]{3,2,1,0:T(8,128)(2,1)} %get-tuple-element.38.x_ref, bf16[16,4,32,128]{3,2,1,0:T(8,128)(2,1)} %get-tuple-element.40.hid_ref, ...), custom_call_target="tpu_custom_call" | custom-call | tf_op jit(solution)/shard_map/pallas_call | solution.py:808
  115.5 1.5 slice_reduce_fusion.1
  117.9 3.3 %all-to-all-start.3 = ((bf16[8,8,250]{2,1,0:T(8,128)(2,1)}), bf16[8,8,250]{2,1,0:T(8,128)(2,1)S(1)}, u32[]{:S(2)}, u32[]{:S(2)}) async-start(bf16[8,8,250]{2,1,0:T(8,128)(2,1)} %broadcast_in_dim.19), calls=%async_computation.3 | async-start | bytes 65536 | tf_op jit(solution)/shard_map/all_to_all | solution.py:823
  121.8 0.8 add_convert_fusion
  122.6 1.0 reduce_sum.114
  123.7 3.2 %all-to-all-done.3 = bf16[8,8,250]{2,1,0:T(8,128)(2,1)S(1)} async-done(((bf16[8,8,250]{2,1,0:T(8,128)(2,1)}), bf16[8,8,250]{2,1,0:T(8,128)(2,1)S(1)}, u32[]{:S(2)}, u32[]{:S(2)}) %all-to-all-start.3) | async-done | bytes 32032 | tf_op jit(solution)/shard_map/all_to_all | solution.py:823
  127.8 0.8 convolution_convert_fusion.1
  128.6 0.8 reshape.175
  129.5 3.4 %all-to-all-start.4 = ((bf16[8,8,16,128]{3,2,1,0:T(8,128)(2,1)}), bf16[8,8,16,128]{3,2,1,0:T(8,128)(2,1)S(1)}, u32[]{:S(2)}, u32[]{:S(2)}) async-start(bf16[8,8,16,128]{3,2,1,0:T(8,128)(2,1)} %reshape.175), calls=%async_computation.4 | async-start | bytes 524288 | tf_op jit(solution)/shard_map/all_to_all | solution.py:823
  134.4 2.0 copy.165
  136.4 6.2 %all-to-all-done.4 = bf16[8,8,16,128]{3,2,1,0:T(8,128)(2,1)S(1)} async-done(((bf16[8,8,16,128]{3,2,1,0:T(8,128)(2,1)}), bf16[8,8,16,128]{3,2,1,0:T(8,128)(2,1)S(1)}, u32[]{:S(2)}, u32[]{:S(2)}) %all-to-all-start.4) | async-done | bytes 262176 | tf_op jit(solution)/shard_map/all_to_all | solution.py:823
  142.5 3.7 %all-to-all-start.5 = ((bf16[4,2,250,256]{3,1,2,0:T(2,128)(2,1)}), bf16[4,2,250,256]{3,1,2,0:T(2,128)(2,1)S(1)}, u32[]{:S(2)}, u32[]{:S(2)}) async-start(bf16[4,2,250,256]{3,1,2,0:T(2,128)(2,1)} %copy.165), calls=%async_computation.5 | async-start | bytes 2048000 | tf_op jit(solution)/shard_map/all_to_all | solution.py:823
  146.4 0.8 pad_maximum_fusion.dec_ref
  147.9 0.8 pad_maximum_fusion.1.fc_ref
  148.7 24.0 %shard_map.489 = (f32[1600,128]{1,0:T(8,128)}, f32[32,144]{1,0:T(8,128)}, f32[224,128]{1,0:T(8,128)}) custom-call(s32[1]{0:T(128)} %bitcast.half_ref, bf16[17,4,16,128]{3,2,1,0:T(8,128)(2,1)} %get-tuple-element.38.x_ref, bf16[16,4,32,128]{3,2,1,0:T(8,128)(2,1)} %get-tuple-element.39.enc_ref, bf16[16,4,32,128]{3,2,1,0:T(8,128)(2,1)} %get-tuple-element.40.hid_ref, ...), custom_call_target="tpu_custom_call" | custom-call | tf_op jit(solution)/shard_map/pallas_call | solution.py:808
  172.7 1.0 reduce_sum.111
  173.7 1.2 convert_element_type.133
  174.9 0.9 fusion.4
  176.9 1.3 convert_reduce_fusion
  178.3 0.7 multiply_reduce_fusion.1
  179.0 2.0 fusion.42
  181.2 1.0 maximum_maximum_fusion
  182.2 3.9 %all-to-all-start.6 = ((bf16[32,64,128]{2,1,0:T(8,128)(2,1)}), bf16[32,64,128]{2,1,0:T(8,128)(2,1)S(1)}, u32[]{:S(2)}, u32[]{:S(2)}) async-start(bf16[32,64,128]{2,1,0:T(8,128)(2,1)} %maximum_maximum_fusion), calls=%async_computation.6 | async-start | bytes 1048576 | tf_op jit(solution)/shard_map/all_to_all | solution.py:823
  186.5 15.9 %all-to-all-done.6 = bf16[32,64,128]{2,1,0:T(8,128)(2,1)S(1)} async-done(((bf16[32,64,128]{2,1,0:T(8,128)(2,1)}), bf16[32,64,128]{2,1,0:T(8,128)(2,1)S(1)}, u32[]{:S(2)}, u32[]{:S(2)}) %all-to-all-start.6) | async-done | bytes 524320 | tf_op jit(solution)/shard_map/all_to_all | solution.py:823
  202.4 1.5 broadcast_in_dim.23
  203.9 3.5 %all-to-all-start.8 = ((bf16[4,2,250,256]{3,1,2,0:T(2,128)(2,1)}), bf16[4,2,250,256]{3,1,2,0:T(2,128)(2,1)S(1)}, u32[]{:S(2)}, u32[]{:S(2)}) async-start(bf16[4,2,250,256]{3,1,2,0:T(2,128)(2,1)} %broadcast_in_dim.23), calls=%async_computation.8 | async-start | bytes 2048000 | tf_op jit(solution)/shard_map/all_to_all | solution.py:823
  207.6 13.7 %all-to-all-done.8 = bf16[4,2,250,256]{3,1,2,0:T(2,128)(2,1)S(1)} async-done(((bf16[4,2,250,256]{3,1,2,0:T(2,128)(2,1)}), bf16[4,2,250,256]{3,1,2,0:T(2,128)(2,1)S(1)}, u32[]{:S(2)}, u32[]{:S(2)}) %all-to-all-start.8) | async-done | bytes 1024032 | tf_op jit(solution)/shard_map/all_to_all | solution.py:823
  221.3 1.0 broadcast_in_dim.22
  222.4 3.3 %all-to-all-start.7 = ((bf16[32,64,128]{2,1,0:T(8,128)(2,1)}), bf16[32,64,128]{2,1,0:T(8,128)(2,1)}, u32[]{:S(2)}, u32[]{:S(2)}) async-start(bf16[32,64,128]{2,1,0:T(8,128)(2,1)} %broadcast_in_dim.22), calls=%async_computation.7 | async-start | bytes 1048576 | tf_op jit(solution)/shard_map/all_to_all | solution.py:823
  225.7 2.8 copy.174
  228.5 4.1 %copy.169 = f32[2,250,1024]{1,2,0:T(8,128)} copy(f32[2,250,1024]{2,0,1:T(2,128)} %param.47) | data formatting | bytes 4096000 | tf_op args[15]
  232.6 4.1 %copy.172 = f32[2,250,1024]{1,2,0:T(8,128)} copy(f32[2,250,1024]{2,0,1:T(2,128)} %param.54) | data formatting | bytes 4096000 | tf_op args[22]
  236.7 2.5 copy.171
  240.6 1.5 all-to-all-done.7
  242.1 2.0 slice_convert_fusion
  244.1 2.1 reshape.189
  248.3 1.9 multiply_reduce_fusion
  252.1 1.4 copy-done.1
  253.5 5.4 %multiply_subtract_fusion = (f32[2,250,1024]{1,2,0:T(8,128)}, f32[2,250,1024]{1,2,0:T(8,128)}, f32[2,250,1024]{1,2,0:T(8,128)}) fusion(f32[2,250,1024]{1,2,0:T(8,128)S(1)} %copy.174, f32[4,2,250,256]{2,3,0,1:T(8,128)S(1)} %convert_multiply_fusion, f32[2,250,1024]{1,2,0:T(8,128)S(1)} %copy-done.1, f32[2,250,1024]{1,2,0:T(8,128)} %copy.172), kind=kLoop, calls=%fused_computation.4 | loop fusion | flops 7680000 | bytes 14336000 | tf_op jit(solution)/shard_map/sub | solution.py:154
  258.9 4.1 %copy.178 = f32[2,250,1024]{2,0,1:T(2,128)} copy(f32[2,250,1024]{1,2,0:T(8,128)} %get-tuple-element.160) | data formatting | bytes 4096000
  263.0 4.3 %copy.179 = f32[2,250,1024]{2,0,1:T(2,128)} copy(f32[2,250,1024]{1,2,0:T(8,128)} %get-tuple-element.161) | data formatting | bytes 4096000
  267.3 2.3 copy.180
  269.8 1.4 multiply_subtract_fusion.2
  271.3 3.5 %multiply_subtract_fusion.1 = (f32[1600,128]{1,0:T(8,128)}, f32[1600,128]{1,0:T(8,128)}, f32[1600,128]{1,0:T(8,128)}) fusion(f32[1600,128]{1,0:T(8,128)S(1)} %copy-done.3, f32[]{:T(128)S(6)} %mul.369, f32[1696,128]{1,0:T(8,128)} %reshape.189, f32[1600,128]{1,0:T(8,128)} %param.46, f32[1600,128]{1,0:T(8,128)} %param.53), kind=kLoop, calls=%fused_computation.28 | loop fusion | flops 3276800 | bytes 5734404 | tf_op jit(solution)/shard_map/sub | solution.py:154
  (154 shorter events, 18.3 us)
Async XLA Ops:
  0.7 10.1 %copy-start.15 = (bf16[144,75]{1,0:T(8,128)(2,1)S(1)}, bf16[144,75]{1,0:T(8,128)(2,1)}, u32[]{:S(2)}) copy-start(bf16[144,75]{1,0:T(8,128)(2,1)} %constant.62.clone) | copy-start | bytes 64804
  0.7 9.9 %copy-start.25 = (f32[517]{0:T(1024)S(1)}, f32[517]{0:T(1024)}, u32[]{:S(2)}) copy-start(f32[517]{0:T(1024)} %param.44) | copy-start | bytes 6208
  0.7 10.0 %slice-start.1 = ((f32[517]{0:T(1024)}), f32[224]{0:T(256)S(1)}, s32[]{:S(2)}) async-start(f32[517]{0:T(1024)} %param.44), calls=%async_computation.10 | async-start | bytes 2048 | tf_op jit(solution)/shard_map/slice | solution.py:880
  0.7 10.0 %copy-start.33 = (s32[4,16,2]{1,2,0:T(2,128)S(1)}, s32[4,16,2]{1,2,0:T(2,128)}, u32[]{:S(2)}) copy-start(s32[4,16,2]{1,2,0:T(2,128)} %param.34) | copy-start | bytes 1540
  0.7 10.1 %copy-start.12 = (f32[75,32]{0,1:T(8,128)S(1)}, f32[75,32]{0,1:T(8,128)}, u32[]{:S(2)}) copy-start(f32[75,32]{0,1:T(8,128)} %param.38) | copy-start | bytes 28804
  4.2 16.8 %all-to-all-start = ((bf16[8,144,128]{2,1,0:T(8,128)(2,1)}), bf16[8,144,128]{2,1,0:T(8,128)(2,1)S(1)}, u32[]{:S(2)}, u32[]{:S(2)}) async-start(bf16[8,144,128]{2,1,0:T(8,128)(2,1)} %bitcast.4), calls=%async_computation | async-start | bytes 589824 | tf_op jit(solution)/shard_map/all_to_all | solution.py:823
  21.0 0.8 copy-start.5
  45.8 6.5 %copy-start.30 = (f32[4,16,3]{1,0,2:T(4,128)S(1)}, f32[4,16,3]{1,0,2:T(4,128)}, u32[]{:S(2)}) copy-start(f32[4,16,3]{1,0,2:T(4,128)} %param.36) | copy-start | bytes 2308
  45.8 6.6 %copy-start.27 = (f32[4,16,4]{1,2,0:T(4,128)S(1)}, f32[4,16,4]{1,2,0:T(4,128)}, u32[]{:S(2)}) copy-start(f32[4,16,4]{1,2,0:T(4,128)} %param.35) | copy-start | bytes 3076
  45.8 6.7 %copy-start.16 = (f32[32,11]{0,1:T(8,128)S(1)}, f32[32,11]{0,1:T(8,128)}, u32[]{:S(2)}) copy-start(f32[32,11]{0,1:T(8,128)} %param.43) | copy-start | bytes 4228
  45.8 14.1 %copy-start = (bf16[1024,1024]{1,0:T(8,128)(2,1)S(1)}, bf16[1024,1024]{1,0:T(8,128)(2,1)}, u32[]{:S(2)}) copy-start(bf16[1024,1024]{1,0:T(8,128)(2,1)} %constant.63.clone) | copy-start | bytes 6291460
  45.8 13.2 %all-to-all-start.1 = ((bf16[8,8,16,128]{3,2,1,0:T(8,128)(2,1)}), bf16[8,8,16,128]{3,2,1,0:T(8,128)(2,1)S(1)}, u32[]{:S(2)}, u32[]{:S(2)}) async-start(bf16[8,8,16,128]{3,2,1,0:T(8,128)(2,1)} %get-tuple-element.43), calls=%async_computation.1 | async-start | bytes 524288 | tf_op jit(solution)/shard_map/all_to_all | solution.py:823
  59.9 8.3 %copy-start.7 = (s32[4,16,4,64]{3,2,1,0:T(4,128)S(1)}, s32[4,16,4,64]{3,2,1,0:T(4,128)}, u32[]{:S(2)}) copy-start(s32[4,16,4,64]{3,2,1,0:T(4,128)} %param.33) | copy-start | bytes 196612
  64.1 9.9 %all-to-all-start.2 = ((f32[8,8,250]{2,1,0:T(8,128)}), f32[8,8,250]{2,1,0:T(8,128)}, u32[]{:S(2)}, u32[]{:S(2)}) async-start(f32[8,8,250]{2,1,0:T(8,128)} %convolution_bitcast_fusion), calls=%async_computation.2 | async-start | bytes 131072 | tf_op jit(solution)/shard_map/all_to_all | solution.py:823
  68.8 48.2 %copy-start.8 = (f32[4,16,4]{2,1,0:T(8,128)S(1)}, f32[4,16,4]{2,1,0:T(8,128)}, u32[]{:S(2)}) copy-start(f32[4,16,4]{2,1,0:T(8,128)} %broadcast_multiply_fusion.1) | copy-start | bytes 3076
  117.9 9.0 %all-to-all-start.3 = ((bf16[8,8,250]{2,1,0:T(8,128)(2,1)}), bf16[8,8,250]{2,1,0:T(8,128)(2,1)S(1)}, u32[]{:S(2)}, u32[]{:S(2)}) async-start(bf16[8,8,250]{2,1,0:T(8,128)(2,1)} %broadcast_in_dim.19), calls=%async_computation.3 | async-start | bytes 65536 | tf_op jit(solution)/shard_map/all_to_all | solution.py:823
  121.2 25.1 %collective-permute-start = (bf16[8,4,32,128]{3,2,1,0:T(8,128)(2,1)}, bf16[8,4,32,128]{3,2,1,0:T(8,128)(2,1)S(1)}, u32[]{:S(2)}, u32[]{:S(2)}) collective-permute-start(bf16[8,4,32,128]{3,2,1,0:T(8,128)(2,1)} %get-tuple-element.44), channel_id=1, source_target_pairs={{0,1},{1,0},{2,3},{3,2},{4,5},{5,4},{6,7},{7,6},{8,9},{9,8},{10,11... | collective-permute-start | bytes 786440 | tf_op jit(solution)/shard_map/ppermute | solution.py:939
  127.6 5.9 %copy-start.23 = (bf16[10,25]{1,0:T(8,128)(2,1)S(1)}, bf16[10,25]{1,0:T(8,128)(2,1)}, u32[]{:S(2)}) copy-start(bf16[10,25]{1,0:T(8,128)(2,1)} %get-tuple-element.175) | copy-start | bytes 1504
  127.6 6.2 %copy-start.24 = (f32[32,128]{1,0:T(8,128)S(1)}, f32[32,128]{1,0:T(8,128)}, u32[]{:S(2)}) copy-start(f32[32,128]{1,0:T(8,128)} %get-tuple-element.48) | copy-start | bytes 49156
  127.7 6.2 %copy-start.6 = (bf16[64,2,4,256]{3,2,1,0:T(4,128)(2,1)S(1)}, bf16[64,2,4,256]{3,2,1,0:T(4,128)(2,1)}, u32[]{:S(2)}) copy-start(bf16[64,2,4,256]{3,2,1,0:T(4,128)(2,1)} %reshape_reshape.3) | copy-start | bytes 786436
  129.5 13.1 %all-to-all-start.4 = ((bf16[8,8,16,128]{3,2,1,0:T(8,128)(2,1)}), bf16[8,8,16,128]{3,2,1,0:T(8,128)(2,1)S(1)}, u32[]{:S(2)}, u32[]{:S(2)}) async-start(bf16[8,8,16,128]{3,2,1,0:T(8,128)(2,1)} %reshape.175), calls=%async_computation.4 | async-start | bytes 524288 | tf_op jit(solution)/shard_map/all_to_all | solution.py:823
  134.4 12.0 %copy-start.9 = (bf16[8,4,32,128]{3,2,1,0:T(8,128)(2,1)S(1)}, bf16[8,4,32,128]{3,2,1,0:T(8,128)(2,1)}, u32[]{:S(2)}) copy-start(bf16[8,4,32,128]{3,2,1,0:T(8,128)(2,1)} %get-tuple-element.44) | copy-start | bytes 786436
  142.5 34.4 %all-to-all-start.5 = ((bf16[4,2,250,256]{3,1,2,0:T(2,128)(2,1)}), bf16[4,2,250,256]{3,1,2,0:T(2,128)(2,1)S(1)}, u32[]{:S(2)}, u32[]{:S(2)}) async-start(bf16[4,2,250,256]{3,1,2,0:T(2,128)(2,1)} %copy.165), calls=%async_computation.5 | async-start | bytes 2048000 | tf_op jit(solution)/shard_map/all_to_all | solution.py:823
  146.3 1.6 collective-permute-start.1
  148.7 26.2 %copy-start.10 = (f32[144,75]{1,0:T(8,128)S(1)}, f32[144,75]{1,0:T(8,128)}, u32[]{:S(2)}) copy-start(f32[144,75]{1,0:T(8,128)} %constant.66.clone) | copy-start | bytes 129604
  176.7 4.4 %copy-start.34 = (bf16[64]{0:T(256)(128)(2,1)S(1)}, bf16[64]{0:T(256)(128)(2,1)}, u32[]{:S(2)}) copy-start(bf16[64]{0:T(256)(128)(2,1)} %pad.52.clone) | copy-start | bytes 388
  182.2 20.3 %all-to-all-start.6 = ((bf16[32,64,128]{2,1,0:T(8,128)(2,1)}), bf16[32,64,128]{2,1,0:T(8,128)(2,1)S(1)}, u32[]{:S(2)}, u32[]{:S(2)}) async-start(bf16[32,64,128]{2,1,0:T(8,128)(2,1)} %maximum_maximum_fusion), calls=%async_computation.6 | async-start | bytes 1048576 | tf_op jit(solution)/shard_map/all_to_all | solution.py:823
  203.9 17.3 %all-to-all-start.8 = ((bf16[4,2,250,256]{3,1,2,0:T(2,128)(2,1)}), bf16[4,2,250,256]{3,1,2,0:T(2,128)(2,1)S(1)}, u32[]{:S(2)}, u32[]{:S(2)}) async-start(bf16[4,2,250,256]{3,1,2,0:T(2,128)(2,1)} %broadcast_in_dim.23), calls=%async_computation.8 | async-start | bytes 2048000 | tf_op jit(solution)/shard_map/all_to_all | solution.py:823
  221.3 1.1 copy-start.4
  222.4 19.7 %all-to-all-start.7 = ((bf16[32,64,128]{2,1,0:T(8,128)(2,1)}), bf16[32,64,128]{2,1,0:T(8,128)(2,1)}, u32[]{:S(2)}, u32[]{:S(2)}) async-start(bf16[32,64,128]{2,1,0:T(8,128)(2,1)} %broadcast_in_dim.22), calls=%async_computation.7 | async-start | bytes 1048576 | tf_op jit(solution)/shard_map/all_to_all | solution.py:823
  251.9 1.6 copy-start.1
  263.0 4.3 %copy-start.2 = (f32[2,250,1024]{1,2,0:T(8,128)S(1)}, f32[2,250,1024]{1,2,0:T(8,128)}, u32[]{:S(2)}) copy-start(f32[2,250,1024]{1,2,0:T(8,128)} %get-tuple-element.162) | copy-start | bytes 6144004
  267.3 2.4 slice-start
  267.3 2.5 copy-start.11
  267.3 2.5 copy-start.17
  267.3 2.5 copy-start.18
  267.3 3.9 %copy-start.3 = (f32[1600,128]{1,0:T(8,128)S(1)}, f32[1600,128]{1,0:T(8,128)}, u32[]{:S(2)}) copy-start(f32[1600,128]{1,0:T(8,128)} %w_ref.5) | copy-start | bytes 2457604
  271.2 3.6 %copy-start.26 = (f32[517]{0:T(1024)S(1)}, f32[517]{0:T(1024)}, u32[]{:S(2)}) copy-start(f32[517]{0:T(1024)} %param.44) | copy-start | bytes 6208
  271.2 3.6 %copy-start.31 = (f32[517]{0:T(1024)S(1)}, f32[517]{0:T(1024)}, u32[]{:S(2)}) copy-start(f32[517]{0:T(1024)} %param.51) | copy-start | bytes 6208
  271.2 3.6 %copy-start.32 = (f32[517]{0:T(1024)S(1)}, f32[517]{0:T(1024)}, u32[]{:S(2)}) copy-start(f32[517]{0:T(1024)} %param.58) | copy-start | bytes 6208
  271.2 4.3 %copy-start.28 = (f32[32,11]{0,1:T(8,128)S(1)}, f32[32,11]{0,1:T(8,128)}, u32[]{:S(2)}) copy-start(f32[32,11]{0,1:T(8,128)} %param.50) | copy-start | bytes 4228
  271.2 4.2 %copy-start.29 = (f32[32,11]{0,1:T(8,128)S(1)}, f32[32,11]{0,1:T(8,128)}, u32[]{:S(2)}) copy-start(f32[32,11]{0,1:T(8,128)} %param.57) | copy-start | bytes 4228
  271.2 4.9 %copy-start.14 = (f32[15,250]{1,0:T(8,128)S(1)}, f32[15,250]{1,0:T(8,128)}, u32[]{:S(2)}) copy-start(f32[15,250]{1,0:T(8,128)} %param.41) | copy-start | bytes 45004
  271.2 4.9 %copy-start.19 = (f32[15,250]{1,0:T(8,128)S(1)}, f32[15,250]{1,0:T(8,128)}, u32[]{:S(2)}) copy-start(f32[15,250]{1,0:T(8,128)} %param.48) | copy-start | bytes 45004
  271.3 4.8 %copy-start.20 = (f32[15,250]{1,0:T(8,128)S(1)}, f32[15,250]{1,0:T(8,128)}, u32[]{:S(2)}) copy-start(f32[15,250]{1,0:T(8,128)} %param.55) | copy-start | bytes 45004
  271.3 5.5 %copy-start.13 = (f32[75,32]{0,1:T(8,128)S(1)}, f32[75,32]{0,1:T(8,128)}, u32[]{:S(2)}) copy-start(f32[75,32]{0,1:T(8,128)} %param.38) | copy-start | bytes 28804
  271.3 5.5 %copy-start.21 = (f32[75,32]{0,1:T(8,128)S(1)}, f32[75,32]{0,1:T(8,128)}, u32[]{:S(2)}) copy-start(f32[75,32]{0,1:T(8,128)} %param.45) | copy-start | bytes 28804
  271.3 5.5 %copy-start.22 = (f32[75,32]{0,1:T(8,128)S(1)}, f32[75,32]{0,1:T(8,128)}, u32[]{:S(2)}) copy-start(f32[75,32]{0,1:T(8,128)} %param.52) | copy-start | bytes 28804

commit v3 on v2

--- a/solution.py
+++ b/solution.py
@@ -457,6 +457,14 @@
     return lax.dot_general(left, right, (((1,), (1,)), ((), ())), preferred_element_type=F32)
 
 
+def nn_exact(left, right):
+    return lax.dot_general(left, right, (((1,), (0,)), ((), ())), preferred_element_type=F32, precision=HIGH)
+
+
+def nt_exact(left, right):
+    return lax.dot_general(left, right, (((1,), (1,)), ((), ())), preferred_element_type=F32, precision=HIGH)
+
+
 def logistic(v):
     return 0.5 * jnp.tanh(0.5 * v) + 0.5
 
@@ -464,6 +472,11 @@
 def one_hot_eye(size):
     row = lax.broadcasted_iota(jnp.int32, (size, size), 0)
     return (row == lax.broadcasted_iota(jnp.int32, (size, size), 1)).astype(BF)
+
+
+def split(value):
+    high = value.astype(BF)
+    return high, (value - high.astype(F32)).astype(BF)
 
 
 def one_hot_mod(shape, period, axis):
@@ -503,6 +516,17 @@
             total = value if total is None else jnp.where(band == part, value, total)
         swapped.append(total)
     return swapped
+
+
+def wide(tile):
+    return jnp.concatenate([tile] * TILES, axis=1)
+
+
+def folded(values):
+    total = values[:, :LANES]
+    for tile in range(1, values.shape[1] // LANES):
+        total = total + values[:, tile * LANES : (tile + 1) * LANES]
+    return total
 
 
 def twice(tile):
@@ -593,22 +617,23 @@
 def head_kernel(
     half_ref, x_ref, hid_ref, logit_ref, w_ref, mask_ref, bias_ref, place_ref, placet_ref,
     back_ref, dlog_ref, dwd_ref, dwm_ref, sums_ref,
-    win_s, dk_s, wd_ref, wdt_ref, wm_ref, wmt_ref, over_ref,
+    win_s, wd_ref, wdt_ref, wm_ref, wmt_ref, over_ref, wide_s, everywhere_s, turned_s, d_mix_s, d_spot_s, kernel_s,
 ):
     wd_ref[...] = w_ref[...].astype(BF)
     wdt_ref[...] = nt(one_hot_eye(4 * C), wd_ref[...]).astype(BF)
-    copies = one_hot_mod((4 * C, C), C, 0)
-    fourfold = nn(copies, mask_ref[...].astype(BF)).astype(BF)
     row = lax.broadcasted_iota(jnp.int32, (4 * C, 64), 0)
-    wmt_ref[...] = jnp.where(
-        row // C == lax.broadcasted_iota(jnp.int32, (4 * C, 64), 1) // 16,
-        nn(fourfold, one_hot_mod((NM, 64), 16, 1)), 0.0,
-    ).astype(BF)
+    mine_t = row // C == lax.broadcasted_iota(jnp.int32, (4 * C, 64), 1) // 16
     row = lax.broadcasted_iota(jnp.int32, (64, 4 * C), 0)
-    wm_ref[...] = jnp.where(
-        row // 16 == lax.broadcasted_iota(jnp.int32, (64, 4 * C), 1) // C,
-        nt(one_hot_mod((64, NM), 16, 0), fourfold), 0.0,
-    ).astype(BF)
+    mine = row // 16 == lax.broadcasted_iota(jnp.int32, (64, 4 * C), 1) // C
+    for kind, part in enumerate(split(mask_ref[...])):
+        spread_mask = nt(one_hot_mod((4 * C, C), C, 0), part).astype(BF)
+        wide_t = jnp.where(mine_t, nn(spread_mask, one_hot_mod((NM, 64), 16, 1)), 0.0).astype(BF)
+        wide_m = jnp.where(mine, nt(one_hot_mod((64, NM), 16, 0), spread_mask), 0.0).astype(BF)
+        wmt_ref[:, kind * 64 : kind * 64 + 64] = wide_t
+        wm_ref[:, kind * 4 * C : (kind + 1) * 4 * C] = wide_m
+        if kind == 0:
+            wmt_ref[:, 128:192] = wide_t
+            wm_ref[:, 8 * C : 12 * C] = wide_m
     for sub in range(4):
         over_ref[sub * C : (sub + 1) * C, :] = bias_ref[7 * C : 8 * C]
         over_ref[4 * C + sub * 16 : 4 * C + (sub + 1) * 16, :] = bias_ref[8 * C : 8 * C + 16]
@@ -616,103 +641,125 @@
     base = half_ref[0] * own
     lanes = lane_places()
     dwd_ref[...] = jnp.zeros_like(dwd_ref)
-    dwm_ref[...] = jnp.zeros_like(dwm_ref)
+    wide_s[...] = jnp.zeros_like(wide_s)
     sums_ref[...] = jnp.zeros_like(sums_ref)
-    row8 = lax.broadcasted_iota(jnp.int32, (8, 2 * LANES), 0)
+    cells = TILES * LANES
+    row8 = lax.broadcasted_iota(jnp.int32, (8, cells), 0)
     color = (row8 % 4) != 3
     row16 = lax.broadcasted_iota(jnp.int32, (16, 32), 0)
     lane16 = lax.broadcasted_iota(jnp.int32, (16, 32), 1)
 
+    for sub in range(4):
+        everywhere_s[sub * WIN : (sub + 1) * WIN] = place_ref[sub]
+        turned_s[:, sub * WIN : (sub + 1) * WIN] = placet_ref[sub]
+    row = lax.broadcasted_iota(jnp.int32, (4 * WIN, 64), 0) // WIN
+    own_spots = row == lax.broadcasted_iota(jnp.int32, (4 * WIN, 64), 1) // 16
+    row = lax.broadcasted_iota(jnp.int32, (64, 4 * WIN), 0) // 16
+    own_turned = row == lax.broadcasted_iota(jnp.int32, (64, 4 * WIN), 1) // WIN
+
     def frame(i, _):
         t = base + i
         spread(image_tiles(x_ref, t), lanes, 1, win_s, 16, 0)
+        window = jnp.concatenate([win_s[tile : tile + 3].reshape(WIN, LANES) for tile in range(TILES)], axis=1)
+        window = window.reshape(18, 8, cells)
         logits = logit_ref[i]
         powers = jnp.exp(logits - jnp.max(logits, -1, keepdims=True))
         kernels = powers / jnp.sum(powers, -1, keepdims=True)
         kernels = jnp.where(row16 == 0, (lane16 == KK // 2).astype(F32), jnp.where(row16 <= NK, kernels, 0.0))
-        kernels_low = kernels.astype(BF)
-        dk_s[...] = jnp.zeros_like(dk_s)
-        for two in range(0, TILES, 2):
-            hidden = jnp.concatenate([hid_ref[t, two], hid_ref[t, two + 1]], axis=1)
-            window = stacked(win_s, two, 3)
-            upper = nn(wdt_ref[...], hidden) + twice(over_ref[0 : 4 * C])
-            gate = logistic(upper)
-            active = (upper * gate).astype(BF)
-            scores = nn(wm_ref[...], active) + twice(over_ref[4 * C : 4 * C + 64])
-            scores = scores.reshape(4, 16, 2 * LANES)
-            powers = jnp.exp(scores - jnp.max(scores, 1, keepdims=True))
-            masks = powers / jnp.sum(powers, 1, keepdims=True)
-            after = jnp.concatenate([x_ref[t + 1, two], x_ref[t + 1, two + 1]], axis=1).astype(F32)
-            d_scores = []
-            for sub in range(4):
-                mask_low = masks[sub].astype(BF)
-                spots = nt(place_ref[sub], kernels_low).astype(BF)
-                mixing = nn(spots, mask_low)
-                both = jnp.sum((mixing * window).reshape(18, 8, 2 * LANES), 0)
-                result = both + pltpu.roll(both, 4, 0)
-                goal = after[(sub % 2) * 8 : (sub % 2) * 8 + 8]
-                turned = pltpu.roll(goal, 4, 0)
-                goal = jnp.where((row8 < 4) == (sub // 2 == 0), goal, turned)
-                counted = goal[3:4]
-                diff = jnp.where(color, result - goal, 0.0)
-                weighted = diff * counted
-                lost = weighted * diff
-                sums_ref[192:200] += lost[:, :LANES] + lost[:, LANES:]
-                d_result = 2.0 * weighted
-                d_mix = (window.reshape(18, 8, 2 * LANES) * d_result[None]).reshape(WIN, 2 * LANES).astype(BF)
-                spots_t = nn(kernels_low, placet_ref[sub]).astype(BF)
-                d_mask = nn(spots_t, d_mix)
-                d_spots = nt(mask_low, d_mix)
-                dk_s[...] += lax.dot_general(
-                    d_spots, place_ref[sub].astype(F32), (((1,), (0,)), ((), ())),
-                    preferred_element_type=F32, precision=HIGH,
-                )
-                inner = jnp.sum(masks[sub] * d_mask, 0, keepdims=True)
-                d_scores.append(masks[sub] * (d_mask - inner))
-            d_score = jnp.concatenate(d_scores, axis=0)
-            sums_ref[128:192] += d_score[:, :LANES] + d_score[:, LANES:]
-            d_score_low = d_score.astype(BF)
-            d_active = nn(wmt_ref[...], d_score_low)
-            dwm_ref[...] += nt(active, d_score_low)
-            d_upper = d_active * (gate * (1.0 + upper * (1.0 - gate)))
-            sums_ref[0:128] += d_upper[:, :LANES] + d_upper[:, LANES:]
-            d_upper_low = d_upper.astype(BF)
-            dwd_ref[...] += nt(hidden, d_upper_low)
-            back = nn(wd_ref[...], d_upper_low).astype(BF)
-            for one in range(2):
-                back_ref[i, two + one] = back[:, one * LANES : (one + 1) * LANES]
-        d_kernels = dk_s[...]
-        inner = jnp.sum(d_kernels * kernels, -1, keepdims=True)
-        dlog_ref[i] = kernels * (d_kernels - inner)
+        kernel_s[i] = kernels
+        spots = []
+        turned = []
+        for part in split(kernels):
+            part = jnp.concatenate([part, part, part, part], axis=0)
+            spots.append(jnp.where(own_spots, nt(everywhere_s[...], part), 0.0).astype(BF))
+            turned.append(jnp.where(own_turned, nn(part, turned_s[...]), 0.0).astype(BF))
+        spots = jnp.concatenate([spots[0], spots[1], spots[0]], axis=1)
+        turned = jnp.concatenate(turned, axis=0)
+        hidden = jnp.concatenate([hid_ref[t, tile] for tile in range(TILES)], axis=1)
+        upper = nn(wdt_ref[...], hidden) + wide(over_ref[0 : 4 * C])
+        gate = logistic(upper)
+        active, active_rest = split(upper * gate)
+        scores = nn(wm_ref[...], jnp.concatenate([active, active, active_rest], axis=0)) + wide(over_ref[4 * C : 4 * C + 64])
+        scores = scores.reshape(4, 16, cells)
+        powers = jnp.exp(scores - jnp.max(scores, 1, keepdims=True))
+        masks = powers / jnp.sum(powers, 1, keepdims=True)
+        mask_low, mask_rest = split(masks.reshape(64, cells))
+        mixing = nn(spots, jnp.concatenate([mask_low, mask_low, mask_rest], axis=0)).reshape(4, 18, 8, cells)
+        after = jnp.concatenate([x_ref[t + 1, tile] for tile in range(TILES)], axis=1).astype(F32)
+        lost = None
+        for sub in range(4):
+            both = jnp.sum(mixing[sub] * window, 0)
+            result = both + pltpu.roll(both, 4, 0)
+            goal = after[(sub % 2) * 8 : (sub % 2) * 8 + 8]
+            goal = jnp.where((row8 < 4) == (sub // 2 == 0), goal, pltpu.roll(goal, 4, 0))
+            diff = jnp.where(color, result - goal, 0.0)
+            weighted = diff * goal[3:4]
+            part = weighted * diff
+            lost = part if lost is None else lost + part
+            d_result = 2.0 * weighted
+            d_mix_s[sub * WIN : (sub + 1) * WIN] = (window * d_result[None]).reshape(WIN, cells).astype(BF)
+        sums_ref[192:200] += folded(lost)
+        d_mask = nn(turned, d_mix_s[...])
+        d_mask = (d_mask[:64] + d_mask[64:]).reshape(4, 16, cells)
+        d_spot_s[i] = nt(mask_low, d_mix_s[...])
+        inner = jnp.sum(masks * d_mask, 1, keepdims=True)
+        d_score = (masks * (d_mask - inner)).reshape(64, cells)
+        sums_ref[128:192] += folded(d_score)
+        d_score_low, d_score_rest = split(d_score)
+        d_active = nn(wmt_ref[...], jnp.concatenate([d_score_low, d_score_low, d_score_rest], axis=0))
+        wide_s[...] += nt(d_score_low, active)
+        d_upper = d_active * (gate * (1.0 + upper * (1.0 - gate)))
+        sums_ref[0:128] += folded(d_upper)
+        d_upper_low = d_upper.astype(BF)
+        dwd_ref[...] += nt(hidden, d_upper_low)
+        back = nn(wd_ref[...], d_upper_low).astype(BF)
+        for tile in range(TILES):
+            back_ref[i, tile] = back[:, tile * LANES : (tile + 1) * LANES]
         return 0
 
     lax.fori_loop(0, own, frame, 0)
+    d_kernels = None
+    for sub in range(4):
+        rows = jnp.concatenate([d_spot_s[i, sub * 16 : sub * 16 + 16] for i in range(own)], axis=0)
+        place = lax.broadcasted_iota(jnp.int32, rows.shape, 1) // WIN
+        part = nn_exact(jnp.where(place == sub, rows, 0.0), everywhere_s[...].astype(F32))
+        d_kernels = part if d_kernels is None else d_kernels + part
+    for i in range(own):
+        kernels = kernel_s[i]
+        d_one = d_kernels[16 * i : 16 * i + 16]
+        inner = jnp.sum(d_one * kernels, -1, keepdims=True)
+        dlog_ref[i] = kernels * (d_one - inner)
+    row = lax.broadcasted_iota(jnp.int32, (64, 4 * C), 0)
+    lane = lax.broadcasted_iota(jnp.int32, (64, 4 * C), 1)
+    own_block = jnp.where(row // 16 == lane // C, wide_s[...], 0.0)
+    fold = lax.broadcasted_iota(jnp.int32, (4 * C, LANES), 0) % C
+    fold = (fold == lax.broadcasted_iota(jnp.int32, (4 * C, LANES), 1)).astype(F32)
+    dwm_ref[...] = jnp.sum(nn_exact(own_block, fold).reshape(4, 16, LANES), 0)
 
 
 def backward_kernel(
-    half_ref, x_ref, enc_ref, hid_ref, act_ref, cell_ref, dec_ref, fc_ref, w_ref, we_ref, bias_ref,
-    dw_ref, dwe_ref, sums_ref,
-    gate_s, keep_s, denc_s, back_s, state_s, win_s, join_s, wb_ref,
+    half_ref, act_ref, cell_ref, dec_ref, fc_ref, w_ref,
+    keep_ref, denc_ref, lines_ref,
+    gate_s, back_s, state_s, wb_s,
 ):
     for tap in range(KK):
         place = tap % KS * 2 * C
         turn = (KS - 1 - tap // KS) * 4 * C
-        wb_ref[place : place + 2 * C, turn : turn + 4 * C] = w_ref[tap * 2 * C : (tap + 1) * 2 * C, :].astype(BF)
-    steps = enc_ref.shape[0]
+        wb_s[place : place + 2 * C, turn : turn + 4 * C] = w_ref[tap * 2 * C : (tap + 1) * 2 * C, :].astype(BF)
+    steps = act_ref.shape[0]
     own = steps // HALVES
     base = half_ref[0] * own
     lanes = lane_places()
     back_s[...] = jnp.zeros_like(back_s)
     state_s[...] = jnp.zeros_like(state_s)
-    dw_ref[...] = jnp.zeros_like(dw_ref)
-    dwe_ref[...] = jnp.zeros_like(dwe_ref)
-    sums_ref[...] = jnp.zeros_like(sums_ref)
+    lines_ref[...] = jnp.zeros_like(lines_ref)
 
     def retreat(step, _):
         t = steps - 1 - step
         half = t // own
         inside = t % own
-        mine = jnp.where(half == half_ref[0], 1.0, 0.0)
+        mine = half == half_ref[0]
+        counted = jnp.where(mine, 1.0, 0.0)
         earlier = jnp.maximum(t - 1, 0)
         started = jnp.where(t > 0, 1.0, 0.0)
         tiles = []
@@ -741,26 +788,74 @@
                 ],
                 axis=0,
             )
-            sums_ref[3 * C : 7 * C] += d_gates * mine
-            low = d_gates.astype(BF)
-            keep_s[t, tile] = low
-            tiles.append(low.astype(F32))
+            lines_ref[...] += d_gates * counted
+            tiles.append(d_gates.astype(BF))
+
+        @pl.when(mine)
+        def _():
+            for tile in range(TILES):
+                keep_ref[inside, tile] = tiles[tile]
+
+        wide = [tile.astype(F32) for tile in tiles]
         for index in range(TILES + 4):
             tile = index - 2
-            gate_s[index] = moved(tiles[tile % TILES], lanes, 0, tile // TILES).astype(BF)
+            gate_s[index] = moved(wide[tile % TILES], lanes, 0, tile // TILES).astype(BF)
+        d_enc = []
         for two in range(0, TILES, 2):
-            sums = nn(wb_ref[...], stacked(gate_s, two, KS))
+            sums = nn(wb_s[...], stacked(gate_s, two, KS))
             for one in range(2):
                 part = sums[:, one * LANES : (one + 1) * LANES]
                 total = None
                 for shift in range(KS):
                     value = moved(part[shift * 2 * C : (shift + 1) * 2 * C], lanes, 2 - shift, 0)
                     total = value if total is None else total + value
-                denc_s[t, two + one] = total[:C]
+                d_enc.append(total[:C])
                 back_s[two + one] = total[C:]
+
+        @pl.when(mine)
+        def _():
+            for tile in range(TILES):
+                denc_ref[inside, tile] = d_enc[tile]
+
         return 0
 
     lax.fori_loop(0, steps, retreat, 0)
+
+
+ROW_DEC = KK * 2 * C
+ROW_COND = ROW_DEC + C
+ROW_ENC = ROW_COND + 32
+ROW_MASK = ROW_ENC + C
+ROW_VECTOR = ROW_MASK + 16
+ROWS = ROW_VECTOR + 16
+PART = 64
+SMALL = ROWS - ROW_DEC
+
+
+def vector_places():
+    place = np.zeros((7 * C + 4 * C + 64, 5 * LANES), np.float32)
+    for line in range(7 * C):
+        place[line, line] = 1.0
+    for line in range(4 * C):
+        place[7 * C + line, 7 * C + NK * KK + line % C] = 1.0
+    for line in range(64):
+        if line % 16 < NM:
+            place[11 * C + line, 8 * C + NK * KK + line % 16] = 1.0
+    return place
+
+
+def pack_kernel(
+    half_ref, x_ref, enc_ref, hid_ref, keep_ref, denc_ref, lines_ref, head_ref, ddec_ref, dmask_ref, dcond_ref,
+    dline_ref, scalar_ref, we_ref, bias_ref, place_ref, encoder_ref,
+    block_ref,
+    win_s, join_s, dwe_s, sums_s, packed_s,
+):
+    own = keep_ref.shape[0]
+    base = half_ref[0] * own
+    lanes = lane_places()
+    dwe_s[...] = jnp.zeros_like(dwe_s)
+    sums_s[...] = jnp.zeros_like(sums_s)
+    packed_s[...] = jnp.zeros_like(packed_s)
 
     def gather(i, _):
         t = base + i
@@ -772,8 +867,8 @@
         )
         spread(image_tiles(x_ref, t), lanes, 1, win_s, 16, 0)
         for two in range(0, TILES, 2):
-            d_gates = jnp.concatenate([keep_s[t, two], keep_s[t, two + 1]], axis=1)
-            dw_ref[...] += nt(stacked(join_s, two, KS), d_gates)
+            d_gates = jnp.concatenate([keep_ref[i, two], keep_ref[i, two + 1]], axis=1)
+            packed_s[0:ROW_DEC] += nt(stacked(join_s, two, KS), d_gates)
             window = stacked(win_s, two, 3)
             pre = nn(we_ref[...], window) + twice(bias_ref[0:C])
             centered = pre - jnp.mean(pre, 0, keepdims=True)
@@ -782,7 +877,7 @@
             gain = twice(bias_ref[C : 2 * C])
             value = normal * gain + twice(bias_ref[2 * C : 3 * C])
             gate = logistic(value)
-            d_out = jnp.concatenate([denc_s[t, two], denc_s[t, two + 1]], axis=1)
+            d_out = jnp.concatenate([denc_ref[i, two], denc_ref[i, two + 1]], axis=1)
             d_value = d_out * (gate * (1.0 + value * (1.0 - gate)))
             d_gain = d_value * normal
             d_normal = d_value * gain
@@ -791,22 +886,173 @@
                 - jnp.mean(d_normal, 0, keepdims=True)
                 - normal * jnp.mean(d_normal * normal, 0, keepdims=True)
             )
-            sums_ref[0:C] += d_pre[:, :LANES] + d_pre[:, LANES:]
-            sums_ref[C : 2 * C] += d_gain[:, :LANES] + d_gain[:, LANES:]
-            sums_ref[2 * C : 3 * C] += d_value[:, :LANES] + d_value[:, LANES:]
-            dwe_ref[...] += nt(d_pre.astype(BF), window)
+            sums_s[0:C] += d_pre[:, :LANES] + d_pre[:, LANES:]
+            sums_s[C : 2 * C] += d_gain[:, :LANES] + d_gain[:, LANES:]
+            sums_s[2 * C : 3 * C] += d_value[:, :LANES] + d_value[:, LANES:]
+            dwe_s[...] += nt(d_pre.astype(BF), window)
         return 0
 
     lax.fori_loop(0, own, gather, 0)
+    packed_s[ROW_DEC:ROW_COND] = ddec_ref[...]
+    packed_s[ROW_COND:ROW_ENC] = dcond_ref[...]
+    packed_s[ROW_ENC:ROW_MASK] = nn_exact(dwe_s[...], encoder_ref[...])
+    packed_s[ROW_MASK:ROW_VECTOR] = dmask_ref[...]
+    ones = jnp.ones((8, LANES), F32)
+    sums_s[3 * C : 7 * C] = lines_ref[...]
+    sums_s[7 * C : 11 * C + 64] = head_ref[0:192]
+    line = nn_exact(nt_exact(ones, sums_s[...]), place_ref[...])[0:1] + jnp.sum(dline_ref[...], 0, keepdims=True)
+    packed_s[ROW_VECTOR : ROW_VECTOR + 8] = jnp.concatenate(
+        [line[:, place * LANES : (place + 1) * LANES] for place in range(5)] + [jnp.zeros((3, LANES), F32)], axis=0
+    )
+    lost = jnp.sum(jnp.sum(head_ref[192:196], 0, keepdims=True), 1, keepdims=True)
+    lane = lax.broadcasted_iota(jnp.int32, (1, LANES), 1)
+    value = jnp.where(lane == 0, lost, scalar_ref[...])
+    terms = []
+    for _ in range(3):
+        low = value.astype(BF).astype(F32)
+        terms.append(low)
+        value = value - low
+    devices = block_ref.shape[0]
+    large = ROW_DEC // devices
+    small = SMALL // devices
+    fill = jnp.zeros((PART - large - 2 * small - 3, LANES), F32)
+    for device in range(devices):
+        value = packed_s[ROW_DEC + device * small : ROW_DEC + (device + 1) * small]
+        high = value.astype(BF).astype(F32)
+        rows = [packed_s[device * large : (device + 1) * large], high, value - high] + terms + [fill]
+        block_ref[device] = jnp.concatenate(rows, axis=0).astype(BF)
+
+
+def total_kernel(got_ref, out_ref, scalar_ref):
+    devices, rows, _ = got_ref.shape
+    total = got_ref[0].astype(F32)
+    for device in range(1, devices):
+        total = total + got_ref[device].astype(F32)
+    large = ROW_DEC // devices
+    small = SMALL // devices
+    end = large + 2 * small
+    scalar_ref[...] = total[end : end + 1] + total[end + 1 : end + 2] + total[end + 2 : end + 3]
+    value = total[large : large + small] + total[large + small : end]
+    high = value.astype(BF).astype(F32)
+    low = jnp.concatenate([total[:large], high, value - high, total[end:]], axis=0).astype(BF)
+    for device in range(devices):
+        out_ref[device] = low
+
+
+def logit_map_kernel(hid_ref, sum_ref, out_ref, squares_ref, turned_s):
+    logits = NK * KK
+    eye = one_hot_eye(logits)
+    groups, items, _ = sum_ref.shape
+    for group in range(groups):
+        turned_s[:, group * items : (group + 1) * items] = nt(eye, sum_ref[group]).astype(BF)
+    squares = jnp.zeros((1, LANES), F32)
+    stride = 2 * WB * C // LANES
+    for row in range(2):
+        for start in range(0, WB * C, 2 * LANES):
+            hid = jnp.concatenate(
+                [hid_ref[group, row, :, start : start + 2 * LANES] for group in range(groups)], axis=0
+            )
+            grad = nn(turned_s[...], hid)
+            for one in range(2):
+                part = grad[:, one * LANES : (one + 1) * LANES]
+                squares = squares + jnp.sum(part * part, 0, keepdims=True)
+                out_ref[pl.ds((start // LANES + one) * 2 + row, logits, stride=stride), :] = part
+    squares_ref[...] = squares
+
+
+def update(weight, grad, first, second, rate):
+    first = BETA_ONE * first + (1.0 - BETA_ONE) * grad
+    second = BETA_TWO * second + (1.0 - BETA_TWO) * grad * grad
+    shown = second * (1.0 / (1.0 - BETA_TWO**STEP_NO))
+    step = first * (1.0 / (1.0 - BETA_ONE**STEP_NO)) / (shown * lax.rsqrt(shown) + ADAM_EPS)
+    return (weight - rate * (step + DECAY * weight), first, second)
+
+
+def update_kernel(rates, got_ref, scalar_ref, dfc_ref, *refs):
+    weights, firsts, seconds = refs[0:7], refs[7:14], refs[14:21]
+    norm_ref = refs[21]
+    news = refs[22:29], refs[29:36], refs[36:43]
+    packed_s, fc_s, lstm_s, sems = refs[43:]
+    devices = got_ref.shape[0]
+    large = ROW_DEC // devices
+    small = SMALL // devices
+    for device in range(devices):
+        rows = got_ref[device].astype(F32)
+        packed_s[device * large : (device + 1) * large] = rows[:large]
+        packed_s[ROW_DEC + device * small : ROW_DEC + (device + 1) * small] = (
+            rows[large : large + small] + rows[large + small : large + 2 * small]
+        )
+
+    def add_rows(block, total):
+        rows = packed_s[pl.ds(pl.multiple_of(block * 32, 32), 32)]
+        return total + jnp.sum((rows * rows).reshape(4, 8, LANES), 0)
+
+    squares = lax.fori_loop(0, ROWS // 32, add_rows, jnp.zeros((8, LANES), F32))
+    terms = scalar_ref[...]
+    squares = jnp.sum(jnp.sum(squares, 0, keepdims=True), 1, keepdims=True) + terms[:, 2:3]
+    inv_count = 1.0 / terms[:, 1:2]
+    norm = jnp.sqrt(squares) * inv_count
+    factor = inv_count * (CLIP_NORM / jnp.maximum(norm, CLIP_NORM))
+    norm_ref[...] = jnp.sum(norm)
+
+    copies = []
+
+    def in_blocks(index, grad_ref, scratch, chunks):
+        rows = grad_ref.shape[0] if index == 2 else ROW_DEC
+        chunk = rows // chunks
+        wide = chunk // 2
+        for at in range(chunks):
+
+            def block(i, _):
+                here = pl.ds(pl.multiple_of(at * chunk + i * wide, 8), wide)
+                new = update(
+                    weights[index][here], grad_ref[here] * factor, firsts[index][here], seconds[index][here],
+                    rates[index],
+                )
+                for kind in range(3):
+                    scratch[kind, here] = new[kind]
+                return 0
+
+            lax.fori_loop(0, chunk // wide, block, 0)
+            for kind in range(3):
+                here = pl.ds(at * chunk, chunk)
+                copy = pltpu.make_async_copy(
+                    scratch.at[kind, here], news[kind][index].at[here], sems.at[len(copies)]
+                )
+                copy.start()
+                copies.append(copy)
+
+    in_blocks(2, dfc_ref, fc_s, 5)
+    in_blocks(1, packed_s, lstm_s, 2)
+
+    def step(index, grad):
+        new = update(weights[index][...], grad * factor, firsts[index][...], seconds[index][...], rates[index])
+        for kind in range(3):
+            news[kind][index][...] = new[kind]
+
+    step(0, packed_s[ROW_ENC:ROW_MASK, : KK * 3])
+    cond = jnp.concatenate([packed_s[ROW_COND : ROW_COND + 16], packed_s[ROW_COND + 16 : ROW_COND + 32]], axis=1)
+    step(3, cond[:COND, : NK * KK])
+    step(4, packed_s[ROW_DEC:ROW_COND])
+    step(5, packed_s[ROW_MASK : ROW_MASK + NM, 0:C])
+    line = jnp.concatenate([packed_s[ROW_VECTOR + place : ROW_VECTOR + place + 1] for place in range(5)], axis=1)
+    step(6, line[:, : weights[6].shape[1]])
+    for copy in copies:
+        copy.wait()
 
 
 SMEM_SPEC = pl.BlockSpec(memory_space=pltpu.SMEM)
 VMEM_SPEC = pl.BlockSpec(memory_space=pltpu.VMEM)
 
 
-def call(kernel, outs, scratch, half, *operands):
+def cost(micros):
+    return pl.CostEstimate(flops=int(micros * 8e8), bytes_accessed=1024, transcendentals=0)
+
+
+def call(kernel, micros, outs, scratch, half, *operands):
     return pl.pallas_call(
         kernel,
+        cost_estimate=cost(micros),
         out_shape=[jax.ShapeDtypeStruct(shape, kind) for shape, kind in outs],
         in_specs=[SMEM_SPEC] + [VMEM_SPEC] * len(operands),
         out_specs=[VMEM_SPEC] * len(outs),
@@ -834,21 +1080,6 @@
     order = np.zeros((WB * C, WB * C), np.float32)
     order[sent, natural] = 1.0
     return order
-
-
-def in_three(values):
-    terms = []
-    for _ in range(3):
-        low = lax.optimization_barrier(values.astype(BF))
-        terms.append(low)
-        values = values - low.astype(F32)
-    return jnp.concatenate(terms)
-
-
-def in_rows(values):
-    flat = values.reshape(-1)
-    rows = -(-flat.shape[0] // LANES)
-    return jnp.pad(flat, (0, rows * LANES - flat.shape[0])).reshape(rows, LANES)
 
 
 def whole_clips(
@@ -882,6 +1113,7 @@
     cells = (steps, TILES, C, LANES)
     x, enc, hid, act, cell, strips_out = call(
         forward_kernel,
+        20,
         [
             ((shots, TILES, 16, LANES), BF), (cells, BF), (cells, BF), ((steps, TILES, 4 * C, LANES), F32),
             (cells, F32), ((count, own, 16, LANES), BF),
@@ -895,9 +1127,10 @@
     items = clips * steps
     order = jnp.asarray(strip_order(), BF)
     k_fc = w_fc.astype(BF)
-    strip_hid = exchange(strips_out, "row").reshape(items * 2, WB * C)
-    strip_hid = jnp.dot(strip_hid, order, preferred_element_type=F32).astype(BF).reshape(items, 2, WB * C)
-    parts = jnp.einsum("mjk,jnk->mn", strip_hid, k_fc, preferred_element_type=F32)
+    strip_hid = exchange(strips_out, "row").reshape(items, 2, WB * C)
+    strip_hid = jnp.einsum("mjk,kl->jml", strip_hid, order, preferred_element_type=F32).astype(BF)
+    parts = jnp.einsum("jmk,jnk->mn", strip_hid, k_fc, preferred_element_type=F32)
+    strip_hid_all = to_all(strip_hid, "clip")
     summed = jnp.sum(exchange(parts.reshape(count, own, NK * KK), "row"), 0)
     presence = flags.astype(F32)
     conditions = jnp.concatenate(
@@ -913,21 +1146,25 @@
     logits = jnp.pad(
         logits.reshape(own, NK, KK), ((0, 0), (1, 5), (0, 32 - KK)), constant_values=-1e30
     )
-    dec, d_logit, d_dec, d_mask_wide, head_sums = call(
+    dec, d_logit, d_dec, d_mask, head_sums = call(
         head_kernel,
+        30,
         [
-            ((own, TILES, C, LANES), BF), ((own, 16, 32), F32), ((C, 4 * C), F32), ((4 * C, 64), F32),
+            ((own, TILES, C, LANES), BF), ((own, 16, 32), F32), ((C, 4 * C), F32), ((16, LANES), F32),
             ((200, LANES), F32),
         ],
         [
-            ((6, 48, LANES), F32), ((16, 32), F32), ((C, 4 * C), BF), ((4 * C, C), BF), ((64, 4 * C), BF),
-            ((4 * C, 64), BF), ((4 * C + 64, LANES), F32),
+            ((6, 48, LANES), F32), ((C, 4 * C), BF), ((4 * C, C), BF), ((64, 12 * C), BF),
+            ((4 * C, 192), BF), ((4 * C + 64, LANES), F32), ((64, 4 * C), F32),
+            ((4 * WIN, 32), BF), ((32, 4 * WIN), BF), ((4 * WIN, TILES * LANES), BF), ((own, 64, 4 * WIN), F32),
+            ((own, 16, 32), F32),
         ],
-        half_1, x, hid, logits, w_deconv, w_mask, bias,
+        half_1, x, hid, logits, w_deconv, w_mask.T, bias,
         jnp.asarray(places, BF), jnp.asarray(places.transpose(0, 2, 1), BF),
     )
     d_logit = d_logit[:, 1 : NK + 1, :KK].reshape(own, NK * KK)
-    d_sum = to_all(d_logit.astype(BF), "row").reshape(items, NK * KK)
+    every_sum = to_all(d_logit.astype(BF), ("clip", "row")).reshape(-1, items, NK * KK)
+    d_sum = lax.dynamic_index_in_dim(every_sum, lax.axis_index("clip"), 0, False)
     back_fc = jnp.einsum("mn,jnk->mjk", d_sum, k_fc, preferred_element_type=F32).astype(BF)
     back_fc = lax.dot_general(
         back_fc.reshape(items * 2, WB * C), order, (((1,), (1,)), ((), ())), preferred_element_type=F32
@@ -939,73 +1176,93 @@
         other = lax.ppermute(block, "row", swap)
         return jnp.stack([jnp.where(half == 0, block, other), jnp.where(half == 0, other, block)])
 
-    d_lstm, d_enc_wide, sums = call(
+    keep, d_enc, lines = call(
         backward_kernel,
-        [((KK * 2 * C, 4 * C), F32), ((C, WIN), F32), ((7 * C, LANES), F32)],
+        16,
+        [((own, TILES, 4 * C, LANES), BF), ((own, TILES, C, LANES), F32), ((4 * C, LANES), F32)],
         [
-            ((8, 4 * C, LANES), BF), ((steps, TILES, 4 * C, LANES), BF), (cells, F32), ((TILES, C, LANES), F32),
-            ((TILES, C, LANES), F32), ((6, 48, LANES), BF), ((8, KS * 2 * C, LANES), BF),
+            ((8, 4 * C, LANES), BF), ((TILES, C, LANES), F32), ((TILES, C, LANES), F32),
             ((KS * 2 * C, KS * 4 * C), BF),
         ],
-        half_1, x, enc, hid, act, cell, in_order(dec), in_order(back_fc), w_lstm, wide_enc, bias,
+        half_1, act, cell, in_order(dec), in_order(back_fc), w_lstm,
     )
     groups = lax.axis_size("clip")
-    part = WB * C // groups
-    d_fc = jnp.einsum(
-        "mjqk,mn->qjnk", strip_hid.reshape(items, 2, groups, part), d_sum, preferred_element_type=F32
-    ).astype(BF)
-    d_fc = jnp.sum(exchange(d_fc, "clip").astype(F32), 0)
-    fc_squares = jnp.sum(d_fc * d_fc)
-    d_fc = jnp.transpose(to_all(d_fc.astype(BF), "clip"), (1, 2, 0, 3)).reshape(w_fc.shape).astype(F32)
-
-    d_enc = jnp.einsum("rk,or->ko", jnp.asarray(encoder, F32), d_enc_wide, precision=HIGH)
+
+    strip_hid_all, every_sum, _ = lax.optimization_barrier((strip_hid_all, every_sum, lines))
+    d_fc, fc_squares = pl.pallas_call(
+        logit_map_kernel,
+        cost_estimate=cost(2),
+        out_shape=[
+            jax.ShapeDtypeStruct((w_fc.size // LANES, LANES), F32), jax.ShapeDtypeStruct((1, LANES), F32)
+        ],
+        in_specs=[VMEM_SPEC] * 2,
+        out_specs=[VMEM_SPEC] * 2,
+        scratch_shapes=[pltpu.VMEM((NK * KK, groups * items), BF)],
+        compiler_params=pltpu.CompilerParams(vmem_limit_bytes=VMEM_BYTES),
+    )(strip_hid_all, every_sum)
+    fc_squares = jnp.sum(fc_squares) / groups
+
     d_cond = jnp.dot(cond.T, d_logit, precision=HIGH)
-    d_mask = sum(d_mask_wide[sub * C : (sub + 1) * C, sub * 16 : sub * 16 + NM] for sub in range(4))
-    head_lines = jnp.sum(head_sums, 1)
-    d_vector = jnp.concatenate(
-        [
-            jnp.sum(sums, 1),
-            jnp.sum(d_logit, 0),
-            jnp.sum(head_lines[:128].reshape(4, C), 0),
-            jnp.sum(head_lines[128:192].reshape(4, 16), 0)[:NM],
-        ]
-    )
-    scalars = jnp.stack([jnp.sum(head_lines[192:196]), jnp.sum(valid.astype(F32)), fc_squares])
+    d_cond = jnp.pad(d_cond, ((0, 16 - COND), (0, 2 * LANES - NK * KK)))
+    d_cond = jnp.concatenate([d_cond[:, :LANES], d_cond[:, LANES:]], axis=0)
+    d_line = jnp.pad(d_logit, ((0, 0), (7 * C, 5 * LANES - 7 * C - NK * KK)))
+    scalars = jnp.stack([jnp.zeros_like(fc_squares), jnp.sum(valid.astype(F32)), fc_squares])
+    scalars = jnp.pad(scalars, (0, LANES - 3)).reshape(1, LANES)
     both = ("clip", "row")
     devices = lax.axis_size(both)
-    small = [d_enc, d_cond, d_dec, d_mask, d_vector]
-    block = jnp.concatenate([in_rows(value.astype(BF)) for value in [d_lstm] + small])
-    each = -(-block.shape[0] // devices)
-    block = jnp.pad(block, ((0, devices * each - block.shape[0]), (0, 0))).reshape(devices, each, LANES)
-    extra = jnp.pad(in_three(scalars), (0, LANES - 9))
-    extra = jnp.broadcast_to(extra, (devices, 1, LANES))
-    fill = jnp.zeros((devices, -(each + 1) % 16, LANES), BF)
-    got = jnp.sum(exchange(jnp.concatenate([block, extra, fill], axis=1), both).astype(F32), 0)
-    loss_sum, valid_count, squares = got[each, 0:3] + got[each, 3:6] + got[each, 6:9]
-    got = to_all(got.astype(BF), both)[:, :each].reshape(devices * each, LANES).astype(F32)
-    summed = []
-    start = 0
-    for value in [d_lstm] + small:
-        rows = -(-value.size // LANES)
-        summed.append(got[start : start + rows].reshape(-1)[: value.size].reshape(value.shape))
-        start += rows
-    d_lstm, d_enc, d_cond, d_dec, d_mask, d_vector = summed
-    inv_count = 1.0 / valid_count
-    grads = (d_enc, d_lstm, d_fc, d_cond, d_dec, d_mask, d_vector)
-    squares = squares + jnp.sum(got * got)
-    grad_norm = jnp.sqrt(squares) * inv_count
-    factor = inv_count * (CLIP_NORM / jnp.maximum(grad_norm, CLIP_NORM))
+    block = call(
+        pack_kernel,
+        12,
+        [((devices, PART, LANES), BF)],
+        [
+            ((6, 48, LANES), BF), ((8, KS * 2 * C, LANES), BF), ((C, WIN), F32), ((11 * C + 64, LANES), F32),
+            ((ROWS, LANES), F32),
+        ],
+        half_1, x, enc, hid, keep, d_enc, lines, head_sums, d_dec, d_mask, d_cond, d_line, scalars, wide_enc, bias,
+        jnp.asarray(vector_places(), F32), jnp.asarray(np.pad(encoder, ((0, 0), (0, LANES - KK * 3))), F32),
+    )[0]
+    sums, scalars = pl.pallas_call(
+        total_kernel,
+        out_shape=[jax.ShapeDtypeStruct(block.shape, BF), jax.ShapeDtypeStruct((1, LANES), F32)],
+        in_specs=[VMEM_SPEC],
+        out_specs=[VMEM_SPEC, VMEM_SPEC],
+        compiler_params=pltpu.CompilerParams(vmem_limit_bytes=VMEM_BYTES),
+    )(exchange(block, both))
+    sums = exchange(sums, both)
     rates = learning_rates(w_fc.shape[0] * count)
-    weights = (w_enc, w_lstm, w_fc, w_cond, w_deconv, w_mask, vector)
-    firsts = (m_enc, m_lstm, m_fc, m_cond, m_deconv, m_mask, m_vector)
-    seconds = (v_enc, v_lstm, v_fc, v_cond, v_deconv, v_mask, v_vector)
-    new = [
-        adam(weights[index], grads[index] * factor, firsts[index], seconds[index], rates[index])
-        for index in range(7)
-    ]
-    outs = [loss_sum, valid_count, grad_norm]
+
+    def shown(group):
+        enc, lstm, fc, cond, dec, mask, line = group
+        fc = fc.reshape(2, NK * KK, WB * C // LANES, LANES)
+        fc = jnp.transpose(fc, (1, 2, 0, 3)).reshape(-1, LANES)
+        return [enc.T, lstm, fc, cond, dec, mask.T, line.reshape(1, -1)]
+
+    def back(group):
+        enc, lstm, fc, cond, dec, mask, line = group
+        fc = fc.reshape(NK * KK, WB * C // LANES, 2, LANES)
+        fc = jnp.transpose(fc, (2, 0, 1, 3)).reshape(w_fc.shape)
+        return [enc.T, lstm, fc, cond, dec, mask.T, line.reshape(-1)]
+
+    weights = shown([w_enc, w_lstm, w_fc, w_cond, w_deconv, w_mask, vector])
+    firsts = shown([m_enc, m_lstm, m_fc, m_cond, m_deconv, m_mask, m_vector])
+    seconds = shown([v_enc, v_lstm, v_fc, v_cond, v_deconv, v_mask, v_vector])
+    shapes = [jax.ShapeDtypeStruct(value.shape, F32) for value in weights]
+    any_spec = pl.BlockSpec(memory_space=pl.ANY)
+    places_out = [VMEM_SPEC, any_spec, any_spec] + [VMEM_SPEC] * 4
+    new = pl.pallas_call(
+        functools.partial(update_kernel, rates),
+        out_shape=[jax.ShapeDtypeStruct((), F32)] + shapes * 3,
+        in_specs=[VMEM_SPEC] * 24,
+        out_specs=[SMEM_SPEC] + places_out * 3,
+        scratch_shapes=[
+            pltpu.VMEM((ROWS, LANES), F32), pltpu.VMEM((3,) + shapes[2].shape, F32),
+            pltpu.VMEM((3,) + shapes[1].shape, F32), pltpu.SemaphoreType.DMA((21,)),
+        ],
+        compiler_params=pltpu.CompilerParams(vmem_limit_bytes=VMEM_BYTES),
+    )(sums, scalars, d_fc, *weights, *firsts, *seconds)
+    outs = [scalars[0, 0], scalars[0, 1], new[0]]
     for kind in range(3):
-        outs.extend(new[index][kind] for index in range(7))
+        outs.extend(back(new[1 + 7 * kind : 8 + 7 * kind]))
     return tuple(outs)
 
 

time: 281 us -> 220 us (0.78)
  local copies, waits for them, and re-layouts: 48.4 us -> 13.7 us
  other arithmetic: 36.3 us -> 12.7 us
  blocking collectives: 0 us -> 20.3 us
  starting transfers between devices: 35.5 us -> 26.7 us
  waiting for transfers between devices: 59.3 us -> 52.2 us
  between operations: 4.56 us -> 1.68 us
    unnamed x80 -> x36, local copies, waits for them, and re-layouts: 24.4 us -> 2.04 us
    all_to_all x0 -> x1, blocking collectives: none -> 20.3 us  [exchange(): return lax.all_to_all(block, axes, 0, 0, tiled=True)]
    sub x7 -> x0, other arithmetic: 12.8 us -> none  [adam(): return (weight - rate * (update + DECAY * weight), first, second)]
    all_to_all x9 -> x7, starting transfers between devices: 35.1 us -> 26.2 us  [exchange(): return lax.all_to_all(block, axes, 0, 0, tiled=True)]
    reduce_sum x10 -> x1, other arithmetic: 8.19 us -> 1.26 us  [whole_clips(): fc_squares = jnp.sum(fc_squares) / groups]
    all_to_all x9 -> x7, waiting for transfers between devices: 58.7 us -> 52.2 us  [exchange(): return lax.all_to_all(block, axes, 0, 0, tiled=True)]
    convert_element_type x9 -> x1, other arithmetic: 6.08 us -> 0.01 us  [whole_clips(): d_logit.astype(BF)]
    convert_element_type x3 -> x0, local copies, waits for them, and re-layouts: 4.27 us -> none  [the longest x1 2.15 us: whole_clips(): to_all(got.astype(BF), both)[:, :each].reshape(devices * each, LANES)]
  transfers between devices with their start and end apart: 11 -> 9, of which waited for: 9 -> 6; matrix products, arithmetic and copies ran while one was open for 13% -> 5% of each run, Pallas kernels for 9% -> 7%
where the time goes in v3:
time: 220 us; the launch traced here: 219 us
  Pallas kernels  84.9 us (39%)
  waiting for transfers between devices  52.2 us (24%)
  starting transfers between devices  26.7 us (12%)
  blocking collectives  20.3 us (9%)
  local copies, waits for them, and re-layouts  13.7 us (6%)
  other arithmetic  12.7 us (6%)
  matrix products  6.39 us (3%)
    pallas_call x4, Pallas kernels, call(): pl.pallas_call(kernel, cost_estimate=cost(micros), out_shape=[jax.ShapeDt...  68.8 us
    all_to_all x7, waiting for transfers between devices, exchange(): return lax.all_to_all(block, axes, 0, 0, tiled=True)  52.2 us
    all_to_all x7, starting transfers between devices, exchange(): return lax.all_to_all(block, axes, 0, 0, tiled=True)  26.2 us
    all_to_all x1, blocking collectives, exchange(): return lax.all_to_all(block, axes, 0, 0, tiled=True)  20.3 us
    pallas_call x1, Pallas kernels, whole_clips(): pl.pallas_call(functools.partial(update_kernel, rates), out_shape=[jax.Sh...  10.5 us
  transfers between devices with their start and end apart: 9, of which 6 were waited for; matrix products, arithmetic and copies ran while one was open for 5% of the time, Pallas kernels for 7%

profile of v3, /device:TPU:0, one launch (start us, length us, event | category | flops | bytes accessed | tf_op | source)
XLA Modules:
  0.0 218.6 jit_solution(13599449649925962222)
XLA Ops:
  0.7 1.1 copy.69
  1.8 0.9 convert_element_type.47
  2.8 0.5 maximum_bitcast_fusion
  3.3 0.1 reshape.149
  3.5 0.8 broadcast_in_dim.10
  4.2 6.3 %all-to-all-start = ((bf16[8,144,128]{2,1,0:T(8,128)(2,1)}), bf16[8,144,128]{2,1,0:T(8,128)(2,1)S(1)}, u32[]{:S(2)}, u32[]{:S(2)}) async-start(bf16[8,144,128]{2,1,0:T(8,128)(2,1)} %bitcast.4), calls=%async_computation | async-start | bytes 589824 | tf_op jit(solution)/shard_map/all_to_all | solution.py:1069
  10.8 0.8 fusion.1.we_ref
  11.5 9.4 %all-to-all-done.raw_ref = bf16[8,144,128]{2,1,0:T(8,128)(2,1)S(1)} async-done(((bf16[8,144,128]{2,1,0:T(8,128)(2,1)}), bf16[8,144,128]{2,1,0:T(8,128)(2,1)S(1)}, u32[]{:S(2)}, u32[]{:S(2)}) %all-to-all-start) | async-done | bytes 294944 | tf_op jit(solution)/shard_map/all_to_all | solution.py:1069
  21.0 0.8 broadcast_in_dim.11.bias_ref
  21.8 24.2 %shard_map.496 = (bf16[17,4,16,128]{3,2,1,0:T(8,128)(2,1)}, bf16[16,4,32,128]{3,2,1,0:T(8,128)(2,1)}, bf16[16,4,32,128]{3,2,1,0:T(8,128)(2,1)}, f32[16,4,128,128...) custom-call(s32[1]{0:T(128)} %bitcast.half_ref, bf16[8,144,128]{2,1,0:T(8,128)(2,1)} %copy-done.5, ...), custom_call_target="tpu_custom_call" | custom-call | flops 16000000000 | bytes 1024 | tf_op jit(solution)/shard_map/pallas_call | solution.py:1053
  46.0 3.6 %all-to-all-start.1 = ((bf16[8,8,16,128]{3,2,1,0:T(8,128)(2,1)}), bf16[8,8,16,128]{3,2,1,0:T(8,128)(2,1)S(1)}, u32[]{:S(2)}, u32[]{:S(2)}) async-start(bf16[8,8,16,128]{3,2,1,0:T(8,128)(2,1)} %get-tuple-element.71), calls=%async_computation.1 | async-start | bytes 524288 | tf_op jit(solution)/shard_map/all_to_all | solution.py:1069
  49.5 0.7 convert_element_type.52
  50.3 0.1 copy.74
  50.4 0.1 copy.73
  50.6 8.6 %all-to-all-done.1 = bf16[8,8,16,128]{3,2,1,0:T(8,128)(2,1)S(1)} async-done(((bf16[8,8,16,128]{3,2,1,0:T(8,128)(2,1)}), bf16[8,8,16,128]{3,2,1,0:T(8,128)(2,1)S(1)}, u32[]{:S(2)}, u32[]{:S(2)}) %all-to-all-start.1) | async-done | bytes 262176 | tf_op jit(solution)/shard_map/all_to_all | solution.py:1069
  59.3 2.0 fusion
  61.3 1.1 convolution_bitcast_fusion
  62.4 3.4 %all-to-all-start.2 = ((f32[8,8,250]{2,1,0:T(8,128)}), f32[8,8,250]{2,1,0:T(8,128)S(1)}, u32[]{:S(2)}, u32[]{:S(2)}) async-start(f32[8,8,250]{2,1,0:T(8,128)} %convolution_bitcast_fusion), calls=%async_computation.2 | async-start | bytes 131072 | tf_op jit(solution)/shard_map/all_to_all | solution.py:1069
  65.9 5.7 %all-to-all-done.2 = f32[8,8,250]{2,1,0:T(8,128)S(1)} async-done(((f32[8,8,250]{2,1,0:T(8,128)}), f32[8,8,250]{2,1,0:T(8,128)S(1)}, u32[]{:S(2)}, u32[]{:S(2)}) %all-to-all-start.2) | async-done | bytes 64032 | tf_op jit(solution)/shard_map/all_to_all | solution.py:1069
  71.7 0.2 fusion.2
  71.9 0.1 reshape.153
  72.0 0.6 pad.31.logit_ref
  72.6 16.4 %shard_map.497 = (bf16[8,4,32,128]{3,2,1,0:T(8,128)(2,1)}, f32[8,16,32]{2,1,0:T(8,128)}, f32[32,128]{1,0:T(8,128)}, f32[16,128]{1,0:T(8,128)}, f32[200,128]{1,0:T(8,128)}) custom-call(s32[1]{0:T(128)} %bitcast.half_ref, bf16[17,4,16,128]{3,2,1,0:T(8,128)(2,1)} %get-tuple-element.66.x_ref, bf16[16,4,32,128]{3,2,1,0:T(8,128)(2,1)} %get-tuple-element.68.hid_ref, ...), custom_call_target="tpu_custom_call" | custom-call | flops 24000000000 | bytes 1024 | tf_op jit(solution)/shard_map/pallas_call | solution.py:1053
  89.0 1.0 slice.39
  90.0 0.1 reshape.154
  90.1 0.7 broadcast_in_dim.13
  90.8 3.3 %all-to-all-start.3 = ((bf16[32,8,250]{2,1,0:T(8,128)(2,1)}), bf16[32,8,250]{2,1,0:T(8,128)(2,1)}, u32[]{:S(2)}, u32[]{:S(2)}) async-start(bf16[32,8,250]{2,1,0:T(8,128)(2,1)} %broadcast_in_dim.13), calls=%async_computation.3 | async-start | bytes 262144 | tf_op jit(solution)/shard_map/all_to_all | solution.py:1069
  94.1 8.1 %all-to-all-done.3 = bf16[32,8,250]{2,1,0:T(8,128)(2,1)} async-done(((bf16[32,8,250]{2,1,0:T(8,128)(2,1)}), bf16[32,8,250]{2,1,0:T(8,128)(2,1)}, u32[]{:S(2)}, u32[]{:S(2)}) %all-to-all-start.3) | async-done | bytes 128032 | tf_op jit(solution)/shard_map/all_to_all | solution.py:1069
  102.2 1.2 convolution_convert_fusion.2
  103.4 0.3 copy.76
  103.7 0.1 reshape.156
  103.8 0.8 convolution_convert_fusion
  104.7 0.8 reshape.157
  105.5 3.4 %all-to-all-start.4 = ((bf16[8,8,16,128]{3,2,1,0:T(8,128)(2,1)}), bf16[8,8,16,128]{3,2,1,0:T(8,128)(2,1)S(1)}, u32[]{:S(2)}, u32[]{:S(2)}) async-start(bf16[8,8,16,128]{3,2,1,0:T(8,128)(2,1)} %reshape.157), calls=%async_computation.4 | async-start | bytes 524288 | tf_op jit(solution)/shard_map/all_to_all | solution.py:1069
  108.9 0.7 convert_reduce_fusion
  109.6 0.4 collective-permute-start
  110.0 0.3 fusion.14
  110.2 0.7 pad.33.dline_ref
  111.0 0.6 pad_maximum_fusion.2.dcond_ref
  111.6 7.0 %all-to-all-done.4 = bf16[8,8,16,128]{3,2,1,0:T(8,128)(2,1)S(1)} async-done(((bf16[8,8,16,128]{3,2,1,0:T(8,128)(2,1)}), bf16[8,8,16,128]{3,2,1,0:T(8,128)(2,1)S(1)}, u32[]{:S(2)}, u32[]{:S(2)}) %all-to-all-start.4) | async-done | bytes 262176 | tf_op jit(solution)/shard_map/all_to_all | solution.py:1069
  118.6 1.1 broadcast_in_dim.14
  119.7 3.7 %all-to-all-start.5 = ((bf16[4,2,64,1024]{3,2,1,0:T(8,128)(2,1)}), bf16[4,2,64,1024]{3,2,1,0:T(8,128)(2,1)S(1)}, u32[]{:S(2)}, u32[]{:S(2)}) async-start(bf16[4,2,64,1024]{3,2,1,0:T(8,128)(2,1)} %broadcast_in_dim.14), calls=%async_computation.5 | async-start | bytes 2097152 | tf_op jit(solution)/shard_map/all_to_all | solution.py:1069
  123.5 1.0 select_bitcast_fusion.3
  124.5 0.8 pad_maximum_fusion.dec_ref
  125.4 0.8 pad_maximum_fusion.1.fc_ref
  126.2 16.2 %shard_map.498 = (bf16[8,4,128,128]{3,2,1,0:T(8,128)(2,1)}, f32[8,4,32,128]{3,2,1,0:T(8,128)}, f32[128,128]{1,0:T(8,128)}) custom-call(s32[1]{0:T(128)} %bitcast.half_ref, f32[16,4,128,128]{3,2,1,0:T(8,128)} %get-tuple-element.69.act_ref, f32[16,4,32,128]{3,2,1,0:T(8,128)} %get-tuple-element.70.cell_ref, ...), custom_call_target="tpu_custom_call" | custom-call | flops 12800000000 | bytes 1024 | tf_op jit(solution)/shard_map/pallas_call | solution.py:1053
  142.5 1.0 copy-done.3
  143.4 3.7 %shard_map.499 = (f32[4000,128]{1,0:T(8,128)}, f32[1,128]{1,0:T(1,128)}) custom-call(bf16[4,2,64,1024]{3,2,1,0:T(8,128)(2,1)} %copy-done.3, bf16[4,64,250]{2,1,0:T(8,128)(2,1)} %bitcast.16.sum_ref), custom_call_target="tpu_custom_call" | custom-call | flops 1600000000 | bytes 1024 | tf_op jit(solution)/shard_map/pallas_call | solution.py:1192
  147.1 1.3 reduce_sum.29
  149.0 1.2 fusion.13.scalar_ref
  150.3 12.0 %shard_map.500 = bf16[32,64,128]{2,1,0:T(8,128)(2,1)} custom-call(s32[1]{0:T(128)} %bitcast.half_ref, bf16[17,4,16,128]{3,2,1,0:T(8,128)(2,1)} %get-tuple-element.66.x_ref, bf16[16,4,32,128]{3,2,1,0:T(8,128)(2,1)} %get-tuple-element.67.enc_ref, bf16[16,4,32,128]{3,2,1,0:T(8,128)(2,1)} %get-tuple-element.68.hid_ref, ...), custom_call_target="tpu_custom_call" | custom-call | flops 9600000000 | bytes 1024 | tf_op jit(solution)/shard_map/pallas_call | solution.py:1053
  162.3 20.3 %all_to_all.40.got_ref = bf16[32,64,128]{2,1,0:T(8,128)(2,1)} all-to-all(bf16[32,64,128]{2,1,0:T(8,128)(2,1)} %shard_map.500), channel_id=1, replica_groups=mesh['clip'=4,'row'=8] {'clip','row'}, dimensions={0} | all-to-all | bytes 1048576 | tf_op jit(solution)/shard_map/all_to_all | solution.py:1069
  182.5 2.0 shard_map.501
  184.5 2.6 %all-to-all-start.7 = ((bf16[32,64,128]{2,1,0:T(8,128)(2,1)}), bf16[32,64,128]{2,1,0:T(8,128)(2,1)S(1)}, u32[]{:S(2)}, u32[]{:S(2)}) async-start(bf16[32,64,128]{2,1,0:T(8,128)(2,1)} %get-tuple-element.84), calls=%async_computation.7 | async-start | bytes 1048576 | tf_op jit(solution)/shard_map/all_to_all | solution.py:1069
  187.1 0.6 reshape.161.refs_6_
  187.7 0.6 reshape.164.refs_13_
  188.3 0.6 reshape.167.refs_20_
  188.8 1.3 fusion.18
  190.2 13.3 %all-to-all-done.7.got_ref = bf16[32,64,128]{2,1,0:T(8,128)(2,1)S(1)} async-done(((bf16[32,64,128]{2,1,0:T(8,128)(2,1)}), bf16[32,64,128]{2,1,0:T(8,128)(2,1)S(1)}, u32[]{:S(2)}, u32[]{:S(2)}) %all-to-all-start.7) | async-done | bytes 524320 | tf_op jit(solution)/shard_map/all_to_all | solution.py:1069
  203.4 0.8 copy-done.2
  204.2 10.5 %shard_map.502 = (f32[]{:T(128)}, f32[32,75]{1,0:T(8,128)}, f32[1600,128]{1,0:T(8,128)}, f32[4000,128]{1,0:T(8,128)}, f32[15,250]{1,0:T(8,128)}, /*index=5*/f32[...) custom-call(bf16[32,64,128]{2,1,0:T(8,128)(2,1)} %copy-done.2, ...), custom_call_target="tpu_custom_call" | custom-call | tf_op jit(solution)/shard_map/pallas_call | solution.py:1252
  214.7 1.3 reduce
  216.0 1.3 reduce.1
  217.3 1.3 reduce.2
  (55 shorter events, 0.9 us)
Async XLA Ops:
  0.7 10.1 %copy-start.8 = (bf16[144,75]{1,0:T(8,128)(2,1)S(1)}, bf16[144,75]{1,0:T(8,128)(2,1)}, u32[]{:S(2)}) copy-start(bf16[144,75]{1,0:T(8,128)(2,1)} %constant.67.clone) | copy-start | bytes 64804
  0.7 9.9 %copy-start.9 = (f32[517]{0:T(1024)S(1)}, f32[517]{0:T(1024)}, u32[]{:S(2)}) copy-start(f32[517]{0:T(1024)} %param.45) | copy-start | bytes 6208
  0.7 10.0 %slice-start = ((f32[517]{0:T(1024)}), f32[224]{0:T(256)S(1)}, s32[]{:S(2)}) async-start(f32[517]{0:T(1024)} %param.45), calls=%async_computation.8 | async-start | bytes 2048 | tf_op jit(solution)/shard_map/slice | solution.py:1111
  0.7 10.1 %copy-start.6 = (f32[75,32]{0,1:T(8,128)S(1)}, f32[75,32]{0,1:T(8,128)}, u32[]{:S(2)}) copy-start(f32[75,32]{0,1:T(8,128)} %param.39) | copy-start | bytes 28804
  4.2 16.8 %all-to-all-start = ((bf16[8,144,128]{2,1,0:T(8,128)(2,1)}), bf16[8,144,128]{2,1,0:T(8,128)(2,1)S(1)}, u32[]{:S(2)}, u32[]{:S(2)}) async-start(bf16[8,144,128]{2,1,0:T(8,128)(2,1)} %bitcast.4), calls=%async_computation | async-start | bytes 589824 | tf_op jit(solution)/shard_map/all_to_all | solution.py:1069
  21.0 0.8 copy-start.5
  21.8 27.8 %copy-start = (f32[2,250,1024]{2,0,1:T(2,128)S(1)}, f32[2,250,1024]{2,0,1:T(2,128)}, u32[]{:S(2)}) copy-start(f32[2,250,1024]{2,0,1:T(2,128)} %param.41) | copy-start | bytes 6144004
  46.0 4.3 %copy-start.13 = (s32[4,16,2]{1,2,0:T(2,128)S(1)}, s32[4,16,2]{1,2,0:T(2,128)}, u32[]{:S(2)}) copy-start(s32[4,16,2]{1,2,0:T(2,128)} %param.35) | copy-start | bytes 1540
  46.0 4.3 %copy-start.12 = (f32[4,16,3]{1,0,2:T(4,128)S(1)}, f32[4,16,3]{1,0,2:T(4,128)}, u32[]{:S(2)}) copy-start(f32[4,16,3]{1,0,2:T(4,128)} %param.37) | copy-start | bytes 2308
  46.0 4.4 %copy-start.11 = (f32[4,16,4]{1,2,0:T(4,128)S(1)}, f32[4,16,4]{1,2,0:T(4,128)}, u32[]{:S(2)}) copy-start(f32[4,16,4]{1,2,0:T(4,128)} %param.36) | copy-start | bytes 3076
  46.0 13.2 %all-to-all-start.1 = ((bf16[8,8,16,128]{3,2,1,0:T(8,128)(2,1)}), bf16[8,8,16,128]{3,2,1,0:T(8,128)(2,1)S(1)}, u32[]{:S(2)}, u32[]{:S(2)}) async-start(bf16[8,8,16,128]{3,2,1,0:T(8,128)(2,1)} %get-tuple-element.71), calls=%async_computation.1 | async-start | bytes 524288 | tf_op jit(solution)/shard_map/all_to_all | solution.py:1069
  59.3 12.4 %copy-start.16 = (f32[4,8]{1,0:T(4,128)S(1)}, f32[4,8]{1,0:T(4,128)}, u32[]{:S(2)}) copy-start(f32[4,8]{1,0:T(4,128)} %param.38) | copy-start | bytes 388
  59.3 12.4 %copy-start.7 = (f32[15,250]{1,0:T(8,128)S(1)}, f32[15,250]{1,0:T(8,128)}, u32[]{:S(2)}) copy-start(f32[15,250]{1,0:T(8,128)} %refs_3_.1) | copy-start | bytes 45004
  62.4 9.2 %all-to-all-start.2 = ((f32[8,8,250]{2,1,0:T(8,128)}), f32[8,8,250]{2,1,0:T(8,128)S(1)}, u32[]{:S(2)}, u32[]{:S(2)}) async-start(f32[8,8,250]{2,1,0:T(8,128)} %convolution_bitcast_fusion), calls=%async_computation.2 | async-start | bytes 131072 | tf_op jit(solution)/shard_map/all_to_all | solution.py:1069
  89.0 14.8 %copy-start.1 = (bf16[1024,1024]{1,0:T(8,128)(2,1)S(1)}, bf16[1024,1024]{1,0:T(8,128)(2,1)}, u32[]{:S(2)}) copy-start(bf16[1024,1024]{1,0:T(8,128)(2,1)} %constant.68.clone) | copy-start | bytes 6291460
  90.8 11.5 %all-to-all-start.3 = ((bf16[32,8,250]{2,1,0:T(8,128)(2,1)}), bf16[32,8,250]{2,1,0:T(8,128)(2,1)}, u32[]{:S(2)}, u32[]{:S(2)}) async-start(bf16[32,8,250]{2,1,0:T(8,128)(2,1)} %broadcast_in_dim.13), calls=%async_computation.3 | async-start | bytes 262144 | tf_op jit(solution)/shard_map/all_to_all | solution.py:1069
  103.7 5.2 %copy-start.4 = (s32[4,16,4,64]{3,2,1,0:T(4,128)S(1)}, s32[4,16,4,64]{3,2,1,0:T(4,128)}, u32[]{:S(2)}) copy-start(s32[4,16,4,64]{3,2,1,0:T(4,128)} %param.34) | copy-start | bytes 196612
  105.5 13.1 %all-to-all-start.4 = ((bf16[8,8,16,128]{3,2,1,0:T(8,128)(2,1)}), bf16[8,8,16,128]{3,2,1,0:T(8,128)(2,1)S(1)}, u32[]{:S(2)}, u32[]{:S(2)}) async-start(bf16[8,8,16,128]{3,2,1,0:T(8,128)(2,1)} %reshape.157), calls=%async_computation.4 | async-start | bytes 524288 | tf_op jit(solution)/shard_map/all_to_all | solution.py:1069
  109.6 13.9 %collective-permute-start = (bf16[8,4,32,128]{3,2,1,0:T(8,128)(2,1)}, bf16[8,4,32,128]{3,2,1,0:T(8,128)(2,1)S(1)}, u32[]{:S(2)}, u32[]{:S(2)}) collective-permute-start(bf16[8,4,32,128]{3,2,1,0:T(8,128)(2,1)} %get-tuple-element.72), channel_id=1, source_target_pairs={{0,1},{1,0},{2,3},{3,2},{4,5},{5,4},{6,7},{7,6},{8,9},{9,8},{10,11... | collective-permute-start | bytes 786440 | tf_op jit(solution)/shard_map/ppermute | solution.py:1176
  119.7 22.8 %all-to-all-start.5 = ((bf16[4,2,64,1024]{3,2,1,0:T(8,128)(2,1)}), bf16[4,2,64,1024]{3,2,1,0:T(8,128)(2,1)S(1)}, u32[]{:S(2)}, u32[]{:S(2)}) async-start(bf16[4,2,64,1024]{3,2,1,0:T(8,128)(2,1)} %broadcast_in_dim.14), calls=%async_computation.5 | async-start | bytes 2097152 | tf_op jit(solution)/shard_map/all_to_all | solution.py:1069
  123.4 1.9 collective-permute-start.1
  142.5 1.0 copy-start.3
  162.2 24.8 %copy-start.10 = (f32[517]{0:T(1024)S(1)}, f32[517]{0:T(1024)}, u32[]{:S(2)}) copy-start(f32[517]{0:T(1024)} %param.45) | copy-start | bytes 6208
  162.2 25.4 %copy-start.14 = (f32[517]{0:T(1024)S(1)}, f32[517]{0:T(1024)}, u32[]{:S(2)}) copy-start(f32[517]{0:T(1024)} %param.52) | copy-start | bytes 6208
  162.3 26.0 %copy-start.15 = (f32[517]{0:T(1024)S(1)}, f32[517]{0:T(1024)}, u32[]{:S(2)}) copy-start(f32[517]{0:T(1024)} %param.59) | copy-start | bytes 6208
  184.5 19.0 %all-to-all-start.7 = ((bf16[32,64,128]{2,1,0:T(8,128)(2,1)}), bf16[32,64,128]{2,1,0:T(8,128)(2,1)S(1)}, u32[]{:S(2)}, u32[]{:S(2)}) async-start(bf16[32,64,128]{2,1,0:T(8,128)(2,1)} %get-tuple-element.84), calls=%async_computation.7 | async-start | bytes 1048576 | tf_op jit(solution)/shard_map/all_to_all | solution.py:1069
  203.4 0.8 copy-start.2

commit v4 on v3

--- a/solution.py
+++ b/solution.py
@@ -536,9 +536,9 @@
 def forward_kernel(
     half_ref, raw_ref, we_ref, w_ref, bias_ref,
     x_ref, enc_ref, hid_ref, act_ref, cell_ref, strip_ref,
-    win_s, enc_s, hid_s, state_s, rows_s, wx_s, wh_s,
+    win_s, enc_s, hid_s, state_s, rows_s, wx_s, wh_s, even_s, odd_s,
 ):
-    steps = enc_ref.shape[0]
+    steps = hid_ref.shape[0]
     lanes = lane_places()
     for kind, target in ((0, wx_s), (1, wh_s)):
         for tap in range(KK):
@@ -547,7 +547,7 @@
         target[...] = nt(one_hot_eye(4 * C), rows_s[...]).astype(BF)
     unpack_images(raw_ref, x_ref)
 
-    def encode(t, _):
+    def encode(t, gates_s):
         spread(image_tiles(x_ref, t), lanes, 1, win_s, 16, 0)
         tiles = []
         for two in range(0, TILES, 2):
@@ -564,38 +564,42 @@
         for two in range(0, TILES, 2):
             gates = nn(wx_s[...], stacked(enc_s, two, KS)) + twice(bias_ref[3 * C : 7 * C])
             for one in range(2):
-                act_ref[t, two + one] = gates[:, one * LANES : (one + 1) * LANES]
-        return 0
-
-    lax.fori_loop(0, steps, encode, 0)
+                gates_s[two + one] = gates[:, one * LANES : (one + 1) * LANES]
+
     hid_s[...] = jnp.zeros_like(hid_s)
     state_s[...] = jnp.zeros_like(state_s)
 
-    def advance(t, _):
+    def advance(t, gates_s, later_s):
+        sums = [nn(wh_s[...], stacked(hid_s, two, KS)) for two in range(0, TILES, 2)]
+        encode(t + 1, later_s)
         hidden = []
-        for two in range(0, TILES, 2):
-            sums = nn(wh_s[...], stacked(hid_s, two, KS))
-            for one in range(2):
-                tile = two + one
-                gates = act_ref[t, tile] + sums[:, one * LANES : (one + 1) * LANES]
-                gate_in = logistic(gates[0:C])
-                gate_keep = logistic(gates[C : 2 * C] + 1.0)
-                gate_out = logistic(gates[2 * C : 3 * C])
-                gate_new = jnp.tanh(gates[3 * C : 4 * C])
-                cell = gate_keep * state_s[tile] + gate_in * gate_new
-                act_ref[t, tile, 0:C] = gate_in
-                act_ref[t, tile, C : 2 * C] = gate_keep
-                act_ref[t, tile, 2 * C : 3 * C] = gate_out
-                act_ref[t, tile, 3 * C : 4 * C] = gate_new
-                state_s[tile] = cell
-                cell_ref[t, tile] = cell
-                low = (gate_out * jnp.tanh(cell)).astype(BF)
-                hid_ref[t, tile] = low
-                hidden.append(low.astype(F32))
+        for tile in range(TILES):
+            start = tile % 2 * LANES
+            gates = gates_s[tile] + sums[tile // 2][:, start : start + LANES]
+            gate_in = logistic(gates[0:C])
+            gate_keep = logistic(gates[C : 2 * C] + 1.0)
+            gate_out = logistic(gates[2 * C : 3 * C])
+            gate_new = jnp.tanh(gates[3 * C : 4 * C])
+            cell = gate_keep * state_s[tile] + gate_in * gate_new
+            act_ref[t, tile, 0:C] = gate_in
+            act_ref[t, tile, C : 2 * C] = gate_keep
+            act_ref[t, tile, 2 * C : 3 * C] = gate_out
+            act_ref[t, tile, 3 * C : 4 * C] = gate_new
+            state_s[tile] = cell
+            cell_ref[t, tile] = cell
+            low = (gate_out * jnp.tanh(cell)).astype(BF)
+            hid_ref[t, tile] = low
+            hidden.append(low.astype(F32))
         spread(hidden, lanes, 2, hid_s, C, 0)
+
+    encode(0, even_s)
+
+    def advance_two(pair, _):
+        advance(2 * pair, even_s, odd_s)
+        advance(2 * pair + 1, odd_s, even_s)
         return 0
 
-    lax.fori_loop(0, steps, advance, 0)
+    lax.fori_loop(0, steps // 2, advance_two, 0)
     own = steps // HALVES
     base = half_ref[0] * own
 
@@ -617,7 +621,8 @@
 def head_kernel(
     half_ref, x_ref, hid_ref, logit_ref, w_ref, mask_ref, bias_ref, place_ref, placet_ref,
     back_ref, dlog_ref, dwd_ref, dwm_ref, sums_ref,
-    win_s, wd_ref, wdt_ref, wm_ref, wmt_ref, over_ref, wide_s, everywhere_s, turned_s, d_mix_s, d_spot_s, kernel_s,
+    even_s, odd_s, wd_ref, wdt_ref, wm_ref, wmt_ref, over_ref, wide_s, everywhere_s, turned_s, d_even_s, d_odd_s,
+    d_spot_s, kernel_s,
 ):
     wd_ref[...] = w_ref[...].astype(BF)
     wdt_ref[...] = nt(one_hot_eye(4 * C), wd_ref[...]).astype(BF)
@@ -657,7 +662,7 @@
     row = lax.broadcasted_iota(jnp.int32, (64, 4 * WIN), 0) // 16
     own_turned = row == lax.broadcasted_iota(jnp.int32, (64, 4 * WIN), 1) // WIN
 
-    def frame(i, _):
+    def frame(i, win_s, d_mix_s):
         t = base + i
         spread(image_tiles(x_ref, t), lanes, 1, win_s, 16, 0)
         window = jnp.concatenate([win_s[tile : tile + 3].reshape(WIN, LANES) for tile in range(TILES)], axis=1)
@@ -715,9 +720,13 @@
         back = nn(wd_ref[...], d_upper_low).astype(BF)
         for tile in range(TILES):
             back_ref[i, tile] = back[:, tile * LANES : (tile + 1) * LANES]
+
+    def two_frames(pair, _):
+        frame(2 * pair, even_s, d_even_s)
+        frame(2 * pair + 1, odd_s, d_odd_s)
         return 0
 
-    lax.fori_loop(0, own, frame, 0)
+    lax.fori_loop(0, own // 2, two_frames, 0)
     d_kernels = None
     for sub in range(4):
         rows = jnp.concatenate([d_spot_s[i, sub * 16 : sub * 16 + 16] for i in range(own)], axis=0)
@@ -738,9 +747,9 @@
 
 
 def backward_kernel(
-    half_ref, act_ref, cell_ref, dec_ref, fc_ref, w_ref,
+    half_ref, act_ref, cell_ref, dec_ref, other_dec_ref, fc_ref, other_fc_ref, w_ref,
     keep_ref, denc_ref, lines_ref,
-    gate_s, back_s, state_s, wb_s,
+    gate_s, back_s, state_s, wb_s, even_s, odd_s,
 ):
     for tap in range(KK):
         place = tap % KS * 2 * C
@@ -754,53 +763,69 @@
     state_s[...] = jnp.zeros_like(state_s)
     lines_ref[...] = jnp.zeros_like(lines_ref)
 
-    def retreat(step, _):
-        t = steps - 1 - step
+    def prepare(t, factor_s):
         half = t // own
         inside = t % own
         mine = half == half_ref[0]
-        counted = jnp.where(mine, 1.0, 0.0)
         earlier = jnp.maximum(t - 1, 0)
         started = jnp.where(t > 0, 1.0, 0.0)
-        tiles = []
         for tile in range(TILES):
             pair = tile // 2
             low_row = tile % 2
             parts = [
-                fc_ref[half, 2 * band + pair, inside].astype(F32)[8 * low_row : 8 * low_row + 8]
+                jnp.where(
+                    mine, fc_ref[2 * band + pair, inside].astype(F32), other_fc_ref[2 * band + pair, inside].astype(F32)
+                )[8 * low_row : 8 * low_row + 8]
                 for band in range(BANDS)
             ]
             from_fc = jnp.concatenate(block_swap(parts, lanes[1]), axis=0)
-            back = back_s[tile] + from_fc + dec_ref[half, inside, tile].astype(F32)
+            from_dec = jnp.where(
+                mine, dec_ref[inside, tile].astype(F32), other_dec_ref[inside, tile].astype(F32)
+            )
             gate_in = act_ref[t, tile, 0:C]
             gate_keep = act_ref[t, tile, C : 2 * C]
             gate_out = act_ref[t, tile, 2 * C : 3 * C]
             gate_new = act_ref[t, tile, 3 * C : 4 * C]
             bent = jnp.tanh(cell_ref[t, tile])
-            d_cell = state_s[tile] + back * gate_out * (1.0 - bent * bent)
-            state_s[tile] = d_cell * gate_keep
+            factors = [
+                from_fc + from_dec,
+                gate_out * (1.0 - bent * bent),
+                gate_keep,
+                gate_new * gate_in * (1.0 - gate_in),
+                (cell_ref[earlier, tile] * started) * gate_keep * (1.0 - gate_keep),
+                bent * gate_out * (1.0 - gate_out),
+                gate_in * (1.0 - gate_new * gate_new),
+            ]
+            for index, factor in enumerate(factors):
+                factor_s[tile, index * C : (index + 1) * C] = factor
+
+    def retreat(t, factor_s, next_s):
+        half = t // own
+        inside = t % own
+        counted = jnp.where(half == half_ref[0], 1.0, 0.0)
+        place = jnp.where(half == half_ref[0], inside, own)
+        tiles = []
+        for tile in range(TILES):
+            back = back_s[tile] + factor_s[tile, 0:C]
+            d_cell = state_s[tile] + back * factor_s[tile, C : 2 * C]
+            state_s[tile] = d_cell * factor_s[tile, 2 * C : 3 * C]
             d_gates = jnp.concatenate(
                 [
-                    d_cell * gate_new * gate_in * (1.0 - gate_in),
-                    d_cell * (cell_ref[earlier, tile] * started) * gate_keep * (1.0 - gate_keep),
-                    back * bent * gate_out * (1.0 - gate_out),
-                    d_cell * gate_in * (1.0 - gate_new * gate_new),
+                    d_cell * factor_s[tile, 3 * C : 4 * C],
+                    d_cell * factor_s[tile, 4 * C : 5 * C],
+                    back * factor_s[tile, 5 * C : 6 * C],
+                    d_cell * factor_s[tile, 6 * C : 7 * C],
                 ],
                 axis=0,
             )
             lines_ref[...] += d_gates * counted
-            tiles.append(d_gates.astype(BF))
-
-        @pl.when(mine)
-        def _():
-            for tile in range(TILES):
-                keep_ref[inside, tile] = tiles[tile]
-
-        wide = [tile.astype(F32) for tile in tiles]
+            low = d_gates.astype(BF)
+            keep_ref[place, tile] = low
+            tiles.append(low.astype(F32))
         for index in range(TILES + 4):
             tile = index - 2
-            gate_s[index] = moved(wide[tile % TILES], lanes, 0, tile // TILES).astype(BF)
-        d_enc = []
+            gate_s[index] = moved(tiles[tile % TILES], lanes, 0, tile // TILES).astype(BF)
+        prepare(jnp.maximum(t - 1, 0), next_s)
         for two in range(0, TILES, 2):
             sums = nn(wb_s[...], stacked(gate_s, two, KS))
             for one in range(2):
@@ -809,17 +834,17 @@
                 for shift in range(KS):
                     value = moved(part[shift * 2 * C : (shift + 1) * 2 * C], lanes, 2 - shift, 0)
                     total = value if total is None else total + value
-                d_enc.append(total[:C])
+                denc_ref[place, two + one] = total[:C]
                 back_s[two + one] = total[C:]
 
-        @pl.when(mine)
-        def _():
-            for tile in range(TILES):
-                denc_ref[inside, tile] = d_enc[tile]
-
+    prepare(steps - 1, even_s)
+
+    def retreat_two(pair, _):
+        retreat(steps - 1 - 2 * pair, even_s, odd_s)
+        retreat(steps - 2 - 2 * pair, odd_s, even_s)
         return 0
 
-    lax.fori_loop(0, steps, retreat, 0)
+    lax.fori_loop(0, steps // 2, retreat_two, 0)
 
 
 ROW_DEC = KK * 2 * C
@@ -846,11 +871,11 @@
 
 def pack_kernel(
     half_ref, x_ref, enc_ref, hid_ref, keep_ref, denc_ref, lines_ref, head_ref, ddec_ref, dmask_ref, dcond_ref,
-    dline_ref, scalar_ref, we_ref, bias_ref, place_ref, encoder_ref,
+    dline_ref, count_ref, squares_ref, we_ref, bias_ref, place_ref, encoder_ref,
     block_ref,
     win_s, join_s, dwe_s, sums_s, packed_s,
 ):
-    own = keep_ref.shape[0]
+    own = keep_ref.shape[0] - 1
     base = half_ref[0] * own
     lanes = lane_places()
     dwe_s[...] = jnp.zeros_like(dwe_s)
@@ -865,10 +890,11 @@
         spread(
             [hid_ref[earlier, tile].astype(F32) * started for tile in range(TILES)], lanes, 2, join_s, 2 * C, C
         )
+        d_gates = jnp.concatenate([keep_ref[i, tile] for tile in range(TILES)], axis=1)
+        joined = jnp.concatenate([stacked(join_s, 0, KS), stacked(join_s, 2, KS)], axis=1)
+        packed_s[0:ROW_DEC] += nt(joined, d_gates)
         spread(image_tiles(x_ref, t), lanes, 1, win_s, 16, 0)
         for two in range(0, TILES, 2):
-            d_gates = jnp.concatenate([keep_ref[i, two], keep_ref[i, two + 1]], axis=1)
-            packed_s[0:ROW_DEC] += nt(stacked(join_s, two, KS), d_gates)
             window = stacked(win_s, two, 3)
             pre = nn(we_ref[...], window) + twice(bias_ref[0:C])
             centered = pre - jnp.mean(pre, 0, keepdims=True)
@@ -906,7 +932,7 @@
     )
     lost = jnp.sum(jnp.sum(head_ref[192:196], 0, keepdims=True), 1, keepdims=True)
     lane = lax.broadcasted_iota(jnp.int32, (1, LANES), 1)
-    value = jnp.where(lane == 0, lost, scalar_ref[...])
+    value = jnp.where(lane == 0, lost, jnp.where(lane == 1, count_ref[...], jnp.where(lane == 2, squares_ref[...], 0.0)))
     terms = []
     for _ in range(3):
         low = value.astype(BF).astype(F32)
@@ -957,15 +983,17 @@
                 part = grad[:, one * LANES : (one + 1) * LANES]
                 squares = squares + jnp.sum(part * part, 0, keepdims=True)
                 out_ref[pl.ds((start // LANES + one) * 2 + row, logits, stride=stride), :] = part
-    squares_ref[...] = squares
-
-
-def update(weight, grad, first, second, rate):
-    first = BETA_ONE * first + (1.0 - BETA_ONE) * grad
-    second = BETA_TWO * second + (1.0 - BETA_TWO) * grad * grad
-    shown = second * (1.0 / (1.0 - BETA_TWO**STEP_NO))
-    step = first * (1.0 / (1.0 - BETA_ONE**STEP_NO)) / (shown * lax.rsqrt(shown) + ADAM_EPS)
-    return (weight - rate * (step + DECAY * weight), first, second)
+    squares_ref[...] = jnp.broadcast_to(jnp.sum(squares, 1, keepdims=True) * (1.0 / groups), (1, LANES))
+
+
+def update(weight, grad, factor, first, second, rate):
+    first = BETA_ONE * first + (factor * (1.0 - BETA_ONE)) * grad
+    second = BETA_TWO * second + (factor * factor * (1.0 - BETA_TWO)) * (grad * grad)
+    root = (second * lax.rsqrt(second)) * (1.0 - BETA_TWO**STEP_NO) ** -0.5 + ADAM_EPS
+    turned = pl.reciprocal(root, approx=True)
+    turned = turned * (2.0 - root * turned)
+    step = first * turned * (rate / (1.0 - BETA_ONE**STEP_NO))
+    return (weight * (1.0 - rate * DECAY) - step, first, second)
 
 
 def update_kernel(rates, got_ref, scalar_ref, dfc_ref, *refs):
@@ -1006,7 +1034,7 @@
             def block(i, _):
                 here = pl.ds(pl.multiple_of(at * chunk + i * wide, 8), wide)
                 new = update(
-                    weights[index][here], grad_ref[here] * factor, firsts[index][here], seconds[index][here],
+                    weights[index][here], grad_ref[here], factor, firsts[index][here], seconds[index][here],
                     rates[index],
                 )
                 for kind in range(3):
@@ -1026,7 +1054,7 @@
     in_blocks(1, packed_s, lstm_s, 2)
 
     def step(index, grad):
-        new = update(weights[index][...], grad * factor, firsts[index][...], seconds[index][...], rates[index])
+        new = update(weights[index][...], grad, factor, firsts[index][...], seconds[index][...], rates[index])
         for kind in range(3):
             news[kind][index][...] = new[kind]
 
@@ -1036,7 +1064,13 @@
     step(4, packed_s[ROW_DEC:ROW_COND])
     step(5, packed_s[ROW_MASK : ROW_MASK + NM, 0:C])
     line = jnp.concatenate([packed_s[ROW_VECTOR + place : ROW_VECTOR + place + 1] for place in range(5)], axis=1)
-    step(6, line[:, : weights[6].shape[1]])
+    width = weights[6].shape[0]
+    new = update(
+        weights[6][...].reshape(1, width), line[:, :width], factor, firsts[6][...].reshape(1, width),
+        seconds[6][...].reshape(1, width), rates[6],
+    )
+    for kind in range(3):
+        news[kind][6][...] = new[kind].reshape(width)
     for copy in copies:
         copy.wait()
 
@@ -1115,21 +1149,23 @@
         forward_kernel,
         20,
         [
-            ((shots, TILES, 16, LANES), BF), (cells, BF), (cells, BF), ((steps, TILES, 4 * C, LANES), F32),
+            ((shots, TILES, 16, LANES), BF), ((shots,) + cells[1:], BF), (cells, BF),
+            ((steps, TILES, 4 * C, LANES), F32),
             (cells, F32), ((count, own, 16, LANES), BF),
         ],
         [
             ((6, 48, LANES), BF), ((8, KS * C, LANES), BF), ((8, KS * C, LANES), BF), ((TILES, C, LANES), F32),
             ((KK * C, LANES), BF), ((4 * C, KK * C), BF), ((4 * C, KK * C), BF),
+            ((TILES, 4 * C, LANES), F32), ((TILES, 4 * C, LANES), F32),
         ],
         half_1, raw, wide_enc, w_lstm, bias,
     )
     items = clips * steps
     order = jnp.asarray(strip_order(), BF)
-    k_fc = w_fc.astype(BF)
+    k_fc = jnp.einsum("jnl,kl->jnk", w_fc.astype(BF), order, preferred_element_type=F32).astype(BF)
     strip_hid = exchange(strips_out, "row").reshape(items, 2, WB * C)
+    parts = jnp.einsum("mjk,jnk->mn", strip_hid, k_fc, preferred_element_type=F32)
     strip_hid = jnp.einsum("mjk,kl->jml", strip_hid, order, preferred_element_type=F32).astype(BF)
-    parts = jnp.einsum("jmk,jnk->mn", strip_hid, k_fc, preferred_element_type=F32)
     strip_hid_all = to_all(strip_hid, "clip")
     summed = jnp.sum(exchange(parts.reshape(count, own, NK * KK), "row"), 0)
     presence = flags.astype(F32)
@@ -1154,9 +1190,10 @@
             ((200, LANES), F32),
         ],
         [
-            ((6, 48, LANES), F32), ((C, 4 * C), BF), ((4 * C, C), BF), ((64, 12 * C), BF),
+            ((6, 48, LANES), F32), ((6, 48, LANES), F32), ((C, 4 * C), BF), ((4 * C, C), BF), ((64, 12 * C), BF),
             ((4 * C, 192), BF), ((4 * C + 64, LANES), F32), ((64, 4 * C), F32),
-            ((4 * WIN, 32), BF), ((32, 4 * WIN), BF), ((4 * WIN, TILES * LANES), BF), ((own, 64, 4 * WIN), F32),
+            ((4 * WIN, 32), BF), ((32, 4 * WIN), BF), ((4 * WIN, TILES * LANES), BF),
+            ((4 * WIN, TILES * LANES), BF), ((own, 64, 4 * WIN), F32),
             ((own, 16, 32), F32),
         ],
         half_1, x, hid, logits, w_deconv, w_mask.T, bias,
@@ -1166,25 +1203,18 @@
     every_sum = to_all(d_logit.astype(BF), ("clip", "row")).reshape(-1, items, NK * KK)
     d_sum = lax.dynamic_index_in_dim(every_sum, lax.axis_index("clip"), 0, False)
     back_fc = jnp.einsum("mn,jnk->mjk", d_sum, k_fc, preferred_element_type=F32).astype(BF)
-    back_fc = lax.dot_general(
-        back_fc.reshape(items * 2, WB * C), order, (((1,), (1,)), ((), ())), preferred_element_type=F32
-    ).astype(BF)
     back_fc = exchange(back_fc.reshape(count, own, 16, LANES), "row")
     swap = [(index, index ^ 1) for index in range(count)]
 
-    def in_order(block):
-        other = lax.ppermute(block, "row", swap)
-        return jnp.stack([jnp.where(half == 0, block, other), jnp.where(half == 0, other, block)])
-
     keep, d_enc, lines = call(
         backward_kernel,
-        16,
-        [((own, TILES, 4 * C, LANES), BF), ((own, TILES, C, LANES), F32), ((4 * C, LANES), F32)],
+        0.1,
+        [((own + 1, TILES, 4 * C, LANES), BF), ((own + 1, TILES, C, LANES), F32), ((4 * C, LANES), F32)],
         [
             ((8, 4 * C, LANES), BF), ((TILES, C, LANES), F32), ((TILES, C, LANES), F32),
-            ((KS * 2 * C, KS * 4 * C), BF),
+            ((KS * 2 * C, KS * 4 * C), BF), ((TILES, 7 * C, LANES), F32), ((TILES, 7 * C, LANES), F32),
         ],
-        half_1, act, cell, in_order(dec), in_order(back_fc), w_lstm,
+        half_1, act, cell, dec, lax.ppermute(dec, "row", swap), back_fc, lax.ppermute(back_fc, "row", swap), w_lstm,
     )
     groups = lax.axis_size("clip")
 
@@ -1200,14 +1230,11 @@
         scratch_shapes=[pltpu.VMEM((NK * KK, groups * items), BF)],
         compiler_params=pltpu.CompilerParams(vmem_limit_bytes=VMEM_BYTES),
     )(strip_hid_all, every_sum)
-    fc_squares = jnp.sum(fc_squares) / groups
-
     d_cond = jnp.dot(cond.T, d_logit, precision=HIGH)
     d_cond = jnp.pad(d_cond, ((0, 16 - COND), (0, 2 * LANES - NK * KK)))
     d_cond = jnp.concatenate([d_cond[:, :LANES], d_cond[:, LANES:]], axis=0)
     d_line = jnp.pad(d_logit, ((0, 0), (7 * C, 5 * LANES - 7 * C - NK * KK)))
-    scalars = jnp.stack([jnp.zeros_like(fc_squares), jnp.sum(valid.astype(F32)), fc_squares])
-    scalars = jnp.pad(scalars, (0, LANES - 3)).reshape(1, LANES)
+    counted = jnp.broadcast_to(jnp.sum(valid.astype(F32)), (1, LANES))
     both = ("clip", "row")
     devices = lax.axis_size(both)
     block = call(
@@ -1218,7 +1245,7 @@
             ((6, 48, LANES), BF), ((8, KS * 2 * C, LANES), BF), ((C, WIN), F32), ((11 * C + 64, LANES), F32),
             ((ROWS, LANES), F32),
         ],
-        half_1, x, enc, hid, keep, d_enc, lines, head_sums, d_dec, d_mask, d_cond, d_line, scalars, wide_enc, bias,
+        half_1, x, enc, hid, keep, d_enc, lines, head_sums, d_dec, d_mask, d_cond, d_line, counted, fc_squares, wide_enc, bias,
         jnp.asarray(vector_places(), F32), jnp.asarray(np.pad(encoder, ((0, 0), (0, LANES - KK * 3))), F32),
     )[0]
     sums, scalars = pl.pallas_call(
@@ -1235,13 +1262,13 @@
         enc, lstm, fc, cond, dec, mask, line = group
         fc = fc.reshape(2, NK * KK, WB * C // LANES, LANES)
         fc = jnp.transpose(fc, (1, 2, 0, 3)).reshape(-1, LANES)
-        return [enc.T, lstm, fc, cond, dec, mask.T, line.reshape(1, -1)]
+        return [enc.T, lstm, fc, cond, dec, mask.T, line]
 
     def back(group):
         enc, lstm, fc, cond, dec, mask, line = group
         fc = fc.reshape(NK * KK, WB * C // LANES, 2, LANES)
         fc = jnp.transpose(fc, (2, 0, 1, 3)).reshape(w_fc.shape)
-        return [enc.T, lstm, fc, cond, dec, mask.T, line.reshape(-1)]
+        return [enc.T, lstm, fc, cond, dec, mask.T, line]
 
     weights = shown([w_enc, w_lstm, w_fc, w_cond, w_deconv, w_mask, vector])
     firsts = shown([m_enc, m_lstm, m_fc, m_cond, m_deconv, m_mask, m_vector])

time: 220 us -> 202 us (0.918)
  Pallas kernels: 84.9 us -> 74.1 us
  other arithmetic: 12.7 us -> 3.61 us
    pallas_call x4, Pallas kernels: 68.8 us -> 58.3 us  [call(): pl.pallas_call(kernel, cost_estimate=cost(micros), out_shape=[jax.ShapeDt...]
    pallas_call x3 -> x0, other arithmetic: 3.85 us -> none  [whole_clips(): pl.pallas_call(functools.partial(update_kernel, rates), out_shape=[jax.Sh...]
    another operation x4 -> x0, other arithmetic: 2.74 us -> none  [in_order(): jnp.stack([jnp.where(half == 0, block, other), jnp.where(half == 0, other...]
where the time goes in v4:
time: 202 us; the launch traced here: 201 us
  Pallas kernels  74.1 us (37%)
  waiting for transfers between devices  53.2 us (26%)
  starting transfers between devices  26.7 us (13%)
  blocking collectives  20.2 us (10%)
  local copies, waits for them, and re-layouts  15.4 us (8%)
  matrix products  6.67 us (3%)
  other arithmetic  3.61 us (2%)
    pallas_call x4, Pallas kernels, call(): pl.pallas_call(kernel, cost_estimate=cost(micros), out_shape=[jax.ShapeDt...  58.3 us
    all_to_all x7, waiting for transfers between devices, exchange(): return lax.all_to_all(block, axes, 0, 0, tiled=True)  53.1 us
    all_to_all x7, starting transfers between devices, exchange(): return lax.all_to_all(block, axes, 0, 0, tiled=True)  26.2 us
    all_to_all x1, blocking collectives, exchange(): return lax.all_to_all(block, axes, 0, 0, tiled=True)  20.2 us
    pallas_call x1, Pallas kernels, whole_clips(): pl.pallas_call(functools.partial(update_kernel, rates), out_shape=[jax.Sh...  10.1 us
  transfers between devices with their start and end apart: 9, of which 6 were waited for; matrix products, arithmetic and copies ran while one was open for 5% of the time, Pallas kernels for 7%

profile of v4, /device:TPU:0, one launch (start us, length us, event | category | flops | bytes accessed | tf_op | source)
XLA Modules:
  0.0 201.0 jit_solution(9812929063989393039)
XLA Ops:
  0.7 0.0 copy-start.12
  0.7 1.1 copy.72
  1.8 0.9 convert_element_type.45
  2.9 0.5 maximum_bitcast_fusion
  3.3 0.1 reshape.125
  3.5 0.8 broadcast_in_dim.12
  4.2 6.3 %all-to-all-start = ((bf16[8,144,128]{2,1,0:T(8,128)(2,1)}), bf16[8,144,128]{2,1,0:T(8,128)(2,1)S(1)}, u32[]{:S(2)}, u32[]{:S(2)}) async-start(bf16[8,144,128]{2,1,0:T(8,128)(2,1)} %bitcast.4), calls=%async_computation | async-start | bytes 589824 | tf_op jit(solution)/shard_map/all_to_all | solution.py:1103
  10.6 0.1 slice.34
  10.6 0.1 slice.35
  10.7 0.1 copy.78
  10.8 0.1 select_maximum_fusion
  10.9 0.8 fusion.1.we_ref
  11.7 9.3 %all-to-all-done.raw_ref = bf16[8,144,128]{2,1,0:T(8,128)(2,1)S(1)} async-done(((bf16[8,144,128]{2,1,0:T(8,128)(2,1)}), bf16[8,144,128]{2,1,0:T(8,128)(2,1)S(1)}, u32[]{:S(2)}, u32[]{:S(2)}) %all-to-all-start) | async-done | bytes 294944 | tf_op jit(solution)/shard_map/all_to_all | solution.py:1103
  21.0 0.8 broadcast_in_dim.13.bias_ref
  21.8 17.6 %shard_map.496 = (bf16[17,4,16,128]{3,2,1,0:T(8,128)(2,1)}, bf16[17,4,32,128]{3,2,1,0:T(8,128)(2,1)}, bf16[16,4,32,128]{3,2,1,0:T(8,128)(2,1)}, f32[16,4,128,128...) custom-call(s32[1]{0:T(128)} %bitcast.half_ref, bf16[8,144,128]{2,1,0:T(8,128)(2,1)} %copy-done.6, ...), custom_call_target="tpu_custom_call" | custom-call | flops 16000000000 | bytes 1024 | tf_op jit(solution)/shard_map/pallas_call | solution.py:1087
  39.4 3.5 %all-to-all-start.1 = ((bf16[8,8,16,128]{3,2,1,0:T(8,128)(2,1)}), bf16[8,8,16,128]{3,2,1,0:T(8,128)(2,1)S(1)}, u32[]{:S(2)}, u32[]{:S(2)}) async-start(bf16[8,8,16,128]{3,2,1,0:T(8,128)(2,1)} %get-tuple-element.71), calls=%async_computation.1 | async-start | bytes 524288 | tf_op jit(solution)/shard_map/all_to_all | solution.py:1103
  42.9 0.1 broadcast_multiply_fusion
  43.0 0.7 convert_element_type.48
  43.7 0.1 copy.77
  43.8 2.9 %convolution_convert_fusion = bf16[1024,2,250]{2,0,1:T(8,128)(2,1)S(1)} fusion(bf16[1024,1024,1]{1,0,2:T(8,128)(2,1)} %constant.85, bf16[2,250,1024]{2,0,1:T(2,128)(2,1)S(1)} %convert_element_type.48), kind=kOutput, calls=%fused_computation | convolution fusion | flops 1049088000 | bytes 4145152 | tf_op jit(solution)/shard_map/jnl,kl->jnk/dot_general | solution.py:1165
  46.7 5.8 %all-to-all-done.1 = bf16[8,8,16,128]{3,2,1,0:T(8,128)(2,1)S(1)} async-done(((bf16[8,8,16,128]{3,2,1,0:T(8,128)(2,1)}), bf16[8,8,16,128]{3,2,1,0:T(8,128)(2,1)S(1)}, u32[]{:S(2)}, u32[]{:S(2)}) %all-to-all-start.1) | async-done | bytes 262176 | tf_op jit(solution)/shard_map/all_to_all | solution.py:1103
  52.6 0.1 dot_general.24
  52.7 0.9 convolution_bitcast_fusion
  53.6 3.4 %all-to-all-start.2 = ((f32[8,8,250]{2,1,0:T(8,128)}), f32[8,8,250]{2,1,0:T(8,128)S(1)}, u32[]{:S(2)}, u32[]{:S(2)}) async-start(f32[8,8,250]{2,1,0:T(8,128)} %convolution_bitcast_fusion), calls=%async_computation.2 | async-start | bytes 131072 | tf_op jit(solution)/shard_map/all_to_all | solution.py:1103
  56.9 0.1 broadcast_multiply_fusion.1
  57.0 0.1 slice.38
  57.1 5.7 %all-to-all-done.2 = f32[8,8,250]{2,1,0:T(8,128)S(1)} async-done(((f32[8,8,250]{2,1,0:T(8,128)}), f32[8,8,250]{2,1,0:T(8,128)S(1)}, u32[]{:S(2)}, u32[]{:S(2)}) %all-to-all-start.2) | async-done | bytes 64032 | tf_op jit(solution)/shard_map/all_to_all | solution.py:1103
  62.8 0.2 fusion.2
  63.0 0.1 reshape.127
  63.1 0.6 pad.27.logit_ref
  63.8 15.3 %shard_map.497 = (bf16[8,4,32,128]{3,2,1,0:T(8,128)(2,1)}, f32[8,16,32]{2,1,0:T(8,128)}, f32[32,128]{1,0:T(8,128)}, f32[16,128]{1,0:T(8,128)}, f32[200,128]{1,0:T(8,128)}) custom-call(s32[1]{0:T(128)} %bitcast.half_ref, bf16[17,4,16,128]{3,2,1,0:T(8,128)(2,1)} %get-tuple-element.66.x_ref, bf16[16,4,32,128]{3,2,1,0:T(8,128)(2,1)} %get-tuple-element.68.hid_ref, ...), custom_call_target="tpu_custom_call" | custom-call | flops 24000000000 | bytes 1024 | tf_op jit(solution)/shard_map/pallas_call | solution.py:1087
  79.0 1.6 slice.39
  80.7 0.9 reshape.128
  81.6 0.7 broadcast_in_dim.15
  82.2 3.3 %all-to-all-start.3 = ((bf16[32,8,250]{2,1,0:T(8,128)(2,1)}), bf16[32,8,250]{2,1,0:T(8,128)(2,1)}, u32[]{:S(2)}, u32[]{:S(2)}) async-start(bf16[32,8,250]{2,1,0:T(8,128)(2,1)} %broadcast_in_dim.15), calls=%async_computation.3 | async-start | bytes 262144 | tf_op jit(solution)/shard_map/all_to_all | solution.py:1103
  85.6 8.1 %all-to-all-done.3 = bf16[32,8,250]{2,1,0:T(8,128)(2,1)} async-done(((bf16[32,8,250]{2,1,0:T(8,128)(2,1)}), bf16[32,8,250]{2,1,0:T(8,128)(2,1)}, u32[]{:S(2)}, u32[]{:S(2)}) %all-to-all-start.3) | async-done | bytes 128032 | tf_op jit(solution)/shard_map/all_to_all | solution.py:1103
  93.7 1.2 convolution_convert_fusion.2
  94.9 0.3 copy.80
  95.2 0.9 reshape.130
  96.0 3.4 %all-to-all-start.4 = ((bf16[8,8,16,128]{3,2,1,0:T(8,128)(2,1)}), bf16[8,8,16,128]{3,2,1,0:T(8,128)(2,1)S(1)}, u32[]{:S(2)}, u32[]{:S(2)}) async-start(bf16[8,8,16,128]{3,2,1,0:T(8,128)(2,1)} %reshape.130), calls=%async_computation.4 | async-start | bytes 524288 | tf_op jit(solution)/shard_map/all_to_all | solution.py:1103
  99.5 0.1 reshape.131
  99.5 0.4 fusion
  100.0 9.1 %all-to-all-done.4.fc_ref = bf16[8,8,16,128]{3,2,1,0:T(8,128)(2,1)S(1)} async-done(((bf16[8,8,16,128]{3,2,1,0:T(8,128)(2,1)}), bf16[8,8,16,128]{3,2,1,0:T(8,128)(2,1)S(1)}, u32[]{:S(2)}, u32[]{:S(2)}) %all-to-all-start.4) | async-done | bytes 262176 | tf_op jit(solution)/shard_map/all_to_all | solution.py:1103
  109.1 1.1 broadcast_in_dim.17
  110.2 3.7 %all-to-all-start.5 = ((bf16[4,2,64,1024]{3,2,1,0:T(8,128)(2,1)}), bf16[4,2,64,1024]{3,2,1,0:T(8,128)(2,1)S(1)}, u32[]{:S(2)}, u32[]{:S(2)}) async-start(bf16[4,2,64,1024]{3,2,1,0:T(8,128)(2,1)} %broadcast_in_dim.17), calls=%async_computation.5 | async-start | bytes 2097152 | tf_op jit(solution)/shard_map/all_to_all | solution.py:1103
  113.9 0.7 convert_reduce_fusion
  114.6 0.5 collective-permute-start.1
  115.1 0.3 fusion.15
  115.4 0.7 pad.29.dline_ref
  116.1 0.6 pad_maximum_fusion.dcond_ref
  116.7 0.7 copy-done.8
  117.4 0.1 copy-done.9
  117.5 14.4 %shard_map.498 = (bf16[9,4,128,128]{3,2,1,0:T(8,128)(2,1)}, f32[9,4,32,128]{3,2,1,0:T(8,128)}, f32[128,128]{1,0:T(8,128)}) custom-call(s32[1]{0:T(128)} %bitcast.half_ref, f32[16,4,128,128]{3,2,1,0:T(8,128)} %get-tuple-element.69.act_ref, f32[16,4,32,128]{3,2,1,0:T(8,128)} %get-tuple-element.70.cell_ref, bf16[8,4,32,128]{3,2,1,0:T(8,128)(2,1)} %get-tuple-element.72.dec_ref, ...), custom_call_target="tpu_custom_call" | custom-call | flops 80000000 | bytes 1024 | tf_op jit(solution)/shard_map/pallas_call | solution.py:1087
  131.9 1.0 copy-done.4
  132.9 3.7 %shard_map.499 = (f32[4000,128]{1,0:T(8,128)}, f32[1,128]{1,0:T(1,128)}) custom-call(bf16[4,2,64,1024]{3,2,1,0:T(8,128)(2,1)} %copy-done.4, bf16[4,64,250]{2,1,0:T(8,128)(2,1)} %bitcast.15.sum_ref), custom_call_target="tpu_custom_call" | custom-call | flops 1600000000 | bytes 1024 | tf_op jit(solution)/shard_map/pallas_call | solution.py:1222
  136.6 1.2 broadcast_in_dim.16.count_ref
  137.7 11.1 %shard_map.500 = bf16[32,64,128]{2,1,0:T(8,128)(2,1)} custom-call(s32[1]{0:T(128)} %bitcast.half_ref, bf16[17,4,16,128]{3,2,1,0:T(8,128)(2,1)} %get-tuple-element.66.x_ref, bf16[17,4,32,128]{3,2,1,0:T(8,128)(2,1)} %get-tuple-element.67.enc_ref, bf16[16,4,32,128]{3,2,1,0:T(8,128)(2,1)} %get-tuple-element.68.hid_ref, ...), custom_call_target="tpu_custom_call" | custom-call | flops 9600000000 | bytes 1024 | tf_op jit(solution)/shard_map/pallas_call | solution.py:1087
  148.8 20.2 %all_to_all.40.got_ref = bf16[32,64,128]{2,1,0:T(8,128)(2,1)} all-to-all(bf16[32,64,128]{2,1,0:T(8,128)(2,1)} %shard_map.500), channel_id=1, replica_groups=mesh['clip'=4,'row'=8] {'clip','row'}, dimensions={0} | all-to-all | bytes 1048576 | tf_op jit(solution)/shard_map/all_to_all | solution.py:1103
  169.0 2.0 shard_map.501
  171.0 2.6 %all-to-all-start.7 = ((bf16[32,64,128]{2,1,0:T(8,128)(2,1)}), bf16[32,64,128]{2,1,0:T(8,128)(2,1)S(1)}, u32[]{:S(2)}, u32[]{:S(2)}) async-start(bf16[32,64,128]{2,1,0:T(8,128)(2,1)} %get-tuple-element.84), calls=%async_computation.7 | async-start | bytes 1048576 | tf_op jit(solution)/shard_map/all_to_all | solution.py:1103
  173.6 1.3 fusion.19
  174.9 15.0 %all-to-all-done.7.got_ref = bf16[32,64,128]{2,1,0:T(8,128)(2,1)S(1)} async-done(((bf16[32,64,128]{2,1,0:T(8,128)(2,1)}), bf16[32,64,128]{2,1,0:T(8,128)(2,1)S(1)}, u32[]{:S(2)}, u32[]{:S(2)}) %all-to-all-start.7) | async-done | bytes 524320 | tf_op jit(solution)/shard_map/all_to_all | solution.py:1103
  190.0 0.8 copy-done.2
  190.8 10.1 %shard_map.502 = (f32[]{:T(128)}, f32[32,75]{1,0:T(8,128)}, f32[1600,128]{1,0:T(8,128)}, f32[4000,128]{1,0:T(8,128)}, f32[15,250]{1,0:T(8,128)}, /*index=5*/f32[...) custom-call(bf16[32,64,128]{2,1,0:T(8,128)(2,1)} %copy-done.2, ...), custom_call_target="tpu_custom_call" | custom-call | tf_op jit(solution)/shard_map/pallas_call | solution.py:1279
  (46 shorter events, 0.2 us)
Async XLA Ops:
  0.7 10.3 %copy-start.12 = (bf16[144,75]{1,0:T(8,128)(2,1)S(1)}, bf16[144,75]{1,0:T(8,128)(2,1)}, u32[]{:S(2)}) copy-start(bf16[144,75]{1,0:T(8,128)(2,1)} %constant.62.clone) | copy-start | bytes 64804
  0.7 9.9 %copy-start.13 = (f32[517]{0:T(1024)S(1)}, f32[517]{0:T(1024)}, u32[]{:S(2)}) copy-start(f32[517]{0:T(1024)} %refs_6_.1) | copy-start | bytes 6208
  0.7 10.2 %slice-start = ((f32[517]{0:T(1024)}), f32[224]{0:T(256)S(1)}, s32[]{:S(2)}) async-start(f32[517]{0:T(1024)} %refs_6_.1), calls=%async_computation.8 | async-start | bytes 2048 | tf_op jit(solution)/shard_map/slice | solution.py:1145
  0.7 10.0 %copy-start.16 = (s32[4,16,2]{1,2,0:T(2,128)S(1)}, s32[4,16,2]{1,2,0:T(2,128)}, u32[]{:S(2)}) copy-start(s32[4,16,2]{1,2,0:T(2,128)} %param.35) | copy-start | bytes 1540
  0.7 10.0 %copy-start.15 = (f32[4,16,3]{1,0,2:T(4,128)S(1)}, f32[4,16,3]{1,0,2:T(4,128)}, u32[]{:S(2)}) copy-start(f32[4,16,3]{1,0,2:T(4,128)} %param.37) | copy-start | bytes 2308
  0.7 10.2 %copy-start.10 = (f32[75,32]{0,1:T(8,128)S(1)}, f32[75,32]{0,1:T(8,128)}, u32[]{:S(2)}) copy-start(f32[75,32]{0,1:T(8,128)} %param.39) | copy-start | bytes 28804
  4.2 16.8 %all-to-all-start = ((bf16[8,144,128]{2,1,0:T(8,128)(2,1)}), bf16[8,144,128]{2,1,0:T(8,128)(2,1)S(1)}, u32[]{:S(2)}, u32[]{:S(2)}) async-start(bf16[8,144,128]{2,1,0:T(8,128)(2,1)} %bitcast.4), calls=%async_computation | async-start | bytes 589824 | tf_op jit(solution)/shard_map/all_to_all | solution.py:1103
  21.0 0.8 copy-start.6
  21.8 21.2 %copy-start = (f32[2,250,1024]{2,0,1:T(2,128)S(1)}, f32[2,250,1024]{2,0,1:T(2,128)}, u32[]{:S(2)}) copy-start(f32[2,250,1024]{2,0,1:T(2,128)} %param.41) | copy-start | bytes 6144004
  39.4 4.3 %copy-start.14 = (f32[4,16,4]{1,2,0:T(4,128)S(1)}, f32[4,16,4]{1,2,0:T(4,128)}, u32[]{:S(2)}) copy-start(f32[4,16,4]{1,2,0:T(4,128)} %param.36) | copy-start | bytes 3076
  39.4 13.2 %all-to-all-start.1 = ((bf16[8,8,16,128]{3,2,1,0:T(8,128)(2,1)}), bf16[8,8,16,128]{3,2,1,0:T(8,128)(2,1)S(1)}, u32[]{:S(2)}, u32[]{:S(2)}) async-start(bf16[8,8,16,128]{3,2,1,0:T(8,128)(2,1)} %get-tuple-element.71), calls=%async_computation.1 | async-start | bytes 524288 | tf_op jit(solution)/shard_map/all_to_all | solution.py:1103
  46.7 16.1 %copy-start.17 = (f32[4,8]{1,0:T(4,128)S(1)}, f32[4,8]{1,0:T(4,128)}, u32[]{:S(2)}) copy-start(f32[4,8]{1,0:T(4,128)} %param.38) | copy-start | bytes 388
  46.7 16.1 %copy-start.11 = (f32[15,250]{1,0:T(8,128)S(1)}, f32[15,250]{1,0:T(8,128)}, u32[]{:S(2)}) copy-start(f32[15,250]{1,0:T(8,128)} %refs_3_.1) | copy-start | bytes 45004
  53.6 9.2 %all-to-all-start.2 = ((f32[8,8,250]{2,1,0:T(8,128)}), f32[8,8,250]{2,1,0:T(8,128)S(1)}, u32[]{:S(2)}, u32[]{:S(2)}) async-start(f32[8,8,250]{2,1,0:T(8,128)} %convolution_bitcast_fusion), calls=%async_computation.2 | async-start | bytes 131072 | tf_op jit(solution)/shard_map/all_to_all | solution.py:1103
  79.0 20.5 %copy-start.1 = (bf16[1024,1024,1]{1,0,2:T(8,128)(2,1)S(1)}, bf16[1024,1024,1]{1,0,2:T(8,128)(2,1)}, u32[]{:S(2)}) copy-start(bf16[1024,1024,1]{1,0,2:T(8,128)(2,1)} %constant.85) | copy-start | bytes 6291460
  82.2 11.5 %all-to-all-start.3 = ((bf16[32,8,250]{2,1,0:T(8,128)(2,1)}), bf16[32,8,250]{2,1,0:T(8,128)(2,1)}, u32[]{:S(2)}, u32[]{:S(2)}) async-start(bf16[32,8,250]{2,1,0:T(8,128)(2,1)} %broadcast_in_dim.15), calls=%async_computation.3 | async-start | bytes 262144 | tf_op jit(solution)/shard_map/all_to_all | solution.py:1103
  96.0 13.1 %all-to-all-start.4 = ((bf16[8,8,16,128]{3,2,1,0:T(8,128)(2,1)}), bf16[8,8,16,128]{3,2,1,0:T(8,128)(2,1)S(1)}, u32[]{:S(2)}, u32[]{:S(2)}) async-start(bf16[8,8,16,128]{3,2,1,0:T(8,128)(2,1)} %reshape.130), calls=%async_computation.4 | async-start | bytes 524288 | tf_op jit(solution)/shard_map/all_to_all | solution.py:1103
  100.0 13.9 %copy-start.5 = (s32[4,16,4,64]{3,2,1,0:T(4,128)S(1)}, s32[4,16,4,64]{3,2,1,0:T(4,128)}, u32[]{:S(2)}) copy-start(s32[4,16,4,64]{3,2,1,0:T(4,128)} %param.34) | copy-start | bytes 196612
  100.0 14.6 %copy-start.7 = (bf16[8,4,32,128]{3,2,1,0:T(8,128)(2,1)S(1)}, bf16[8,4,32,128]{3,2,1,0:T(8,128)(2,1)}, u32[]{:S(2)}) copy-start(bf16[8,4,32,128]{3,2,1,0:T(8,128)(2,1)} %get-tuple-element.72.dec_ref) | copy-start | bytes 786436
  109.1 7.6 %copy-start.3 = (bf16[8,8,16,128]{3,2,1,0:T(8,128)(2,1)}, bf16[8,8,16,128]{3,2,1,0:T(8,128)(2,1)S(1)}, u32[]{:S(2)}) copy-start(bf16[8,8,16,128]{3,2,1,0:T(8,128)(2,1)S(1)} %all-to-all-done.4.fc_ref) | copy-start | bytes 786436
  110.2 21.7 %all-to-all-start.5 = ((bf16[4,2,64,1024]{3,2,1,0:T(8,128)(2,1)}), bf16[4,2,64,1024]{3,2,1,0:T(8,128)(2,1)S(1)}, u32[]{:S(2)}, u32[]{:S(2)}) async-start(bf16[4,2,64,1024]{3,2,1,0:T(8,128)(2,1)} %broadcast_in_dim.17), calls=%async_computation.5 | async-start | bytes 2097152 | tf_op jit(solution)/shard_map/all_to_all | solution.py:1103
  114.6 2.1 %collective-permute-start = (bf16[8,4,32,128]{3,2,1,0:T(8,128)(2,1)S(1)}, bf16[8,4,32,128]{3,2,1,0:T(8,128)(2,1)S(1)}, u32[]{:S(2)}, u32[]{:S(2)}) collective-permute-start(bf16[8,4,32,128]{3,2,1,0:T(8,128)(2,1)S(1)} %copy-done.7), channel_id=1, source_target_pairs={{0,1},{1,0},{2,3},{3,2},{4,5},{5,4},{6,7},{7,6},{8,9},{9,8},{10,11... | collective-permute-start | bytes 786440 | tf_op jit(solution)/shard_map/ppermute | solution.py:1217
  114.6 2.1 %collective-permute-start.1 = (bf16[8,8,16,128]{3,2,1,0:T(8,128)(2,1)S(1)}, bf16[8,8,16,128]{3,2,1,0:T(8,128)(2,1)S(1)}, u32[]{:S(2)}, u32[]{:S(2)}) collective-permute-start(bf16[8,8,16,128]{3,2,1,0:T(8,128)(2,1)S(1)} %all-to-all-done.4.fc_ref), channel_id=1, source_target_pairs={{0,1},{1,0},{2,3},{3,2},{4,5},{5,4},{6,7},{7,6},{8,9},{9,8},{10,11... | collective-permute-start | bytes 786440 | tf_op jit(solution)/shard_map/ppermute | solution.py:1217
  116.7 0.7 copy-start.8
  116.7 0.8 copy-start.9
  131.9 1.0 copy-start.4
  171.0 19.0 %all-to-all-start.7 = ((bf16[32,64,128]{2,1,0:T(8,128)(2,1)}), bf16[32,64,128]{2,1,0:T(8,128)(2,1)S(1)}, u32[]{:S(2)}, u32[]{:S(2)}) async-start(bf16[32,64,128]{2,1,0:T(8,128)(2,1)} %get-tuple-element.84), calls=%async_computation.7 | async-start | bytes 1048576 | tf_op jit(solution)/shard_map/all_to_all | solution.py:1103
  190.0 0.8 copy-start.2

commit v5 on v4

--- a/solution.py
+++ b/solution.py
@@ -535,8 +535,8 @@
 
 def forward_kernel(
     half_ref, raw_ref, we_ref, w_ref, bias_ref,
-    x_ref, enc_ref, hid_ref, act_ref, cell_ref, strip_ref,
-    win_s, enc_s, hid_s, state_s, rows_s, wx_s, wh_s, even_s, odd_s,
+    x_ref, enc_ref, hid_ref, far_act_ref, far_cell_ref, strip_ref,
+    win_s, enc_s, hid_s, state_s, rows_s, wx_s, wh_s, even_s, odd_s, act_ref, cell_ref, sems,
 ):
     steps = hid_ref.shape[0]
     lanes = lane_places()
@@ -592,11 +592,20 @@
             hidden.append(low.astype(F32))
         spread(hidden, lanes, 2, hid_s, C, 0)
 
+    def out_copies(t):
+        return [
+            pltpu.make_async_copy(act_ref.at[t], far_act_ref.at[t], sems.at[0, t]),
+            pltpu.make_async_copy(cell_ref.at[t], far_cell_ref.at[t], sems.at[1, t]),
+        ]
+
     encode(0, even_s)
 
     def advance_two(pair, _):
-        advance(2 * pair, even_s, odd_s)
-        advance(2 * pair + 1, odd_s, even_s)
+        for one, slots in enumerate(((even_s, odd_s), (odd_s, even_s))):
+            advance(2 * pair + one, *slots)
+        for one in range(2):
+            for copy in out_copies(2 * pair + one):
+                copy.start()
         return 0
 
     lax.fori_loop(0, steps // 2, advance_two, 0)
@@ -616,13 +625,16 @@
         return 0
 
     lax.fori_loop(0, own, to_strips, 0)
+    for t in range(steps):
+        for copy in out_copies(t):
+            copy.wait()
 
 
 def head_kernel(
     half_ref, x_ref, hid_ref, logit_ref, w_ref, mask_ref, bias_ref, place_ref, placet_ref,
     back_ref, dlog_ref, dwd_ref, dwm_ref, sums_ref,
     even_s, odd_s, wd_ref, wdt_ref, wm_ref, wmt_ref, over_ref, wide_s, everywhere_s, turned_s, d_even_s, d_odd_s,
-    d_spot_s, kernel_s,
+    d_spot_s, kernel_s, d_logit_s,
 ):
     wd_ref[...] = w_ref[...].astype(BF)
     wdt_ref[...] = nt(one_hot_eye(4 * C), wd_ref[...]).astype(BF)
@@ -699,7 +711,7 @@
             goal = jnp.where((row8 < 4) == (sub // 2 == 0), goal, pltpu.roll(goal, 4, 0))
             diff = jnp.where(color, result - goal, 0.0)
             weighted = diff * goal[3:4]
-            part = weighted * diff
+            part = jnp.where(row8 == 3, goal[3:4], weighted * diff)
             lost = part if lost is None else lost + part
             d_result = 2.0 * weighted
             d_mix_s[sub * WIN : (sub + 1) * WIN] = (window * d_result[None]).reshape(WIN, cells).astype(BF)
@@ -737,7 +749,14 @@
         kernels = kernel_s[i]
         d_one = d_kernels[16 * i : 16 * i + 16]
         inner = jnp.sum(d_one * kernels, -1, keepdims=True)
-        dlog_ref[i] = kernels * (d_one - inner)
+        d_logit_s[16 * i : 16 * i + 16] = kernels * (d_one - inner)
+    total = jnp.zeros(dlog_ref.shape, F32)
+    tap = lax.broadcasted_iota(jnp.int32, (32, 2 * LANES), 0)
+    lane = lax.broadcasted_iota(jnp.int32, (32, 2 * LANES), 1)
+    for kernel in range(NK):
+        place = ((tap < KK) & (lane == kernel * KK + tap)).astype(F32)
+        total = total + nn_exact(d_logit_s[pl.ds(kernel + 1, own, stride=16), :], place)
+    dlog_ref[...] = total
     row = lax.broadcasted_iota(jnp.int32, (64, 4 * C), 0)
     lane = lax.broadcasted_iota(jnp.int32, (64, 4 * C), 1)
     own_block = jnp.where(row // 16 == lane // C, wide_s[...], 0.0)
@@ -747,17 +766,26 @@
 
 
 def backward_kernel(
-    half_ref, act_ref, cell_ref, dec_ref, other_dec_ref, fc_ref, other_fc_ref, w_ref,
+    half_ref, far_act_ref, far_cell_ref, dec_ref, other_dec_ref, fc_ref, other_fc_ref, w_ref,
     keep_ref, denc_ref, lines_ref,
-    gate_s, back_s, state_s, wb_s, even_s, odd_s,
+    gate_s, back_s, state_s, wb_s, even_s, odd_s, act_ref, cell_ref, sems,
 ):
+    steps = far_act_ref.shape[0]
+
+    def act_copy(t):
+        return pltpu.make_async_copy(far_act_ref.at[t], act_ref.at[t], sems.at[0, t])
+
+    def cell_copy(t):
+        return pltpu.make_async_copy(far_cell_ref.at[t], cell_ref.at[t], sems.at[1, t])
+
+    for t in reversed(range(steps)):
+        act_copy(t).start()
+        cell_copy(t).start()
     for tap in range(KK):
         place = tap % KS * 2 * C
         turn = (KS - 1 - tap // KS) * 4 * C
         wb_s[place : place + 2 * C, turn : turn + 4 * C] = w_ref[tap * 2 * C : (tap + 1) * 2 * C, :].astype(BF)
-    steps = act_ref.shape[0]
     own = steps // HALVES
-    base = half_ref[0] * own
     lanes = lane_places()
     back_s[...] = jnp.zeros_like(back_s)
     state_s[...] = jnp.zeros_like(state_s)
@@ -837,11 +865,23 @@
                 denc_ref[place, two + one] = total[:C]
                 back_s[two + one] = total[C:]
 
+    cell_copy(steps - 1).wait()
+    act_copy(steps - 1).wait()
+    cell_copy(steps - 2).wait()
     prepare(steps - 1, even_s)
 
     def retreat_two(pair, _):
-        retreat(steps - 1 - 2 * pair, even_s, odd_s)
-        retreat(steps - 2 - 2 * pair, odd_s, even_s)
+        t = steps - 1 - 2 * pair
+        act_copy(t - 1).wait()
+
+        @pl.when(pair < steps // 2 - 1)
+        def _():
+            act_copy(t - 2).wait()
+            cell_copy(t - 2).wait()
+            cell_copy(t - 3).wait()
+
+        retreat(t, even_s, odd_s)
+        retreat(t - 1, odd_s, even_s)
         return 0
 
     lax.fori_loop(0, steps // 2, retreat_two, 0)
@@ -869,12 +909,35 @@
     return place
 
 
+def logit_map_gradient(hid_ref, sum_ref, out_ref, turned_s):
+    logits = NK * KK
+    groups, items, width = sum_ref.shape
+    eye = one_hot_eye(width)
+    for group in range(groups):
+        turned_s[:, group * items : (group + 1) * items] = nt(eye, sum_ref[group]).astype(BF)
+    squares = jnp.zeros((1, LANES), F32)
+    stride = 2 * WB * C // LANES
+    for row in range(2):
+        for start in range(0, WB * C, 2 * LANES):
+            hid = jnp.concatenate(
+                [hid_ref[group, row, :, start : start + 2 * LANES] for group in range(groups)], axis=0
+            )
+            grad = nn(turned_s[...], hid)[:logits]
+            for one in range(2):
+                part = grad[:, one * LANES : (one + 1) * LANES]
+                squares = squares + jnp.sum(part * part, 0, keepdims=True)
+                out_ref[pl.ds((start // LANES + one) * 2 + row, logits, stride=stride), :] = part
+    return jnp.sum(squares, 1, keepdims=True) * (1.0 / groups)
+
+
 def pack_kernel(
     half_ref, x_ref, enc_ref, hid_ref, keep_ref, denc_ref, lines_ref, head_ref, ddec_ref, dmask_ref, dcond_ref,
-    dline_ref, count_ref, squares_ref, we_ref, bias_ref, place_ref, encoder_ref,
-    block_ref,
-    win_s, join_s, dwe_s, sums_s, packed_s,
+    dline_ref, far_hid_ref, sum_ref, we_ref, bias_ref, place_ref, encoder_ref,
+    block_ref, far_dfc_ref,
+    win_s, join_s, dwe_s, sums_s, packed_s, every_s, dfc_s, turned_s, sems,
 ):
+    every_copy = pltpu.make_async_copy(far_hid_ref, every_s, sems.at[0])
+    every_copy.start()
     own = keep_ref.shape[0] - 1
     base = half_ref[0] * own
     lanes = lane_places()
@@ -919,6 +982,10 @@
         return 0
 
     lax.fori_loop(0, own, gather, 0)
+    every_copy.wait()
+    squares = logit_map_gradient(every_s, sum_ref, dfc_s, turned_s)
+    dfc_copy = pltpu.make_async_copy(dfc_s, far_dfc_ref, sems.at[1])
+    dfc_copy.start()
     packed_s[ROW_DEC:ROW_COND] = ddec_ref[...]
     packed_s[ROW_COND:ROW_ENC] = dcond_ref[...]
     packed_s[ROW_ENC:ROW_MASK] = nn_exact(dwe_s[...], encoder_ref[...])
@@ -926,13 +993,14 @@
     ones = jnp.ones((8, LANES), F32)
     sums_s[3 * C : 7 * C] = lines_ref[...]
     sums_s[7 * C : 11 * C + 64] = head_ref[0:192]
-    line = nn_exact(nt_exact(ones, sums_s[...]), place_ref[...])[0:1] + jnp.sum(dline_ref[...], 0, keepdims=True)
+    line = nn_exact(nt_exact(ones, sums_s[...]), place_ref[...].astype(F32))[0:1] + jnp.sum(dline_ref[...], 0, keepdims=True)
     packed_s[ROW_VECTOR : ROW_VECTOR + 8] = jnp.concatenate(
         [line[:, place * LANES : (place + 1) * LANES] for place in range(5)] + [jnp.zeros((3, LANES), F32)], axis=0
     )
-    lost = jnp.sum(jnp.sum(head_ref[192:196], 0, keepdims=True), 1, keepdims=True)
+    lost = jnp.sum(jnp.sum(head_ref[192:195], 0, keepdims=True), 1, keepdims=True)
+    counted = jnp.sum(head_ref[195:196], 1, keepdims=True)
     lane = lax.broadcasted_iota(jnp.int32, (1, LANES), 1)
-    value = jnp.where(lane == 0, lost, jnp.where(lane == 1, count_ref[...], jnp.where(lane == 2, squares_ref[...], 0.0)))
+    value = jnp.where(lane == 0, lost, jnp.where(lane == 1, counted, jnp.where(lane == 2, squares, 0.0)))
     terms = []
     for _ in range(3):
         low = value.astype(BF).astype(F32)
@@ -947,6 +1015,7 @@
         high = value.astype(BF).astype(F32)
         rows = [packed_s[device * large : (device + 1) * large], high, value - high] + terms + [fill]
         block_ref[device] = jnp.concatenate(rows, axis=0).astype(BF)
+    dfc_copy.wait()
 
 
 def total_kernel(got_ref, out_ref, scalar_ref):
@@ -965,27 +1034,6 @@
         out_ref[device] = low
 
 
-def logit_map_kernel(hid_ref, sum_ref, out_ref, squares_ref, turned_s):
-    logits = NK * KK
-    eye = one_hot_eye(logits)
-    groups, items, _ = sum_ref.shape
-    for group in range(groups):
-        turned_s[:, group * items : (group + 1) * items] = nt(eye, sum_ref[group]).astype(BF)
-    squares = jnp.zeros((1, LANES), F32)
-    stride = 2 * WB * C // LANES
-    for row in range(2):
-        for start in range(0, WB * C, 2 * LANES):
-            hid = jnp.concatenate(
-                [hid_ref[group, row, :, start : start + 2 * LANES] for group in range(groups)], axis=0
-            )
-            grad = nn(turned_s[...], hid)
-            for one in range(2):
-                part = grad[:, one * LANES : (one + 1) * LANES]
-                squares = squares + jnp.sum(part * part, 0, keepdims=True)
-                out_ref[pl.ds((start // LANES + one) * 2 + row, logits, stride=stride), :] = part
-    squares_ref[...] = jnp.broadcast_to(jnp.sum(squares, 1, keepdims=True) * (1.0 / groups), (1, LANES))
-
-
 def update(weight, grad, factor, first, second, rate):
     first = BETA_ONE * first + (factor * (1.0 - BETA_ONE)) * grad
     second = BETA_TWO * second + (factor * factor * (1.0 - BETA_TWO)) * (grad * grad)
@@ -1000,7 +1048,18 @@
     weights, firsts, seconds = refs[0:7], refs[7:14], refs[14:21]
     norm_ref = refs[21]
     news = refs[22:29], refs[29:36], refs[36:43]
-    packed_s, fc_s, lstm_s, sems = refs[43:]
+    packed_s, fc_s, lstm_s, sems, fc_in_s, lstm_in_s, in_sems = refs[43:]
+    ins = []
+    plan = ((2, fc_in_s, 5), (1, lstm_in_s, 2))
+    for index, scratch, chunks in plan:
+        sources = [weights[index], firsts[index], seconds[index]] + ([dfc_ref] if index == 2 else [])
+        chunk = sources[0].shape[0] // chunks
+        for at in range(chunks):
+            for kind, source in enumerate(sources):
+                here = pl.ds(at * chunk, chunk)
+                copy = pltpu.make_async_copy(source.at[here], scratch.at[kind, here], in_sems.at[len(ins)])
+                copy.start()
+                ins.append(copy)
     devices = got_ref.shape[0]
     large = ROW_DEC // devices
     small = SMALL // devices
@@ -1024,34 +1083,28 @@
     norm_ref[...] = jnp.sum(norm)
 
     copies = []
-
-    def in_blocks(index, grad_ref, scratch, chunks):
-        rows = grad_ref.shape[0] if index == 2 else ROW_DEC
+    for (index, scratch, chunks), outs in zip(plan, (fc_s, lstm_s)):
+        rows = scratch.shape[1]
         chunk = rows // chunks
         wide = chunk // 2
         for at in range(chunks):
+            for _ in range(scratch.shape[0]):
+                ins.pop(0).wait()
 
             def block(i, _):
                 here = pl.ds(pl.multiple_of(at * chunk + i * wide, 8), wide)
-                new = update(
-                    weights[index][here], grad_ref[here], factor, firsts[index][here], seconds[index][here],
-                    rates[index],
-                )
+                grad = scratch[3, here] if index == 2 else packed_s[here]
+                new = update(scratch[0, here], grad, factor, scratch[1, here], scratch[2, here], rates[index])
                 for kind in range(3):
-                    scratch[kind, here] = new[kind]
+                    outs[kind, here] = new[kind]
                 return 0
 
-            lax.fori_loop(0, chunk // wide, block, 0)
+            lax.fori_loop(0, 2, block, 0)
             for kind in range(3):
                 here = pl.ds(at * chunk, chunk)
-                copy = pltpu.make_async_copy(
-                    scratch.at[kind, here], news[kind][index].at[here], sems.at[len(copies)]
-                )
+                copy = pltpu.make_async_copy(outs.at[kind, here], news[kind][index].at[here], sems.at[len(copies)])
                 copy.start()
                 copies.append(copy)
-
-    in_blocks(2, dfc_ref, fc_s, 5)
-    in_blocks(1, packed_s, lstm_s, 2)
 
     def step(index, grad):
         new = update(weights[index][...], grad, factor, firsts[index][...], seconds[index][...], rates[index])
@@ -1083,14 +1136,22 @@
     return pl.CostEstimate(flops=int(micros * 8e8), bytes_accessed=1024, transcendentals=0)
 
 
-def call(kernel, micros, outs, scratch, half, *operands):
+ANY_SPEC = pl.BlockSpec(memory_space=pl.ANY)
+
+
+def call(kernel, micros, outs, scratch, half, *operands, far_in=(), far_out=()):
+    def specs(count, far):
+        return [ANY_SPEC if index in far else VMEM_SPEC for index in range(count)]
+
     return pl.pallas_call(
         kernel,
         cost_estimate=cost(micros),
         out_shape=[jax.ShapeDtypeStruct(shape, kind) for shape, kind in outs],
-        in_specs=[SMEM_SPEC] + [VMEM_SPEC] * len(operands),
-        out_specs=[VMEM_SPEC] * len(outs),
-        scratch_shapes=[pltpu.VMEM(shape, kind) for shape, kind in scratch],
+        in_specs=[SMEM_SPEC] + specs(len(operands), far_in),
+        out_specs=specs(len(outs), far_out),
+        scratch_shapes=[
+            pltpu.SemaphoreType.DMA(kind) if shape is None else pltpu.VMEM(shape, kind) for shape, kind in scratch
+        ],
         compiler_params=pltpu.CompilerParams(vmem_limit_bytes=VMEM_BYTES),
     )(half, *operands)
 
@@ -1157,17 +1218,19 @@
             ((6, 48, LANES), BF), ((8, KS * C, LANES), BF), ((8, KS * C, LANES), BF), ((TILES, C, LANES), F32),
             ((KK * C, LANES), BF), ((4 * C, KK * C), BF), ((4 * C, KK * C), BF),
             ((TILES, 4 * C, LANES), F32), ((TILES, 4 * C, LANES), F32),
+            ((steps, TILES, 4 * C, LANES), F32), (cells, F32), (None, (2, steps)),
         ],
-        half_1, raw, wide_enc, w_lstm, bias,
+        half_1, raw, wide_enc, w_lstm, bias, far_out=(3, 4),
     )
     items = clips * steps
     order = jnp.asarray(strip_order(), BF)
-    k_fc = jnp.einsum("jnl,kl->jnk", w_fc.astype(BF), order, preferred_element_type=F32).astype(BF)
+    k_fc = jnp.pad(w_fc.astype(BF), ((0, 0), (0, 2 * LANES - NK * KK), (0, 0)))
+    k_fc = jnp.einsum("jnl,kl->jnk", k_fc, order, preferred_element_type=F32).astype(BF)
     strip_hid = exchange(strips_out, "row").reshape(items, 2, WB * C)
     parts = jnp.einsum("mjk,jnk->mn", strip_hid, k_fc, preferred_element_type=F32)
     strip_hid = jnp.einsum("mjk,kl->jml", strip_hid, order, preferred_element_type=F32).astype(BF)
     strip_hid_all = to_all(strip_hid, "clip")
-    summed = jnp.sum(exchange(parts.reshape(count, own, NK * KK), "row"), 0)
+    summed = jnp.sum(exchange(parts.reshape(count, own, 2 * LANES), "row"), 0)[:, : NK * KK]
     presence = flags.astype(F32)
     conditions = jnp.concatenate(
         [
@@ -1186,7 +1249,7 @@
         head_kernel,
         30,
         [
-            ((own, TILES, C, LANES), BF), ((own, 16, 32), F32), ((C, 4 * C), F32), ((16, LANES), F32),
+            ((own, TILES, C, LANES), BF), ((own, 2 * LANES), F32), ((C, 4 * C), F32), ((16, LANES), F32),
             ((200, LANES), F32),
         ],
         [
@@ -1194,13 +1257,13 @@
             ((4 * C, 192), BF), ((4 * C + 64, LANES), F32), ((64, 4 * C), F32),
             ((4 * WIN, 32), BF), ((32, 4 * WIN), BF), ((4 * WIN, TILES * LANES), BF),
             ((4 * WIN, TILES * LANES), BF), ((own, 64, 4 * WIN), F32),
-            ((own, 16, 32), F32),
+            ((own, 16, 32), F32), ((own * 16, 32), F32),
         ],
         half_1, x, hid, logits, w_deconv, w_mask.T, bias,
         jnp.asarray(places, BF), jnp.asarray(places.transpose(0, 2, 1), BF),
     )
-    d_logit = d_logit[:, 1 : NK + 1, :KK].reshape(own, NK * KK)
-    every_sum = to_all(d_logit.astype(BF), ("clip", "row")).reshape(-1, items, NK * KK)
+    d_logit, strip_hid_all = lax.optimization_barrier((d_logit, strip_hid_all))
+    every_sum = to_all(d_logit.astype(BF), ("clip", "row")).reshape(-1, items, 2 * LANES)
     d_sum = lax.dynamic_index_in_dim(every_sum, lax.axis_index("clip"), 0, False)
     back_fc = jnp.einsum("mn,jnk->mjk", d_sum, k_fc, preferred_element_type=F32).astype(BF)
     back_fc = exchange(back_fc.reshape(count, own, 16, LANES), "row")
@@ -1213,41 +1276,31 @@
         [
             ((8, 4 * C, LANES), BF), ((TILES, C, LANES), F32), ((TILES, C, LANES), F32),
             ((KS * 2 * C, KS * 4 * C), BF), ((TILES, 7 * C, LANES), F32), ((TILES, 7 * C, LANES), F32),
+            ((steps, TILES, 4 * C, LANES), F32), (cells, F32), (None, (2, steps)),
         ],
         half_1, act, cell, dec, lax.ppermute(dec, "row", swap), back_fc, lax.ppermute(back_fc, "row", swap), w_lstm,
-    )
-    groups = lax.axis_size("clip")
-
-    strip_hid_all, every_sum, _ = lax.optimization_barrier((strip_hid_all, every_sum, lines))
-    d_fc, fc_squares = pl.pallas_call(
-        logit_map_kernel,
-        cost_estimate=cost(2),
-        out_shape=[
-            jax.ShapeDtypeStruct((w_fc.size // LANES, LANES), F32), jax.ShapeDtypeStruct((1, LANES), F32)
-        ],
-        in_specs=[VMEM_SPEC] * 2,
-        out_specs=[VMEM_SPEC] * 2,
-        scratch_shapes=[pltpu.VMEM((NK * KK, groups * items), BF)],
-        compiler_params=pltpu.CompilerParams(vmem_limit_bytes=VMEM_BYTES),
-    )(strip_hid_all, every_sum)
+        far_in=(0, 1),
+    )
     d_cond = jnp.dot(cond.T, d_logit, precision=HIGH)
-    d_cond = jnp.pad(d_cond, ((0, 16 - COND), (0, 2 * LANES - NK * KK)))
+    d_cond = jnp.pad(d_cond, ((0, 16 - COND), (0, 0)))
     d_cond = jnp.concatenate([d_cond[:, :LANES], d_cond[:, LANES:]], axis=0)
-    d_line = jnp.pad(d_logit, ((0, 0), (7 * C, 5 * LANES - 7 * C - NK * KK)))
-    counted = jnp.broadcast_to(jnp.sum(valid.astype(F32)), (1, LANES))
+    d_line = jnp.pad(d_logit[:, : NK * KK], ((0, 0), (7 * C, 5 * LANES - 7 * C - NK * KK)))
     both = ("clip", "row")
     devices = lax.axis_size(both)
-    block = call(
+    block, d_fc = call(
         pack_kernel,
         12,
-        [((devices, PART, LANES), BF)],
+        [((devices, PART, LANES), BF), ((w_fc.size // LANES, LANES), F32)],
         [
             ((6, 48, LANES), BF), ((8, KS * 2 * C, LANES), BF), ((C, WIN), F32), ((11 * C + 64, LANES), F32),
-            ((ROWS, LANES), F32),
+            ((ROWS, LANES), F32), (strip_hid_all.shape, BF), ((w_fc.size // LANES, LANES), F32),
+            ((2 * LANES, strip_hid_all.shape[0] * items), BF), (None, (2,)),
         ],
-        half_1, x, enc, hid, keep, d_enc, lines, head_sums, d_dec, d_mask, d_cond, d_line, counted, fc_squares, wide_enc, bias,
-        jnp.asarray(vector_places(), F32), jnp.asarray(np.pad(encoder, ((0, 0), (0, LANES - KK * 3))), F32),
-    )[0]
+        half_1, x, enc, hid, keep, d_enc, lines, head_sums, d_dec, d_mask, d_cond, d_line, strip_hid_all, every_sum,
+        wide_enc, bias,
+        jnp.asarray(vector_places(), BF), jnp.asarray(np.pad(encoder, ((0, 0), (0, LANES - KK * 3))), F32),
+        far_in=(11,), far_out=(1,),
+    )
     sums, scalars = pl.pallas_call(
         total_kernel,
         out_shape=[jax.ShapeDtypeStruct(block.shape, BF), jax.ShapeDtypeStruct((1, LANES), F32)],
@@ -1274,16 +1327,17 @@
     firsts = shown([m_enc, m_lstm, m_fc, m_cond, m_deconv, m_mask, m_vector])
     seconds = shown([v_enc, v_lstm, v_fc, v_cond, v_deconv, v_mask, v_vector])
     shapes = [jax.ShapeDtypeStruct(value.shape, F32) for value in weights]
-    any_spec = pl.BlockSpec(memory_space=pl.ANY)
-    places_out = [VMEM_SPEC, any_spec, any_spec] + [VMEM_SPEC] * 4
+    places_out = [VMEM_SPEC, ANY_SPEC, ANY_SPEC] + [VMEM_SPEC] * 4
     new = pl.pallas_call(
         functools.partial(update_kernel, rates),
         out_shape=[jax.ShapeDtypeStruct((), F32)] + shapes * 3,
-        in_specs=[VMEM_SPEC] * 24,
+        in_specs=[VMEM_SPEC, VMEM_SPEC, ANY_SPEC] + places_out * 3,
         out_specs=[SMEM_SPEC] + places_out * 3,
         scratch_shapes=[
             pltpu.VMEM((ROWS, LANES), F32), pltpu.VMEM((3,) + shapes[2].shape, F32),
             pltpu.VMEM((3,) + shapes[1].shape, F32), pltpu.SemaphoreType.DMA((21,)),
+            pltpu.VMEM((4,) + shapes[2].shape, F32), pltpu.VMEM((3,) + shapes[1].shape, F32),
+            pltpu.SemaphoreType.DMA((26,)),
         ],
         compiler_params=pltpu.CompilerParams(vmem_limit_bytes=VMEM_BYTES),
     )(sums, scalars, d_fc, *weights, *firsts, *seconds)

time: 202 us -> 194 us (0.960)
  Pallas kernels: 74.1 us -> 69.8 us
  waiting for transfers between devices: 53.2 us -> 49.6 us
    pallas_call x1 -> x0, Pallas kernels: 3.69 us -> none  [whole_clips(): pl.pallas_call(logit_map_kernel, cost_estimate=cost(2), out_shape=[jax.Sh...]
    all_to_all x7, waiting for transfers between devices: 53.1 us -> 49.6 us  [exchange(): return lax.all_to_all(block, axes, 0, 0, tiled=True)]
  transfers between devices with their start and end apart: 9 -> 9, of which waited for: 6 -> 6; matrix products, arithmetic and copies ran while one was open for 5% -> 6% of each run, Pallas kernels for 7% -> 8%
where the time goes in v5:
time: 194 us; the launch traced here: 192 us
  Pallas kernels  69.8 us (36%)
  waiting for transfers between devices  49.6 us (26%)
  starting transfers between devices  26.9 us (14%)
  blocking collectives  19.7 us (10%)
  local copies, waits for them, and re-layouts  14.1 us (7%)
  matrix products  7.48 us (4%)
  other arithmetic  3.72 us (2%)
    pallas_call x4, Pallas kernels, call(): pl.pallas_call(kernel, cost_estimate=cost(micros), out_shape=[jax.ShapeDt...  58.3 us
    all_to_all x7, waiting for transfers between devices, exchange(): return lax.all_to_all(block, axes, 0, 0, tiled=True)  49.6 us
    all_to_all x7, starting transfers between devices, exchange(): return lax.all_to_all(block, axes, 0, 0, tiled=True)  26.6 us
    all_to_all x1, blocking collectives, exchange(): return lax.all_to_all(block, axes, 0, 0, tiled=True)  19.7 us
    pallas_call x1, Pallas kernels, whole_clips(): pl.pallas_call(functools.partial(update_kernel, rates), out_shape=[jax.Sh...  9.6 us
  transfers between devices with their start and end apart: 9, of which 6 were waited for; matrix products, arithmetic and copies ran while one was open for 6% of the time, Pallas kernels for 8%

profile of v5, /device:TPU:0, one launch (start us, length us, event | category | flops | bytes accessed | tf_op | source)
XLA Modules:
  0.0 192.5 jit_solution(9305757249016005662)
XLA Ops:
  0.7 0.0 copy-start.14
  0.7 0.0 copy-start
  0.7 1.2 copy.84
  1.9 0.9 convert_element_type.40
  2.9 0.5 maximum_bitcast_fusion
  3.4 0.1 reshape.118
  3.6 0.8 broadcast_in_dim.10
  4.3 6.3 %all-to-all-start = ((bf16[8,144,128]{2,1,0:T(8,128)(2,1)}), bf16[8,144,128]{2,1,0:T(8,128)(2,1)S(1)}, u32[]{:S(2)}, u32[]{:S(2)}) async-start(bf16[8,144,128]{2,1,0:T(8,128)(2,1)} %bitcast.4), calls=%async_computation | async-start | bytes 589824 | tf_op jit(solution)/shard_map/all_to_all | solution.py:1164
  10.6 0.1 slice.37
  10.7 0.1 slice.38
  10.8 0.6 slice.42
  11.4 0.0 slice-start
  11.4 0.0 copy-start.11
  11.5 0.0 copy-start.13
  11.5 0.7 convert_element_type.43
  12.2 1.2 copy.99
  13.4 0.1 copy.89
  13.6 0.1 copy.88
  13.7 0.1 select_maximum_fusion
  13.7 0.1 broadcast_multiply_fusion
  13.8 0.8 fusion.1.we_ref
  14.6 6.5 %all-to-all-done.raw_ref = bf16[8,144,128]{2,1,0:T(8,128)(2,1)S(1)} async-done(((bf16[8,144,128]{2,1,0:T(8,128)(2,1)}), bf16[8,144,128]{2,1,0:T(8,128)(2,1)S(1)}, u32[]{:S(2)}, u32[]{:S(2)}) %all-to-all-start) | async-done | bytes 294944 | tf_op jit(solution)/shard_map/all_to_all | solution.py:1164
  21.1 0.8 broadcast_in_dim.11.bias_ref
  21.9 16.3 %shard_map.496 = (bf16[17,4,16,128]{3,2,1,0:T(8,128)(2,1)}, bf16[17,4,32,128]{3,2,1,0:T(8,128)(2,1)}, bf16[16,4,32,128]{3,2,1,0:T(8,128)(2,1)}, f32[16,4,128,128...) custom-call(s32[1]{0:T(128)} %bitcast.half_ref, bf16[8,144,128]{2,1,0:T(8,128)(2,1)} %copy-done.5, ...), custom_call_target="tpu_custom_call" | custom-call | flops 16000000000 | bytes 1024 | tf_op jit(solution)/shard_map/pallas_call | solution.py:1146
  38.1 3.4 %all-to-all-start.1 = ((bf16[8,8,16,128]{3,2,1,0:T(8,128)(2,1)}), bf16[8,8,16,128]{3,2,1,0:T(8,128)(2,1)S(1)}, u32[]{:S(2)}, u32[]{:S(2)}) async-start(bf16[8,8,16,128]{3,2,1,0:T(8,128)(2,1)} %get-tuple-element.71), calls=%async_computation.1 | async-start | bytes 524288 | tf_op jit(solution)/shard_map/all_to_all | solution.py:1164
  41.6 0.1 broadcast_multiply_fusion.1
  41.6 2.5 %convolution_convert_fusion = bf16[2,256,1024]{2,1,0:T(8,128)(2,1)S(1)} fusion(bf16[1024,1024,1]{1,0,2:T(8,128)(2,1)S(1)} %copy-done.1, bf16[2,250,1024]{2,1,0:T(8,128)(2,1)} %copy.99), kind=kOutput, calls=%fused_computation | convolution fusion | flops 1074266112 | bytes 4169728 | tf_op jit(solution)/shard_map/jnl,kl->jnk/dot_general | solution.py:1228
  44.1 7.1 %all-to-all-done.1 = bf16[8,8,16,128]{3,2,1,0:T(8,128)(2,1)S(1)} async-done(((bf16[8,8,16,128]{3,2,1,0:T(8,128)(2,1)}), bf16[8,8,16,128]{3,2,1,0:T(8,128)(2,1)S(1)}, u32[]{:S(2)}, u32[]{:S(2)}) %all-to-all-start.1) | async-done | bytes 262176 | tf_op jit(solution)/shard_map/all_to_all | solution.py:1164
  51.2 0.8 dot_general.24
  52.0 2.0 %convolution_bitcast_fusion = f32[8,8,256]{2,1,0:T(8,128)} fusion(bf16[2,256,1024]{2,1,0:T(8,128)(2,1)S(1)} %convolution_convert_fusion, bf16[8,8,2,1024]{3,2,1,0:T(2,128)(2,1)} %dot_general.24), kind=kOutput, calls=%fused_computation.4 | convolution fusion | flops 67108864 | bytes 1376256 | tf_op jit(solution)/shard_map/mjk,jnk->mn/dot_general | solution.py:1230
  54.0 3.4 %all-to-all-start.2 = ((f32[8,8,256]{2,1,0:T(8,128)}), f32[8,8,256]{2,1,0:T(8,128)S(1)}, u32[]{:S(2)}, u32[]{:S(2)}) async-start(f32[8,8,256]{2,1,0:T(8,128)} %convolution_bitcast_fusion), calls=%async_computation.2 | async-start | bytes 131072 | tf_op jit(solution)/shard_map/all_to_all | solution.py:1164
  57.4 0.8 reshape.121
  58.1 1.4 fusion
  59.6 3.6 %all-to-all-done.2 = f32[8,8,256]{2,1,0:T(8,128)S(1)} async-done(((f32[8,8,256]{2,1,0:T(8,128)}), f32[8,8,256]{2,1,0:T(8,128)S(1)}, u32[]{:S(2)}, u32[]{:S(2)}) %all-to-all-start.2) | async-done | bytes 65568 | tf_op jit(solution)/shard_map/all_to_all | solution.py:1164
  63.2 1.1 broadcast_in_dim.13
  64.3 3.7 %all-to-all-start.3 = ((bf16[4,2,64,1024]{3,2,1,0:T(8,128)(2,1)}), bf16[4,2,64,1024]{3,2,1,0:T(8,128)(2,1)S(1)}, u32[]{:S(2)}, u32[]{:S(2)}) async-start(bf16[4,2,64,1024]{3,2,1,0:T(8,128)(2,1)} %broadcast_in_dim.13), calls=%async_computation.3 | async-start | bytes 2097152 | tf_op jit(solution)/shard_map/all_to_all | solution.py:1164
  68.1 0.2 fusion.2
  68.3 0.1 reshape.120
  68.4 0.6 pad.32.logit_ref
  69.0 15.7 %shard_map.497 = (bf16[8,4,32,128]{3,2,1,0:T(8,128)(2,1)}, f32[8,256]{1,0:T(8,128)}, f32[32,128]{1,0:T(8,128)}, f32[16,128]{1,0:T(8,128)}, f32[200,128]{1,0:T(8,128)}) custom-call(s32[1]{0:T(128)} %bitcast.half_ref, bf16[17,4,16,128]{3,2,1,0:T(8,128)(2,1)} %get-tuple-element.66.x_ref, bf16[16,4,32,128]{3,2,1,0:T(8,128)(2,1)} %get-tuple-element.68.hid_ref, ...), custom_call_target="tpu_custom_call" | custom-call | flops 24000000000 | bytes 1024 | tf_op jit(solution)/shard_map/pallas_call | solution.py:1146
  84.7 0.8 convert_element_type.48
  85.5 0.7 broadcast_in_dim.14
  86.2 3.6 %all-to-all-start.4 = ((bf16[32,8,256]{2,1,0:T(8,128)(2,1)}), bf16[32,8,256]{2,1,0:T(8,128)(2,1)S(1)}, u32[]{:S(2)}, u32[]{:S(2)}) async-start(bf16[32,8,256]{2,1,0:T(8,128)(2,1)} %broadcast_in_dim.14), calls=%async_computation.4 | async-start | bytes 262144 | tf_op jit(solution)/shard_map/all_to_all | solution.py:1164
  89.8 8.2 %all-to-all-done.4 = bf16[32,8,256]{2,1,0:T(8,128)(2,1)S(1)} async-done(((bf16[32,8,256]{2,1,0:T(8,128)(2,1)}), bf16[32,8,256]{2,1,0:T(8,128)(2,1)S(1)}, u32[]{:S(2)}, u32[]{:S(2)}) %all-to-all-start.4) | async-done | bytes 131104 | tf_op jit(solution)/shard_map/all_to_all | solution.py:1164
  98.0 0.3 convolution_convert_fusion.2
  98.3 0.3 copy.91
  98.6 0.9 reshape.123
  99.4 3.6 %all-to-all-start.5 = ((bf16[8,8,16,128]{3,2,1,0:T(8,128)(2,1)}), bf16[8,8,16,128]{3,2,1,0:T(8,128)(2,1)S(1)}, u32[]{:S(2)}, u32[]{:S(2)}) async-start(bf16[8,8,16,128]{3,2,1,0:T(8,128)(2,1)} %reshape.123), calls=%async_computation.5 | async-start | bytes 524288 | tf_op jit(solution)/shard_map/all_to_all | solution.py:1164
  103.0 0.3 collective-permute-start
  103.4 9.1 %all-to-all-done.5.fc_ref = bf16[8,8,16,128]{3,2,1,0:T(8,128)(2,1)S(1)} async-done(((bf16[8,8,16,128]{3,2,1,0:T(8,128)(2,1)}), bf16[8,8,16,128]{3,2,1,0:T(8,128)(2,1)S(1)}, u32[]{:S(2)}, u32[]{:S(2)}) %all-to-all-start.5) | async-done | bytes 262176 | tf_op jit(solution)/shard_map/all_to_all | solution.py:1164
  112.5 0.3 fusion.15
  112.8 0.7 pad.34.dline_ref
  113.5 0.6 pad_maximum_fusion.dcond_ref
  114.2 0.7 copy-done.7
  114.8 0.1 copy-done.8
  114.9 13.8 %shard_map.498 = (bf16[9,4,128,128]{3,2,1,0:T(8,128)(2,1)}, f32[9,4,32,128]{3,2,1,0:T(8,128)}, f32[128,128]{1,0:T(8,128)}) custom-call(s32[1]{0:T(128)} %bitcast.half_ref, f32[16,4,128,128]{3,2,1,0:T(8,128)} %get-tuple-element.69.far_act_ref, f32[16,4,32,128]{3,2,1,0:T(8,128)} %get-tuple-element.70.far_cell_ref, ...), custom_call_target="tpu_custom_call" | custom-call | flops 80000000 | bytes 1024 | tf_op jit(solution)/shard_map/pallas_call | solution.py:1146
  128.8 12.5 %shard_map.499 = (bf16[32,64,128]{2,1,0:T(8,128)(2,1)}, f32[4000,128]{1,0:T(8,128)}) custom-call(s32[1]{0:T(128)} %bitcast.half_ref, bf16[17,4,16,128]{3,2,1,0:T(8,128)(2,1)} %get-tuple-element.66.x_ref, bf16[17,4,32,128]{3,2,1,0:T(8,128)(2,1)} %get-tuple-element.67.enc_ref, bf16[16,4,32,128]{3,2,1,0:T(8,128)(2,1)} %get-tuple-element.68.hid_ref, ...), custom_call_target="tpu_custom_call" | custom-call | flops 9600000000 | bytes 1024 | tf_op jit(solution)/shard_map/pallas_call | solution.py:1146
  141.3 19.7 %all_to_all.40.got_ref = bf16[32,64,128]{2,1,0:T(8,128)(2,1)} all-to-all(bf16[32,64,128]{2,1,0:T(8,128)(2,1)} %get-tuple-element.82), channel_id=1, replica_groups=mesh['clip'=4,'row'=8] {'clip','row'}, dimensions={0} | all-to-all | bytes 1048576 | tf_op jit(solution)/shard_map/all_to_all | solution.py:1164
  161.0 2.0 %shard_map.500 = (bf16[32,64,128]{2,1,0:T(8,128)(2,1)}, f32[1,128]{1,0:T(1,128)}) custom-call(bf16[32,64,128]{2,1,0:T(8,128)(2,1)} %all_to_all.40.got_ref), custom_call_target="tpu_custom_call" | custom-call | tf_op jit(solution)/shard_map/pallas_call | solution.py:1304
  162.9 2.6 %all-to-all-start.7 = ((bf16[32,64,128]{2,1,0:T(8,128)(2,1)}), bf16[32,64,128]{2,1,0:T(8,128)(2,1)S(1)}, u32[]{:S(2)}, u32[]{:S(2)}) async-start(bf16[32,64,128]{2,1,0:T(8,128)(2,1)} %get-tuple-element.84), calls=%async_computation.7 | async-start | bytes 1048576 | tf_op jit(solution)/shard_map/all_to_all | solution.py:1164
  165.6 1.3 fusion.19
  166.9 15.0 %all-to-all-done.7.got_ref = bf16[32,64,128]{2,1,0:T(8,128)(2,1)S(1)} async-done(((bf16[32,64,128]{2,1,0:T(8,128)(2,1)}), bf16[32,64,128]{2,1,0:T(8,128)(2,1)S(1)}, u32[]{:S(2)}, u32[]{:S(2)}) %all-to-all-start.7) | async-done | bytes 524320 | tf_op jit(solution)/shard_map/all_to_all | solution.py:1164
  181.9 0.8 copy-done.2
  182.7 9.6 %shard_map.501 = (f32[]{:T(128)}, f32[32,75]{1,0:T(8,128)}, f32[1600,128]{1,0:T(8,128)}, f32[4000,128]{1,0:T(8,128)}, f32[15,250]{1,0:T(8,128)}, /*index=5*/f32[...) custom-call(bf16[32,64,128]{2,1,0:T(8,128)(2,1)} %copy-done.2, ...), custom_call_target="tpu_custom_call" | custom-call | tf_op jit(solution)/shard_map/pallas_call | solution.py:1331
  (46 shorter events, 0.2 us)
Async XLA Ops:
  0.7 10.0 %copy-start.14 = (f32[517]{0:T(1024)S(1)}, f32[517]{0:T(1024)}, u32[]{:S(2)}) copy-start(f32[517]{0:T(1024)} %refs_6_.1) | copy-start | bytes 6208
  0.7 10.8 %copy-start = (f32[2,250,1024]{2,0,1:T(2,128)S(1)}, f32[2,250,1024]{2,0,1:T(2,128)}, u32[]{:S(2)}) copy-start(f32[2,250,1024]{2,0,1:T(2,128)} %param.41) | copy-start | bytes 6144004
  4.3 16.8 %all-to-all-start = ((bf16[8,144,128]{2,1,0:T(8,128)(2,1)}), bf16[8,144,128]{2,1,0:T(8,128)(2,1)S(1)}, u32[]{:S(2)}, u32[]{:S(2)}) async-start(bf16[8,144,128]{2,1,0:T(8,128)(2,1)} %bitcast.4), calls=%async_computation | async-start | bytes 589824 | tf_op jit(solution)/shard_map/all_to_all | solution.py:1164
  11.4 2.0 %copy-start.18 = (s32[4,16,2]{1,2,0:T(2,128)S(1)}, s32[4,16,2]{1,2,0:T(2,128)}, u32[]{:S(2)}) copy-start(s32[4,16,2]{1,2,0:T(2,128)} %param.35) | copy-start | bytes 1540
  11.4 2.0 %copy-start.16 = (f32[4,16,3]{1,0,2:T(4,128)S(1)}, f32[4,16,3]{1,0,2:T(4,128)}, u32[]{:S(2)}) copy-start(f32[4,16,3]{1,0,2:T(4,128)} %param.37) | copy-start | bytes 2308
  11.4 2.1 %copy-start.15 = (f32[4,16,4]{1,2,0:T(4,128)S(1)}, f32[4,16,4]{1,2,0:T(4,128)}, u32[]{:S(2)}) copy-start(f32[4,16,4]{1,2,0:T(4,128)} %param.36) | copy-start | bytes 3076
  11.4 2.2 %slice-start = ((f32[517]{0:T(1024)}), f32[224]{0:T(256)S(1)}, s32[]{:S(2)}) async-start(f32[517]{0:T(1024)} %refs_6_.1), calls=%async_computation.8 | async-start | bytes 2048 | tf_op jit(solution)/shard_map/slice | solution.py:1206
  11.4 2.4 %copy-start.11 = (f32[75,32]{0,1:T(8,128)S(1)}, f32[75,32]{0,1:T(8,128)}, u32[]{:S(2)}) copy-start(f32[75,32]{0,1:T(8,128)} %param.39) | copy-start | bytes 28804
  11.5 2.4 %copy-start.13 = (bf16[144,75]{1,0:T(8,128)(2,1)S(1)}, bf16[144,75]{1,0:T(8,128)(2,1)}, u32[]{:S(2)}) copy-start(bf16[144,75]{1,0:T(8,128)(2,1)} %constant.62.clone) | copy-start | bytes 64804
  21.1 0.8 copy-start.5
  21.8 19.8 %copy-start.1 = (bf16[1024,1024,1]{1,0,2:T(8,128)(2,1)S(1)}, bf16[1024,1024,1]{1,0,2:T(8,128)(2,1)}, u32[]{:S(2)}) copy-start(bf16[1024,1024,1]{1,0,2:T(8,128)(2,1)} %constant.87) | copy-start | bytes 6291460
  38.1 13.1 %all-to-all-start.1 = ((bf16[8,8,16,128]{3,2,1,0:T(8,128)(2,1)}), bf16[8,8,16,128]{3,2,1,0:T(8,128)(2,1)S(1)}, u32[]{:S(2)}, u32[]{:S(2)}) async-start(bf16[8,8,16,128]{3,2,1,0:T(8,128)(2,1)} %get-tuple-element.71), calls=%async_computation.1 | async-start | bytes 524288 | tf_op jit(solution)/shard_map/all_to_all | solution.py:1164
  54.0 9.2 %all-to-all-start.2 = ((f32[8,8,256]{2,1,0:T(8,128)}), f32[8,8,256]{2,1,0:T(8,128)S(1)}, u32[]{:S(2)}, u32[]{:S(2)}) async-start(f32[8,8,256]{2,1,0:T(8,128)} %convolution_bitcast_fusion), calls=%async_computation.2 | async-start | bytes 131072 | tf_op jit(solution)/shard_map/all_to_all | solution.py:1164
  59.5 8.5 %copy-start.19 = (f32[4,8]{1,0:T(4,128)S(1)}, f32[4,8]{1,0:T(4,128)}, u32[]{:S(2)}) copy-start(f32[4,8]{1,0:T(4,128)} %param.38) | copy-start | bytes 388
  59.6 8.5 %copy-start.12 = (f32[15,250]{1,0:T(8,128)S(1)}, f32[15,250]{1,0:T(8,128)}, u32[]{:S(2)}) copy-start(f32[15,250]{1,0:T(8,128)} %refs_3_.1) | copy-start | bytes 45004
  59.6 8.5 %copy-start.17 = (f32[250]{0:T(256)S(1)}, f32[250]{0:T(256)}, u32[]{:S(2)}) copy-start(f32[250]{0:T(256)} %slice.42) | copy-start | bytes 3004
  64.3 20.4 %all-to-all-start.3 = ((bf16[4,2,64,1024]{3,2,1,0:T(8,128)(2,1)}), bf16[4,2,64,1024]{3,2,1,0:T(8,128)(2,1)S(1)}, u32[]{:S(2)}, u32[]{:S(2)}) async-start(bf16[4,2,64,1024]{3,2,1,0:T(8,128)(2,1)} %broadcast_in_dim.13), calls=%async_computation.3 | async-start | bytes 2097152 | tf_op jit(solution)/shard_map/all_to_all | solution.py:1164
  84.7 18.3 %copy-start.6 = (bf16[8,4,32,128]{3,2,1,0:T(8,128)(2,1)S(1)}, bf16[8,4,32,128]{3,2,1,0:T(8,128)(2,1)}, u32[]{:S(2)}) copy-start(bf16[8,4,32,128]{3,2,1,0:T(8,128)(2,1)} %get-tuple-element.72.dec_ref) | copy-start | bytes 786436
  84.7 27.8 %copy-start.10 = (f32[8,256]{1,0:T(8,128)S(1)}, f32[8,256]{1,0:T(8,128)}, u32[]{:S(2)}) copy-start(f32[8,256]{1,0:T(8,128)} %get-tuple-element.74) | copy-start | bytes 24580
  84.7 44.0 %copy-start.4 = (bf16[4,2,64,1024]{3,2,1,0:T(8,128)(2,1)}, bf16[4,2,64,1024]{3,2,1,0:T(8,128)(2,1)S(1)}, u32[]{:S(2)}) copy-start(bf16[4,2,64,1024]{3,2,1,0:T(8,128)(2,1)S(1)} %all-to-all-done.3.far_hid_ref) | copy-start | bytes 3145732
  86.2 11.8 %all-to-all-start.4 = ((bf16[32,8,256]{2,1,0:T(8,128)(2,1)}), bf16[32,8,256]{2,1,0:T(8,128)(2,1)S(1)}, u32[]{:S(2)}, u32[]{:S(2)}) async-start(bf16[32,8,256]{2,1,0:T(8,128)(2,1)} %broadcast_in_dim.14), calls=%async_computation.4 | async-start | bytes 262144 | tf_op jit(solution)/shard_map/all_to_all | solution.py:1164
  98.0 30.8 %copy-start.9 = (bf16[32,8,256]{2,1,0:T(8,128)(2,1)}, bf16[32,8,256]{2,1,0:T(8,128)(2,1)S(1)}, u32[]{:S(2)}) copy-start(bf16[32,8,256]{2,1,0:T(8,128)(2,1)S(1)} %all-to-all-done.4) | copy-start | bytes 393220
  99.4 13.1 %all-to-all-start.5 = ((bf16[8,8,16,128]{3,2,1,0:T(8,128)(2,1)}), bf16[8,8,16,128]{3,2,1,0:T(8,128)(2,1)S(1)}, u32[]{:S(2)}, u32[]{:S(2)}) async-start(bf16[8,8,16,128]{3,2,1,0:T(8,128)(2,1)} %reshape.123), calls=%async_computation.5 | async-start | bytes 524288 | tf_op jit(solution)/shard_map/all_to_all | solution.py:1164
  103.0 11.1 %collective-permute-start = (bf16[8,4,32,128]{3,2,1,0:T(8,128)(2,1)S(1)}, bf16[8,4,32,128]{3,2,1,0:T(8,128)(2,1)S(1)}, u32[]{:S(2)}, u32[]{:S(2)}) collective-permute-start(bf16[8,4,32,128]{3,2,1,0:T(8,128)(2,1)S(1)} %copy-done.6), channel_id=1, source_target_pairs={{0,1},{1,0},{2,3},{3,2},{4,5},{5,4},{6,7},{7,6},{8,9},{9,8},{10,11... | collective-permute-start | bytes 786440 | tf_op jit(solution)/shard_map/ppermute | solution.py:1281
  112.5 1.6 copy-start.3
  112.5 1.6 collective-permute-start.1
  114.1 0.7 copy-start.7
  114.1 0.8 copy-start.8
  162.9 19.0 %all-to-all-start.7 = ((bf16[32,64,128]{2,1,0:T(8,128)(2,1)}), bf16[32,64,128]{2,1,0:T(8,128)(2,1)S(1)}, u32[]{:S(2)}, u32[]{:S(2)}) async-start(bf16[32,64,128]{2,1,0:T(8,128)(2,1)} %get-tuple-element.84), calls=%async_computation.7 | async-start | bytes 1048576 | tf_op jit(solution)/shard_map/all_to_all | solution.py:1164
  181.9 0.8 copy-start.2

commit v6 on v5

--- a/solution.py
+++ b/solution.py
@@ -631,8 +631,8 @@
 
 
 def head_kernel(
-    half_ref, x_ref, hid_ref, logit_ref, w_ref, mask_ref, bias_ref, place_ref, placet_ref,
-    back_ref, dlog_ref, dwd_ref, dwm_ref, sums_ref,
+    half_ref, x_ref, hid_ref, logit_ref, w_ref, mask_ref, bias_ref, place_ref, placet_ref, cond_ref,
+    back_ref, dlog_ref, dwd_ref, dwm_ref, sums_ref, copies_ref, dcond_ref,
     even_s, odd_s, wd_ref, wdt_ref, wm_ref, wmt_ref, over_ref, wide_s, everywhere_s, turned_s, d_even_s, d_odd_s,
     d_spot_s, kernel_s, d_logit_s,
 ):
@@ -757,6 +757,12 @@
         place = ((tap < KK) & (lane == kernel * KK + tap)).astype(F32)
         total = total + nn_exact(d_logit_s[pl.ds(kernel + 1, own, stride=16), :], place)
     dlog_ref[...] = total
+    low = total.astype(BF)
+    for device in range(copies_ref.shape[0]):
+        copies_ref[device] = low
+    d_cond = nn_exact(cond_ref[...], total)
+    dcond_ref[0:16] = d_cond[:, :LANES]
+    dcond_ref[16:32] = d_cond[:, LANES:]
     row = lax.broadcasted_iota(jnp.int32, (64, 4 * C), 0)
     lane = lax.broadcasted_iota(jnp.int32, (64, 4 * C), 1)
     own_block = jnp.where(row // 16 == lane // C, wide_s[...], 0.0)
@@ -909,12 +915,14 @@
     return place
 
 
-def logit_map_gradient(hid_ref, sum_ref, out_ref, turned_s):
+def logit_map_gradient(clip_group, hid_ref, sum_ref, out_ref, turned_s):
     logits = NK * KK
     groups, items, width = sum_ref.shape
     eye = one_hot_eye(width)
     for group in range(groups):
-        turned_s[:, group * items : (group + 1) * items] = nt(eye, sum_ref[group]).astype(BF)
+        turned_s[:, group * items : (group + 1) * items] = nt(
+            eye, sum_ref[lax.rem(clip_group + groups - group, groups)]
+        ).astype(BF)
     squares = jnp.zeros((1, LANES), F32)
     stride = 2 * WB * C // LANES
     for row in range(2):
@@ -932,12 +940,17 @@
 
 def pack_kernel(
     half_ref, x_ref, enc_ref, hid_ref, keep_ref, denc_ref, lines_ref, head_ref, ddec_ref, dmask_ref, dcond_ref,
-    dline_ref, far_hid_ref, sum_ref, we_ref, bias_ref, place_ref, encoder_ref,
-    block_ref, far_dfc_ref,
-    win_s, join_s, dwe_s, sums_s, packed_s, every_s, dfc_s, turned_s, sems,
+    dline_ref, sum_ref, we_ref, bias_ref, place_ref, encoder_ref, *rest,
 ):
-    every_copy = pltpu.make_async_copy(far_hid_ref, every_s, sems.at[0])
-    every_copy.start()
+    groups = sum_ref.shape[0]
+    far_hids = rest[:groups]
+    (block_ref, far_dfc_ref, win_even_s, win_odd_s, join_even_s, join_odd_s, dwe_s, sums_s, packed_s, every_s,
+     dfc_s, turned_s, sems) = rest[groups:]
+    hid_copies = [
+        pltpu.make_async_copy(far_hid, every_s.at[group], sems.at[1 + group]) for group, far_hid in enumerate(far_hids)
+    ]
+    for copy in hid_copies:
+        copy.start()
     own = keep_ref.shape[0] - 1
     base = half_ref[0] * own
     lanes = lane_places()
@@ -945,7 +958,7 @@
     sums_s[...] = jnp.zeros_like(sums_s)
     packed_s[...] = jnp.zeros_like(packed_s)
 
-    def gather(i, _):
+    def gather(i, win_s, join_s):
         t = base + i
         earlier = jnp.maximum(t - 1, 0)
         started = jnp.where(t > 0, 1.0, 0.0)
@@ -979,12 +992,17 @@
             sums_s[C : 2 * C] += d_gain[:, :LANES] + d_gain[:, LANES:]
             sums_s[2 * C : 3 * C] += d_value[:, :LANES] + d_value[:, LANES:]
             dwe_s[...] += nt(d_pre.astype(BF), window)
+
+    def gather_two(pair, _):
+        gather(2 * pair, win_even_s, join_even_s)
+        gather(2 * pair + 1, win_odd_s, join_odd_s)
         return 0
 
-    lax.fori_loop(0, own, gather, 0)
-    every_copy.wait()
-    squares = logit_map_gradient(every_s, sum_ref, dfc_s, turned_s)
-    dfc_copy = pltpu.make_async_copy(dfc_s, far_dfc_ref, sems.at[1])
+    lax.fori_loop(0, own // 2, gather_two, 0)
+    for copy in hid_copies:
+        copy.wait()
+    squares = logit_map_gradient(half_ref[1], every_s, sum_ref, dfc_s, turned_s)
+    dfc_copy = pltpu.make_async_copy(dfc_s, far_dfc_ref, sems.at[0])
     dfc_copy.start()
     packed_s[ROW_DEC:ROW_COND] = ddec_ref[...]
     packed_s[ROW_COND:ROW_ENC] = dcond_ref[...]
@@ -993,7 +1011,9 @@
     ones = jnp.ones((8, LANES), F32)
     sums_s[3 * C : 7 * C] = lines_ref[...]
     sums_s[7 * C : 11 * C + 64] = head_ref[0:192]
-    line = nn_exact(nt_exact(ones, sums_s[...]), place_ref[...].astype(F32))[0:1] + jnp.sum(dline_ref[...], 0, keepdims=True)
+    line = nn_exact(nt_exact(ones, sums_s[...]), place_ref[...].astype(F32))[0:1]
+    logit_line = jnp.concatenate([dline_ref[...], jnp.zeros((dline_ref.shape[0], 3 * LANES), F32)], axis=1)
+    line = line + pltpu.roll(jnp.sum(logit_line, 0, keepdims=True), 7 * C, 1)
     packed_s[ROW_VECTOR : ROW_VECTOR + 8] = jnp.concatenate(
         [line[:, place * LANES : (place + 1) * LANES] for place in range(5)] + [jnp.zeros((3, LANES), F32)], axis=0
     )
@@ -1229,7 +1249,6 @@
     strip_hid = exchange(strips_out, "row").reshape(items, 2, WB * C)
     parts = jnp.einsum("mjk,jnk->mn", strip_hid, k_fc, preferred_element_type=F32)
     strip_hid = jnp.einsum("mjk,kl->jml", strip_hid, order, preferred_element_type=F32).astype(BF)
-    strip_hid_all = to_all(strip_hid, "clip")
     summed = jnp.sum(exchange(parts.reshape(count, own, 2 * LANES), "row"), 0)[:, : NK * KK]
     presence = flags.astype(F32)
     conditions = jnp.concatenate(
@@ -1245,12 +1264,14 @@
     logits = jnp.pad(
         logits.reshape(own, NK, KK), ((0, 0), (1, 5), (0, 32 - KK)), constant_values=-1e30
     )
-    dec, d_logit, d_dec, d_mask, head_sums = call(
+    both = ("clip", "row")
+    devices = lax.axis_size(both)
+    dec, d_logit, d_dec, d_mask, head_sums, sent, d_cond = call(
         head_kernel,
         30,
         [
             ((own, TILES, C, LANES), BF), ((own, 2 * LANES), F32), ((C, 4 * C), F32), ((16, LANES), F32),
-            ((200, LANES), F32),
+            ((200, LANES), F32), ((devices, own, 2 * LANES), BF), ((32, LANES), F32),
         ],
         [
             ((6, 48, LANES), F32), ((6, 48, LANES), F32), ((C, 4 * C), BF), ((4 * C, C), BF), ((64, 12 * C), BF),
@@ -1260,13 +1281,18 @@
             ((own, 16, 32), F32), ((own * 16, 32), F32),
         ],
         half_1, x, hid, logits, w_deconv, w_mask.T, bias,
-        jnp.asarray(places, BF), jnp.asarray(places.transpose(0, 2, 1), BF),
-    )
-    d_logit, strip_hid_all = lax.optimization_barrier((d_logit, strip_hid_all))
-    every_sum = to_all(d_logit.astype(BF), ("clip", "row")).reshape(-1, items, 2 * LANES)
+        jnp.asarray(places, BF), jnp.asarray(places.transpose(0, 2, 1), BF), jnp.pad(cond.T, ((0, 16 - COND), (0, 0))),
+    )
+    groups = lax.axis_size("clip")
+    routes = [[(i, (i + step) % groups) for i in range(groups)] for step in range(1, groups)]
+    strip_hids = [strip_hid] + [lax.ppermute(strip_hid, "clip", route) for route in routes]
+    every_sum = exchange(sent, both)
+    every_sum, strip_hids[1] = lax.optimization_barrier((every_sum, strip_hids[1]))
+    every_sum = every_sum.reshape(-1, items, 2 * LANES)
     d_sum = lax.dynamic_index_in_dim(every_sum, lax.axis_index("clip"), 0, False)
     back_fc = jnp.einsum("mn,jnk->mjk", d_sum, k_fc, preferred_element_type=F32).astype(BF)
     back_fc = exchange(back_fc.reshape(count, own, 16, LANES), "row")
+    back_fc, strip_hids[3] = lax.optimization_barrier((back_fc, strip_hids[3]))
     swap = [(index, index ^ 1) for index in range(count)]
 
     keep, d_enc, lines = call(
@@ -1281,25 +1307,20 @@
         half_1, act, cell, dec, lax.ppermute(dec, "row", swap), back_fc, lax.ppermute(back_fc, "row", swap), w_lstm,
         far_in=(0, 1),
     )
-    d_cond = jnp.dot(cond.T, d_logit, precision=HIGH)
-    d_cond = jnp.pad(d_cond, ((0, 16 - COND), (0, 0)))
-    d_cond = jnp.concatenate([d_cond[:, :LANES], d_cond[:, LANES:]], axis=0)
-    d_line = jnp.pad(d_logit[:, : NK * KK], ((0, 0), (7 * C, 5 * LANES - 7 * C - NK * KK)))
-    both = ("clip", "row")
-    devices = lax.axis_size(both)
     block, d_fc = call(
         pack_kernel,
         12,
         [((devices, PART, LANES), BF), ((w_fc.size // LANES, LANES), F32)],
         [
-            ((6, 48, LANES), BF), ((8, KS * 2 * C, LANES), BF), ((C, WIN), F32), ((11 * C + 64, LANES), F32),
-            ((ROWS, LANES), F32), (strip_hid_all.shape, BF), ((w_fc.size // LANES, LANES), F32),
-            ((2 * LANES, strip_hid_all.shape[0] * items), BF), (None, (2,)),
+            ((6, 48, LANES), BF), ((6, 48, LANES), BF), ((8, KS * 2 * C, LANES), BF), ((8, KS * 2 * C, LANES), BF),
+            ((C, WIN), F32), ((11 * C + 64, LANES), F32),
+            ((ROWS, LANES), F32), ((groups,) + strip_hid.shape, BF), ((w_fc.size // LANES, LANES), F32),
+            ((2 * LANES, groups * items), BF), (None, (1 + groups,)),
         ],
-        half_1, x, enc, hid, keep, d_enc, lines, head_sums, d_dec, d_mask, d_cond, d_line, strip_hid_all, every_sum,
+        jnp.stack([half, lax.axis_index("clip")]).astype(jnp.int32), x, enc, hid, keep, d_enc, lines, head_sums, d_dec, d_mask, d_cond, d_logit, every_sum,
         wide_enc, bias,
-        jnp.asarray(vector_places(), BF), jnp.asarray(np.pad(encoder, ((0, 0), (0, LANES - KK * 3))), F32),
-        far_in=(11,), far_out=(1,),
+        jnp.asarray(vector_places(), BF), jnp.asarray(np.pad(encoder, ((0, 0), (0, LANES - KK * 3))), F32), *strip_hids,
+        far_in=tuple(range(16, 16 + groups)), far_out=(1,),
     )
     sums, scalars = pl.pallas_call(
         total_kernel,
@@ -1351,7 +1372,9 @@
     clips, _, _, strip_rows, width = frames.shape
     count = lax.axis_size("row")
     one_clip = strip_rows * count // 2 == TILES * BANDS and width // 2 == WB
-    if one_clip and clips * HALVES == count:
+    devices = lax.axis_size(("clip", "row"))
+    even = ROW_DEC % devices == 0 and SMALL % devices == 0
+    if one_clip and clips * HALVES == count and even and (ROW_DEC + 2 * SMALL) // devices + 3 <= PART:
         return whole_clips(frames, *rest)
     return strips(frames, *rest)
 

time: 194 us -> 189 us (0.974)
  waiting for transfers between devices: 49.6 us -> 47.2 us
    all_to_all x7 -> x6, waiting for transfers between devices: 49.6 us -> 39.6 us  [exchange(): return lax.all_to_all(block, axes, 0, 0, tiled=True)]
    ppermute x0 -> x3, waiting for transfers between devices: none -> 7.5 us  [whole_clips(): lax.ppermute(strip_hid, 'clip', route)]
    all_to_all x7 -> x6, starting transfers between devices: 26.6 us -> 22.3 us  [exchange(): return lax.all_to_all(block, axes, 0, 0, tiled=True)]
    ppermute x0 -> x3, starting transfers between devices: none -> 3.58 us  [whole_clips(): lax.ppermute(strip_hid, 'clip', route)]
  transfers between devices with their start and end apart: 9 -> 11, of which waited for: 6 -> 8; matrix products, arithmetic and copies ran while one was open for 6% -> 6% of each run, Pallas kernels for 8% -> 16%
where the time goes in v6:
time: 189 us; the launch traced here: 188 us
  Pallas kernels  70.2 us (37%)
  waiting for transfers between devices  47.2 us (25%)
  starting transfers between devices  25.8 us (14%)
  blocking collectives  21.2 us (11%)
  local copies, waits for them, and re-layouts  12.2 us (6%)
  matrix products  7.13 us (4%)
  other arithmetic  2.99 us (2%)
    pallas_call x4, Pallas kernels, call(): pl.pallas_call(kernel, cost_estimate=cost(micros), out_shape=[jax.ShapeDt...  58.7 us
    all_to_all x6, waiting for transfers between devices, exchange(): return lax.all_to_all(block, axes, 0, 0, tiled=True)  39.6 us
    all_to_all x6, starting transfers between devices, exchange(): return lax.all_to_all(block, axes, 0, 0, tiled=True)  22.3 us
    all_to_all x1, blocking collectives, exchange(): return lax.all_to_all(block, axes, 0, 0, tiled=True)  21.2 us
    pallas_call x1, Pallas kernels, whole_clips(): pl.pallas_call(functools.partial(update_kernel, rates), out_shape=[jax.Sh...  9.6 us
    ppermute x3, waiting for transfers between devices, whole_clips(): lax.ppermute(strip_hid, 'clip', route)  7.5 us
  transfers between devices with their start and end apart: 11, of which 8 were waited for; matrix products, arithmetic and copies ran while one was open for 6% of the time, Pallas kernels for 16%

profile of v6, /device:TPU:0, one launch (start us, length us, event | category | flops | bytes accessed | tf_op | source)
XLA Modules:
  0.0 188.0 jit_solution(5526741076932229891)
XLA Ops:
  0.7 0.0 copy-start.13
  0.7 0.0 copy-start.11
  0.7 1.1 copy.86
  1.8 0.9 convert_element_type.34
  2.9 0.5 maximum_bitcast_fusion
  3.3 0.1 reshape.113
  3.5 0.8 broadcast_in_dim.6
  4.3 6.3 %all-to-all-start = ((bf16[8,144,128]{2,1,0:T(8,128)(2,1)}), bf16[8,144,128]{2,1,0:T(8,128)(2,1)S(1)}, u32[]{:S(2)}, u32[]{:S(2)}) async-start(bf16[8,144,128]{2,1,0:T(8,128)(2,1)} %bitcast.5), calls=%async_computation | async-start | bytes 589824 | tf_op jit(solution)/shard_map/all_to_all | solution.py:1184
  10.6 0.1 slice.28
  10.7 0.1 slice.29
  10.8 0.1 copy.91
  10.9 0.1 copy.90
  11.0 0.1 select_maximum_fusion
  11.0 0.1 broadcast_multiply_fusion
  11.1 0.8 fusion.1.we_ref
  11.9 9.1 %all-to-all-done.raw_ref = bf16[8,144,128]{2,1,0:T(8,128)(2,1)S(1)} async-done(((bf16[8,144,128]{2,1,0:T(8,128)(2,1)}), bf16[8,144,128]{2,1,0:T(8,128)(2,1)S(1)}, u32[]{:S(2)}, u32[]{:S(2)}) %all-to-all-start) | async-done | bytes 294944 | tf_op jit(solution)/shard_map/all_to_all | solution.py:1184
  21.0 0.8 broadcast_in_dim.7.bias_ref
  21.8 16.3 %shard_map.496 = (bf16[17,4,16,128]{3,2,1,0:T(8,128)(2,1)}, bf16[17,4,32,128]{3,2,1,0:T(8,128)(2,1)}, bf16[16,4,32,128]{3,2,1,0:T(8,128)(2,1)}, f32[16,4,128,128...) custom-call(s32[1]{0:T(128)} %bitcast.half_ref, bf16[8,144,128]{2,1,0:T(8,128)(2,1)} %copy-done.4, ...), custom_call_target="tpu_custom_call" | custom-call | flops 16000000000 | bytes 1024 | tf_op jit(solution)/shard_map/pallas_call | solution.py:1166
  38.1 3.4 %all-to-all-start.1 = ((bf16[8,8,16,128]{3,2,1,0:T(8,128)(2,1)}), bf16[8,8,16,128]{3,2,1,0:T(8,128)(2,1)S(1)}, u32[]{:S(2)}, u32[]{:S(2)}) async-start(bf16[8,8,16,128]{3,2,1,0:T(8,128)(2,1)} %get-tuple-element.75), calls=%async_computation.1 | async-start | bytes 524288 | tf_op jit(solution)/shard_map/all_to_all | solution.py:1184
  41.5 0.1 broadcast_multiply_fusion.1
  41.6 0.1 slice.33
  41.7 0.7 convert_element_type.37
  42.4 0.0 copy-start.1
  42.4 1.2 copy.102
  43.6 0.1 fusion.12
  43.7 0.1 copy.92
  43.8 0.6 pad.29.cond_ref
  44.4 2.5 %convolution_convert_fusion = bf16[2,256,1024]{2,1,0:T(8,128)(2,1)S(1)} fusion(bf16[1024,1024,1]{1,0,2:T(8,128)(2,1)S(1)} %copy-done.1, bf16[2,250,1024]{2,1,0:T(8,128)(2,1)} %copy.102), kind=kOutput, calls=%fused_computation | convolution fusion | flops 1074266112 | bytes 4169728 | tf_op jit(solution)/shard_map/jnl,kl->jnk/dot_general | solution.py:1248
  46.9 4.2 %all-to-all-done.1 = bf16[8,8,16,128]{3,2,1,0:T(8,128)(2,1)S(1)} async-done(((bf16[8,8,16,128]{3,2,1,0:T(8,128)(2,1)}), bf16[8,8,16,128]{3,2,1,0:T(8,128)(2,1)S(1)}, u32[]{:S(2)}, u32[]{:S(2)}) %all-to-all-start.1) | async-done | bytes 262176 | tf_op jit(solution)/shard_map/all_to_all | solution.py:1184
  51.2 0.8 dot_general.21
  52.0 2.0 %convolution_bitcast_fusion = f32[8,8,256]{2,1,0:T(8,128)} fusion(bf16[2,256,1024]{2,1,0:T(8,128)(2,1)S(1)} %convolution_convert_fusion, bf16[8,8,2,1024]{3,2,1,0:T(2,128)(2,1)} %dot_general.21), kind=kOutput, calls=%fused_computation.4 | convolution fusion | flops 67108864 | bytes 1376256 | tf_op jit(solution)/shard_map/mjk,jnk->mn/dot_general | solution.py:1250
  54.0 3.4 %all-to-all-start.2 = ((f32[8,8,256]{2,1,0:T(8,128)}), f32[8,8,256]{2,1,0:T(8,128)S(1)}, u32[]{:S(2)}, u32[]{:S(2)}) async-start(f32[8,8,256]{2,1,0:T(8,128)} %convolution_bitcast_fusion), calls=%async_computation.2 | async-start | bytes 131072 | tf_op jit(solution)/shard_map/all_to_all | solution.py:1184
  57.4 0.8 reshape.116
  58.1 1.4 fusion.rest_0_
  59.5 1.5 collective-permute-start.1
  61.1 2.1 %all-to-all-done.2 = f32[8,8,256]{2,1,0:T(8,128)S(1)} async-done(((f32[8,8,256]{2,1,0:T(8,128)}), f32[8,8,256]{2,1,0:T(8,128)S(1)}, u32[]{:S(2)}, u32[]{:S(2)}) %all-to-all-start.2) | async-done | bytes 65568 | tf_op jit(solution)/shard_map/all_to_all | solution.py:1184
  63.2 0.1 fusion.2
  63.4 0.1 reshape.115
  63.5 0.6 pad.28.logit_ref
  64.1 15.9 %shard_map.497 = (bf16[8,4,32,128]{3,2,1,0:T(8,128)(2,1)}, f32[8,256]{1,0:T(8,128)}, f32[32,128]{1,0:T(8,128)}, f32[16,128]{1,0:T(8,128)}, f32[200,128]{1,0:T(8,...) custom-call(s32[1]{0:T(128)} %bitcast.half_ref, bf16[17,4,16,128]{3,2,1,0:T(8,128)(2,1)} %get-tuple-element.70.x_ref, ...), custom_call_target="tpu_custom_call" | custom-call | flops 24000000000 | bytes 1024 | tf_op jit(solution)/shard_map/pallas_call | solution.py:1166
  80.1 3.1 %all-to-all-start.3 = ((bf16[32,8,256]{2,1,0:T(8,128)(2,1)}), bf16[32,8,256]{2,1,0:T(8,128)(2,1)S(1)}, u32[]{:S(2)}, u32[]{:S(2)}) async-start(bf16[32,8,256]{2,1,0:T(8,128)(2,1)} %get-tuple-element.77), calls=%async_computation.3 | async-start | bytes 262144 | tf_op jit(solution)/shard_map/all_to_all | solution.py:1184
  83.2 8.1 %all-to-all-done.3 = bf16[32,8,256]{2,1,0:T(8,128)(2,1)S(1)} async-done(((bf16[32,8,256]{2,1,0:T(8,128)(2,1)}), bf16[32,8,256]{2,1,0:T(8,128)(2,1)S(1)}, u32[]{:S(2)}, u32[]{:S(2)}) %all-to-all-start.3) | async-done | bytes 131104 | tf_op jit(solution)/shard_map/all_to_all | solution.py:1184
  91.4 0.3 convolution_convert_fusion.2
  91.7 0.3 copy.94
  92.0 0.9 reshape.118
  92.8 3.4 %all-to-all-start.4 = ((bf16[8,8,16,128]{3,2,1,0:T(8,128)(2,1)}), bf16[8,8,16,128]{3,2,1,0:T(8,128)(2,1)S(1)}, u32[]{:S(2)}, u32[]{:S(2)}) async-start(bf16[8,8,16,128]{3,2,1,0:T(8,128)(2,1)} %reshape.118), calls=%async_computation.4 | async-start | bytes 524288 | tf_op jit(solution)/shard_map/all_to_all | solution.py:1184
  96.3 1.2 collective-permute-start.2
  97.5 7.5 %collective-permute-done.2.rest_3_ = bf16[2,64,1024]{2,1,0:T(8,128)(2,1)S(1)} collective-permute-done((bf16[2,64,1024]{2,1,0:T(8,128)(2,1)S(1)}, bf16[2,64,1024]{2,1,0:T(8,128)(2,1)S(1)}, u32[]{:S(2)}, u32[]{:S(2)}) %collective-permute-start.2) | collective-permute-done | bytes 262176 | tf_op jit(solution)/shard_map/ppermute | solution.py:1288
  105.0 0.9 all-to-all-done.4.fc_ref
  105.9 0.8 collective-permute-start.4
  106.8 0.6 pad_add_fusion.half_ref
  107.3 0.1 collective-permute-done.3.other_fc_ref
  107.5 0.6 copy-done.6
  108.1 0.1 copy-done.7
  108.1 13.8 %shard_map.498 = (bf16[9,4,128,128]{3,2,1,0:T(8,128)(2,1)}, f32[9,4,32,128]{3,2,1,0:T(8,128)}, f32[128,128]{1,0:T(8,128)}) custom-call(s32[1]{0:T(128)} %bitcast.half_ref, f32[16,4,128,128]{3,2,1,0:T(8,128)} %get-tuple-element.73.far_act_ref, f32[16,4,32,128]{3,2,1,0:T(8,128)} %get-tuple-element.74.far_cell_ref, ...), custom_call_target="tpu_custom_call" | custom-call | flops 80000000 | bytes 1024 | tf_op jit(solution)/shard_map/pallas_call | solution.py:1166
  122.0 0.7 copy-done.21
  122.7 12.6 %shard_map.499 = (bf16[32,64,128]{2,1,0:T(8,128)(2,1)}, f32[4000,128]{1,0:T(8,128)}) custom-call(s32[2]{0:T(128)} %pad_add_fusion.half_ref, bf16[17,4,16,128]{3,2,1,0:T(8,128)(2,1)} %get-tuple-element.70.x_ref, bf16[17,4,32,128]{3,2,1,0:T(8,128)(2,1)} %get-tuple-element.71.enc_ref, bf16[16,4,32,128]{3,2,1,0:T(8,128)(2,1)} %get-tuple-element.72.hid_ref, ...), custom_call_target="tpu_custom_call" | custom-call | flops 9600000000 | bytes 1024 | tf_op jit(solution)/shard_map/pallas_call | solution.py:1166
  135.3 21.2 %all_to_all.35.got_ref = bf16[32,64,128]{2,1,0:T(8,128)(2,1)} all-to-all(bf16[32,64,128]{2,1,0:T(8,128)(2,1)} %get-tuple-element.90), channel_id=1, replica_groups=mesh['clip'=4,'row'=8] {'clip','row'}, dimensions={0} | all-to-all | bytes 1048576 | tf_op jit(solution)/shard_map/all_to_all | solution.py:1184
  156.6 2.0 %shard_map.500 = (bf16[32,64,128]{2,1,0:T(8,128)(2,1)}, f32[1,128]{1,0:T(1,128)}) custom-call(bf16[32,64,128]{2,1,0:T(8,128)(2,1)} %all_to_all.35.got_ref), custom_call_target="tpu_custom_call" | custom-call | tf_op jit(solution)/shard_map/pallas_call | solution.py:1325
  158.5 2.6 %all-to-all-start.6 = ((bf16[32,64,128]{2,1,0:T(8,128)(2,1)}), bf16[32,64,128]{2,1,0:T(8,128)(2,1)S(1)}, u32[]{:S(2)}, u32[]{:S(2)}) async-start(bf16[32,64,128]{2,1,0:T(8,128)(2,1)} %get-tuple-element.92), calls=%async_computation.6 | async-start | bytes 1048576 | tf_op jit(solution)/shard_map/all_to_all | solution.py:1184
  161.1 1.3 fusion.16
  162.5 15.0 %all-to-all-done.6.got_ref = bf16[32,64,128]{2,1,0:T(8,128)(2,1)S(1)} async-done(((bf16[32,64,128]{2,1,0:T(8,128)(2,1)}), bf16[32,64,128]{2,1,0:T(8,128)(2,1)S(1)}, u32[]{:S(2)}, u32[]{:S(2)}) %all-to-all-start.6) | async-done | bytes 524320 | tf_op jit(solution)/shard_map/all_to_all | solution.py:1184
  177.5 0.8 copy-done.2
  178.3 9.6 %shard_map.501 = (f32[]{:T(128)}, f32[32,75]{1,0:T(8,128)}, f32[1600,128]{1,0:T(8,128)}, f32[4000,128]{1,0:T(8,128)}, f32[15,250]{1,0:T(8,128)}, /*index=5*/f32[...) custom-call(bf16[32,64,128]{2,1,0:T(8,128)(2,1)} %copy-done.2, ...), custom_call_target="tpu_custom_call" | custom-call | tf_op jit(solution)/shard_map/pallas_call | solution.py:1352
  (51 shorter events, 0.2 us)
Async XLA Ops:
  0.7 10.5 %copy-start.13 = (bf16[144,75]{1,0:T(8,128)(2,1)S(1)}, bf16[144,75]{1,0:T(8,128)(2,1)}, u32[]{:S(2)}) copy-start(bf16[144,75]{1,0:T(8,128)(2,1)} %constant.62.clone) | copy-start | bytes 64804
  0.7 9.9 %copy-start.14 = (f32[517]{0:T(1024)S(1)}, f32[517]{0:T(1024)}, u32[]{:S(2)}) copy-start(f32[517]{0:T(1024)} %refs_6_.1) | copy-start | bytes 6208
  0.7 10.3 %slice-start = ((f32[517]{0:T(1024)}), f32[224]{0:T(256)S(1)}, s32[]{:S(2)}) async-start(f32[517]{0:T(1024)} %refs_6_.1), calls=%async_computation.7 | async-start | bytes 2048 | tf_op jit(solution)/shard_map/slice | solution.py:1226
  0.7 10.0 %copy-start.17 = (s32[4,16,2]{1,2,0:T(2,128)S(1)}, s32[4,16,2]{1,2,0:T(2,128)}, u32[]{:S(2)}) copy-start(s32[4,16,2]{1,2,0:T(2,128)} %param.35) | copy-start | bytes 1540
  0.7 10.0 %copy-start.16 = (f32[4,16,3]{1,0,2:T(4,128)S(1)}, f32[4,16,3]{1,0,2:T(4,128)}, u32[]{:S(2)}) copy-start(f32[4,16,3]{1,0,2:T(4,128)} %param.37) | copy-start | bytes 2308
  0.7 10.1 %copy-start.15 = (f32[4,16,4]{1,2,0:T(4,128)S(1)}, f32[4,16,4]{1,2,0:T(4,128)}, u32[]{:S(2)}) copy-start(f32[4,16,4]{1,2,0:T(4,128)} %param.36) | copy-start | bytes 3076
  0.7 10.4 %copy-start.11 = (f32[75,32]{0,1:T(8,128)S(1)}, f32[75,32]{0,1:T(8,128)}, u32[]{:S(2)}) copy-start(f32[75,32]{0,1:T(8,128)} %param.39) | copy-start | bytes 28804
  4.3 16.8 %all-to-all-start = ((bf16[8,144,128]{2,1,0:T(8,128)(2,1)}), bf16[8,144,128]{2,1,0:T(8,128)(2,1)S(1)}, u32[]{:S(2)}, u32[]{:S(2)}) async-start(bf16[8,144,128]{2,1,0:T(8,128)(2,1)} %bitcast.5), calls=%async_computation | async-start | bytes 589824 | tf_op jit(solution)/shard_map/all_to_all | solution.py:1184
  21.0 0.8 copy-start.4
  21.8 19.9 %copy-start = (f32[2,250,1024]{2,0,1:T(2,128)S(1)}, f32[2,250,1024]{2,0,1:T(2,128)}, u32[]{:S(2)}) copy-start(f32[2,250,1024]{2,0,1:T(2,128)} %param.41) | copy-start | bytes 6144004
  38.1 13.1 %all-to-all-start.1 = ((bf16[8,8,16,128]{3,2,1,0:T(8,128)(2,1)}), bf16[8,8,16,128]{3,2,1,0:T(8,128)(2,1)S(1)}, u32[]{:S(2)}, u32[]{:S(2)}) async-start(bf16[8,8,16,128]{3,2,1,0:T(8,128)(2,1)} %get-tuple-element.75), calls=%async_computation.1 | async-start | bytes 524288 | tf_op jit(solution)/shard_map/all_to_all | solution.py:1184
  41.7 2.0 %copy-start.18 = (f32[4,8]{1,0:T(4,128)S(1)}, f32[4,8]{1,0:T(4,128)}, u32[]{:S(2)}) copy-start(f32[4,8]{1,0:T(4,128)} %param.38) | copy-start | bytes 388
  42.4 2.0 %copy-start.1 = (bf16[1024,1024,1]{1,0,2:T(8,128)(2,1)S(1)}, bf16[1024,1024,1]{1,0,2:T(8,128)(2,1)}, u32[]{:S(2)}) copy-start(bf16[1024,1024,1]{1,0,2:T(8,128)(2,1)} %constant.85) | copy-start | bytes 6291460
  52.0 11.3 %copy-start.12 = (f32[15,250]{1,0:T(8,128)S(1)}, f32[15,250]{1,0:T(8,128)}, u32[]{:S(2)}) copy-start(f32[15,250]{1,0:T(8,128)} %refs_3_.1) | copy-start | bytes 45004
  54.0 9.2 %all-to-all-start.2 = ((f32[8,8,256]{2,1,0:T(8,128)}), f32[8,8,256]{2,1,0:T(8,128)S(1)}, u32[]{:S(2)}, u32[]{:S(2)}) async-start(f32[8,8,256]{2,1,0:T(8,128)} %convolution_bitcast_fusion), calls=%async_computation.2 | async-start | bytes 131072 | tf_op jit(solution)/shard_map/all_to_all | solution.py:1184
  59.5 20.5 %copy-start.8 = (bf16[2,64,1024]{2,1,0:T(8,128)(2,1)}, bf16[2,64,1024]{2,1,0:T(8,128)(2,1)S(1)}, u32[]{:S(2)}) copy-start(bf16[2,64,1024]{2,1,0:T(8,128)(2,1)S(1)} %fusion.rest_0_) | copy-start | bytes 786436
  59.5 23.7 %collective-permute-start.1 = (bf16[2,64,1024]{2,1,0:T(8,128)(2,1)S(1)}, bf16[2,64,1024]{2,1,0:T(8,128)(2,1)S(1)}, u32[]{:S(2)}, u32[]{:S(2)}) collective-permute-start(bf16[2,64,1024]{2,1,0:T(8,128)(2,1)S(1)} %fusion.rest_0_), channel_id=1, source_target_pairs={{0,8},{8,16},{16,24},{24,0},{1,9},{9,17},{17,25},{25,1},{2,10},{10... | collective-permute-start | bytes 786440 | tf_op jit(solution)/shard_map/ppermute | solution.py:1288
  80.0 17.4 %copy-start.5 = (bf16[8,4,32,128]{3,2,1,0:T(8,128)(2,1)S(1)}, bf16[8,4,32,128]{3,2,1,0:T(8,128)(2,1)}, u32[]{:S(2)}) copy-start(bf16[8,4,32,128]{3,2,1,0:T(8,128)(2,1)} %get-tuple-element.76.dec_ref) | copy-start | bytes 786436
  80.0 16.2 %copy-start.9 = (bf16[2,64,1024]{2,1,0:T(8,128)(2,1)S(1)}, bf16[2,64,1024]{2,1,0:T(8,128)(2,1)}, u32[]{:S(2)}) copy-start(bf16[2,64,1024]{2,1,0:T(8,128)(2,1)} %copy-done.8) | copy-start | bytes 786436
  80.1 11.3 %all-to-all-start.3 = ((bf16[32,8,256]{2,1,0:T(8,128)(2,1)}), bf16[32,8,256]{2,1,0:T(8,128)(2,1)S(1)}, u32[]{:S(2)}, u32[]{:S(2)}) async-start(bf16[32,8,256]{2,1,0:T(8,128)(2,1)} %get-tuple-element.77), calls=%async_computation.3 | async-start | bytes 262144 | tf_op jit(solution)/shard_map/all_to_all | solution.py:1184
  83.2 38.7 %copy-start.19 = (bf16[2,64,1024]{2,1,0:T(8,128)(2,1)}, bf16[2,64,1024]{2,1,0:T(8,128)(2,1)S(1)}, u32[]{:S(2)}) copy-start(bf16[2,64,1024]{2,1,0:T(8,128)(2,1)S(1)} %collective-permute-done.1.rest_1_) | copy-start | bytes 786436
  91.4 30.6 %copy-start.10 = (bf16[32,8,256]{2,1,0:T(8,128)(2,1)}, bf16[32,8,256]{2,1,0:T(8,128)(2,1)S(1)}, u32[]{:S(2)}) copy-start(bf16[32,8,256]{2,1,0:T(8,128)(2,1)S(1)} %all-to-all-done.3) | copy-start | bytes 393220
  92.8 13.1 %all-to-all-start.4 = ((bf16[8,8,16,128]{3,2,1,0:T(8,128)(2,1)}), bf16[8,8,16,128]{3,2,1,0:T(8,128)(2,1)S(1)}, u32[]{:S(2)}, u32[]{:S(2)}) async-start(bf16[8,8,16,128]{3,2,1,0:T(8,128)(2,1)} %reshape.118), calls=%async_computation.4 | async-start | bytes 524288 | tf_op jit(solution)/shard_map/all_to_all | solution.py:1184
  96.3 8.7 %collective-permute-start.2 = (bf16[2,64,1024]{2,1,0:T(8,128)(2,1)S(1)}, bf16[2,64,1024]{2,1,0:T(8,128)(2,1)S(1)}, u32[]{:S(2)}, u32[]{:S(2)}) collective-permute-start(bf16[2,64,1024]{2,1,0:T(8,128)(2,1)S(1)} %copy-done.9), channel_id=1, source_target_pairs={{0,24},{8,0},{16,8},{24,16},{1,25},{9,1},{17,9},{25,17},{2,26},{10... | collective-permute-start | bytes 786440 | tf_op jit(solution)/shard_map/ppermute | solution.py:1288
  97.5 9.9 %collective-permute-start = (bf16[8,4,32,128]{3,2,1,0:T(8,128)(2,1)S(1)}, bf16[8,4,32,128]{3,2,1,0:T(8,128)(2,1)S(1)}, u32[]{:S(2)}, u32[]{:S(2)}) collective-permute-start(bf16[8,4,32,128]{3,2,1,0:T(8,128)(2,1)S(1)} %copy-done.5), channel_id=1, source_target_pairs={{0,1},{1,0},{2,3},{3,2},{4,5},{5,4},{6,7},{7,6},{8,9},{9,8},{10,11... | collective-permute-start | bytes 786440 | tf_op jit(solution)/shard_map/ppermute | solution.py:1307
  105.0 17.0 %copy-start.20 = (bf16[2,64,1024]{2,1,0:T(8,128)(2,1)}, bf16[2,64,1024]{2,1,0:T(8,128)(2,1)S(1)}, u32[]{:S(2)}) copy-start(bf16[2,64,1024]{2,1,0:T(8,128)(2,1)S(1)} %collective-permute-done.2.rest_3_) | copy-start | bytes 786436
  105.9 1.5 copy-start.3
  105.9 1.5 collective-permute-start.3
  105.9 16.1 %collective-permute-start.4 = (bf16[2,64,1024]{2,1,0:T(8,128)(2,1)S(1)}, bf16[2,64,1024]{2,1,0:T(8,128)(2,1)S(1)}, u32[]{:S(2)}, u32[]{:S(2)}) collective-permute-start(bf16[2,64,1024]{2,1,0:T(8,128)(2,1)S(1)} %copy-done.9), channel_id=1, source_target_pairs={{0,16},{8,24},{16,0},{24,8},{1,17},{9,25},{17,1},{25,9},{2,18},{10... | collective-permute-start | bytes 786440 | tf_op jit(solution)/shard_map/ppermute | solution.py:1288
  107.3 0.7 copy-start.6
  107.5 0.7 copy-start.7
  122.0 0.7 copy-start.21
  158.5 19.0 %all-to-all-start.6 = ((bf16[32,64,128]{2,1,0:T(8,128)(2,1)}), bf16[32,64,128]{2,1,0:T(8,128)(2,1)S(1)}, u32[]{:S(2)}, u32[]{:S(2)}) async-start(bf16[32,64,128]{2,1,0:T(8,128)(2,1)} %get-tuple-element.92), calls=%async_computation.6 | async-start | bytes 1048576 | tf_op jit(solution)/shard_map/all_to_all | solution.py:1184
  177.5 0.8 copy-start.2
